TPU v7x, 32 devices: a whole 2x2x4 slice. The times are simulated.
32 devices in a mesh: groups: 2 (over y), src: 4 (over z), dst: 4 (over x, core).
Axes of the slice: x: 2, y: 2, z: 4, core: 2. Of those that a mesh axis runs over, the one named last changes fastest.
Arguments:
- blocks: bfloat16 [20480, 128, 128], P(('groups', 'src', 'dst')), parts along dimension 0, may hold values from -1 to 1
- block_rows: int32 [20480], P(('groups', 'src', 'dst')), parts along dimension 0, may hold values from 0 to 255, as said below
- block_cols: int32 [20480], P(('groups', 'src', 'dst')), parts along dimension 0, may hold values from 0 to 127, as said below
- row_counts: int32 [65536], P(('groups', 'src')), parts along dimension 0, may hold values from 16 to 5952
- col_counts: int32 [32768], P(('groups', 'dst')), parts along dimension 0, may hold values from 16 to 5952
- start_panel: float32 [32, 32768], P(None, ('groups', 'dst')), parts along dimension 1, may hold values from -30 to 30
Outputs:
- coherent_panel: float32 [32, 32768], P(None, ('groups', 'dst')), parts along dimension 1
There are 2 independent parts, one for each index of `groups`. A program takes and returns all parts, laid end to end along the dimension named above; each array names one. Nothing has to cross between parts.
Inputs may be any that keep to these rules, and one draw needn't show every extreme that they name: `block_rows`: with q = j // 640, s = q // n and d = q % n (n devices along dst), entry j lies in block rows 64 * s to 64 * s + 63; every block row is named by exactly 40 entries, no two of them with the same block column. `block_cols`: with s and d as for block_rows, entry j lies in block columns 32 * d to 32 * d + 31; every block column is named by some entry.
All inputs are finite; a program needn't handle non-finite values.
Results may differ from a plain program's by a relative error of at most 0.0047.
Values may be sent and summed in bfloat16 or wider, within the bound.
No kernel may reach another device: no remote copies, remote signals or barrier semaphores. Data moves between devices by JAX's collectives and lax.ppermute only.
A program may use at most 128 MiB of HBM per device.

v0:
```python
import functools

import jax
import jax.numpy as jnp
from jax import lax
from jax.experimental import pallas as pl
from jax.experimental.pallas import tpu as pltpu
from jax.sharding import PartitionSpec as P

ITERS = 2
F32 = jnp.float32
BF16 = jnp.bfloat16
VMEM = pl.BlockSpec(memory_space=pltpu.VMEM)
SMEM = pl.BlockSpec(memory_space=pltpu.SMEM)
ANY = pl.BlockSpec(memory_space=pl.ANY)
LIMIT = 20 << 20


def params():
    return pltpu.CompilerParams(vmem_limit_bytes=LIMIT)


def dot_nn(a, b, precision=None):
    return lax.dot_general(
        a, b, (((1,), (0,)), ((), ())), preferred_element_type=F32, precision=precision
    )


def dot_nt(a, b, precision=None):
    return lax.dot_general(
        a, b, (((1,), (1,)), ((), ())), preferred_element_type=F32, precision=precision
    )


def unroll_of(total):
    for size in (128, 64, 32, 16, 8, 4, 2, 1):
        if total % size == 0:
            return size
    return 1


def add_group(pieces, ids_ref, first, base, accs):
    for t, piece in enumerate(pieces):
        acc = accs[t % len(accs)]
        place = ids_ref[first + t] - base
        acc[place] += piece


def forward_group(panel_ref, cols_ref, col_base, blocks_ref, first, size):
    pieces = []
    side = panel_ref.shape[1]
    for t in range(0, size, 2):
        one = panel_ref[cols_ref[first + t] - col_base]
        two = panel_ref[cols_ref[first + t + 1] - col_base]
        zero = jnp.zeros_like(one)
        left = jnp.concatenate(
            [jnp.concatenate([one, zero], 1), jnp.concatenate([zero, two], 1)], 0
        )
        right = jnp.concatenate([blocks_ref[first + t], blocks_ref[first + t + 1]], 1)
        out = dot_nt(left, right)
        pieces += [out[:side], out[side:]]
    return pieces


def adjoint_group(panel_ref, rows_ref, row_base, blocks_ref, first, size):
    pieces = []
    side, box = panel_ref.shape[1:]
    for t in range(0, size, 2):
        left = jnp.concatenate(
            [
                panel_ref[rows_ref[first + t] - row_base],
                panel_ref[rows_ref[first + t + 1] - row_base],
            ],
            0,
        )
        right = jnp.concatenate([blocks_ref[first + t], blocks_ref[first + t + 1]], 1)
        out = dot_nn(left, right)
        pieces += [out[:side, :box], out[side:, box:]]
    return pieces


def inverse_factor(gram):
    side = gram.shape[0]
    row_ids = lax.broadcasted_iota(jnp.int32, (side, 2 * side), 0)
    col_ids = lax.broadcasted_iota(jnp.int32, (side, 2 * side), 1)
    eye = (col_ids == row_ids + side).astype(F32)
    work = jnp.concatenate([gram, jnp.zeros_like(gram)], 1) + eye
    for j in range(side - 1):
        pivot_row = work[j : j + 1, :]
        scaled_row = pivot_row / work[j : j + 1, j : j + 1]
        column = jnp.where(row_ids[:, :1] > j, work[:, j : j + 1], 0.0)
        work = work - column * scaled_row
    diag = jnp.sum(jnp.where(col_ids == row_ids, work, 0.0), axis=1, keepdims=True)
    return work[:, side:] / jnp.sqrt(diag)


def orth_matrix(gram):
    first = inverse_factor(gram)
    high = lax.Precision.HIGHEST
    again = dot_nt(dot_nn(first, gram, high), first, high)
    return dot_nn(inverse_factor(again), first, high)


def tree_sum(parts):
    while len(parts) > 1:
        parts = [parts[i] + parts[i + 1] for i in range(0, len(parts), 2)]
    return parts[0]


def basis_of(w_ref, gram_refs, box_total):
    gram = tree_sum([g[...] for g in gram_refs]) / box_total
    matrix = orth_matrix(gram)
    top = matrix.astype(BF16)
    rest = matrix - top.astype(F32)
    mid = rest.astype(BF16)
    low = (rest - mid.astype(F32)).astype(BF16)
    side = matrix.shape[0]
    wide = jnp.concatenate([w_ref[c] for c in range(w_ref.shape[0])], 1)
    out = dot_nn(jnp.concatenate([top, mid, low], 0), wide)
    return out[:side] + out[side : 2 * side] + out[2 * side :]


def store_scaled(basis, counts_ref, panel_ref):
    box = panel_ref.shape[2]
    scaled = (basis / jnp.sqrt(counts_ref[...].astype(F32))).astype(BF16)
    for c in range(panel_ref.shape[0]):
        panel_ref[c] = scaled[:, c * box : (c + 1) * box]


def split_halves(accs, core, keep_ref, send_ref):
    half = keep_ref.shape[0]
    mine = pl.ds(core * half, half)
    other = pl.ds((1 - core) * half, half)
    keep_ref[...] = functools.reduce(jnp.add, [a[mine] for a in accs])
    send_ref[...] = functools.reduce(jnp.add, [a[other] for a in accs]).astype(BF16)


def first_forward_kernel(
    unroll, rows_ref, cols_ref, start_ref, counts_ref, hbm_ref,
    keep_ref, send_ref, blocks_ref, panel_ref, acc_a, acc_b, sems,
):
    total = blocks_ref.shape[0]

    def part(i):
        span = pl.ds(i * unroll, unroll)
        return pltpu.make_async_copy(hbm_ref.at[span], blocks_ref.at[span], sems.at[i])

    for i in range(total // unroll):
        part(i).start()
    core = lax.axis_index("dst") % 2
    row_base = lax.axis_index("src") * acc_a.shape[0]
    col_base = lax.axis_index("dst") * panel_ref.shape[0]
    store_scaled(start_ref[...], counts_ref, panel_ref)
    acc_a[...] = jnp.zeros_like(acc_a)
    acc_b[...] = jnp.zeros_like(acc_b)

    def step(i, carry):
        part(i).wait()
        first = i * unroll
        pieces = forward_group(panel_ref, cols_ref, col_base, blocks_ref, first, unroll)
        add_group(pieces, rows_ref, first, row_base, (acc_a, acc_b))
        return carry

    lax.fori_loop(0, total // unroll, step, 0)
    split_halves((acc_a, acc_b), core, keep_ref, send_ref)


def forward_kernel(unroll, box_total, n_gram, rows_ref, cols_ref, counts_ref, blocks_ref, w_ref, *refs):
    gram_refs = refs[:n_gram]
    keep_ref, send_ref, panel_ref, acc_a, acc_b = refs[n_gram:]
    core = lax.axis_index("dst") % 2
    row_base = lax.axis_index("src") * acc_a.shape[0]
    col_base = lax.axis_index("dst") * panel_ref.shape[0]
    store_scaled(basis_of(w_ref, gram_refs, box_total), counts_ref, panel_ref)
    acc_a[...] = jnp.zeros_like(acc_a)
    acc_b[...] = jnp.zeros_like(acc_b)

    def step(i, carry):
        first = i * unroll
        pieces = forward_group(panel_ref, cols_ref, col_base, blocks_ref, first, unroll)
        add_group(pieces, rows_ref, first, row_base, (acc_a, acc_b))
        return carry

    lax.fori_loop(0, blocks_ref.shape[0] // unroll, step, 0)
    split_halves((acc_a, acc_b), core, keep_ref, send_ref)


def adjoint_kernel(unroll, n_src, rows_ref, cols_ref, counts_ref, blocks_ref, mine_ref, other_ref, *refs):
    keep_ref, send_refs = refs[0], refs[1:n_src]
    panel_ref, acc_a, acc_b = refs[n_src:]
    core = lax.axis_index("dst") % 2
    source = lax.axis_index("src")
    row_base = source * panel_ref.shape[0]
    col_base = lax.axis_index("dst") * acc_a.shape[0]
    half = mine_ref.shape[0]
    panel_ref[pl.ds(core * half, half)] = mine_ref[...]
    panel_ref[pl.ds((1 - core) * half, half)] = other_ref[...]
    acc_a[...] = jnp.zeros_like(acc_a)
    acc_b[...] = jnp.zeros_like(acc_b)

    def step(i, carry):
        first = i * unroll
        pieces = adjoint_group(panel_ref, rows_ref, row_base, blocks_ref, first, unroll)
        add_group(pieces, cols_ref, first, col_base, (acc_a, acc_b))
        return carry

    lax.fori_loop(0, blocks_ref.shape[0] // unroll, step, 0)
    size = keep_ref.shape[0]
    for k in range(n_src):
        span = pl.ds((source ^ k) * size, size)
        scale = jnp.sqrt(counts_ref[span].astype(F32))
        value = (acc_a[span] + acc_b[span]) / scale
        if k == 0:
            keep_ref[...] = value
        else:
            send_refs[k - 1][...] = value.astype(BF16)


def gram_kernel(n_src, *refs):
    chunk_refs, (w_ref, gram_ref) = refs[:n_src], refs[n_src:]
    source = lax.axis_index("src")
    size = chunk_refs[0].shape[0]
    for k in range(n_src):
        w_ref[pl.ds((source ^ k) * size, size)] = chunk_refs[k][...]
    wide = jnp.concatenate([w_ref[c] for c in range(w_ref.shape[0])], 1)
    gram_ref[...] = dot_nt(wide, wide)


def basis_kernel(box_total, n_gram, w_ref, *refs):
    refs[n_gram][...] = basis_of(w_ref, refs[:n_gram], box_total)


def swap(x, axis, bits):
    size = lax.axis_size(axis)
    return lax.ppermute(x, axis, [(i, i ^ bits) for i in range(size)])


def per_device(blocks, block_rows, block_cols, row_counts, col_counts, start_panel):
    total, box, _ = blocks.shape
    side = start_panel.shape[0]
    row_blocks = row_counts.shape[0] // box
    col_blocks = col_counts.shape[0] // box
    n_src, n_dst = lax.axis_size("src"), lax.axis_size("dst")
    box_total = float(col_blocks * box * n_dst)
    unroll = unroll_of(total)
    half = row_blocks // 2
    size = col_blocks // n_src
    wide_counts = col_counts.reshape(1, col_blocks * box)
    tall_counts = col_counts.reshape(col_blocks, 1, box)
    core = lax.axis_index("dst") % 2
    row_scale = row_counts.reshape(2, half, 1, box)[core].astype(F32)

    keep_out = jax.ShapeDtypeStruct((half, side, box), F32)
    send_out = jax.ShapeDtypeStruct((half, side, box), BF16)
    forward_scratch = [
        pltpu.VMEM((col_blocks, side, box), BF16),
        pltpu.VMEM((row_blocks, side, box), F32),
        pltpu.VMEM((row_blocks, side, box), F32),
    ]
    held = None
    w_full, grams = None, None
    for sweep in range(ITERS):
        if sweep == 0:
            keep, send, held = pl.pallas_call(
                functools.partial(first_forward_kernel, unroll),
                in_specs=[SMEM, SMEM, VMEM, VMEM, ANY],
                out_specs=[VMEM, VMEM, VMEM],
                out_shape=[keep_out, send_out, pltpu.VMEM(blocks.shape, BF16)],
                scratch_shapes=forward_scratch + [pltpu.SemaphoreType.DMA((total // unroll,))],
                compiler_params=params(),
                name="first_forward",
            )(block_rows, block_cols, start_panel, wide_counts, blocks)
        else:
            keep, send = pl.pallas_call(
                functools.partial(forward_kernel, unroll, box_total, n_dst),
                in_specs=[SMEM, SMEM] + [VMEM] * (3 + n_dst),
                out_specs=[VMEM, VMEM],
                out_shape=[keep_out, send_out],
                scratch_shapes=forward_scratch,
                compiler_params=params(),
                name="forward",
            )(block_rows, block_cols, wide_counts, held, w_full, *grams)
        held = pltpu.with_memory_space_constraint(held, pltpu.VMEM)
        summed = keep + swap(send, "dst", 1).astype(F32)
        bits = 2
        while bits < n_dst:
            summed = summed + swap(summed.astype(BF16), "dst", bits).astype(F32)
            bits *= 2
        mine = (summed / row_scale).astype(BF16)
        other = swap(mine, "dst", 1)
        chunk = (size, side, box)
        outs = pl.pallas_call(
            functools.partial(adjoint_kernel, unroll, n_src),
            in_specs=[SMEM, SMEM] + [VMEM] * 4,
            out_specs=[VMEM] * n_src,
            out_shape=[jax.ShapeDtypeStruct(chunk, F32)]
            + [jax.ShapeDtypeStruct(chunk, BF16)] * (n_src - 1),
            scratch_shapes=[
                pltpu.VMEM((row_blocks, side, box), BF16),
                pltpu.VMEM((col_blocks, side, box), F32),
                pltpu.VMEM((col_blocks, side, box), F32),
            ],
            compiler_params=params(),
            name="adjoint",
        )(block_rows, block_cols, tall_counts, held, mine, other)
        got = [swap(outs[k], "src", k) for k in range(1, n_src)]
        own = tree_sum([outs[0]] + [g.astype(F32) for g in got]).astype(BF16)
        chunks = [own] + [swap(own, "src", k) for k in range(1, n_src)]
        w_full, gram = pl.pallas_call(
            functools.partial(gram_kernel, n_src),
            in_specs=[VMEM] * n_src,
            out_specs=[VMEM, VMEM],
            out_shape=[
                jax.ShapeDtypeStruct((col_blocks, side, box), BF16),
                jax.ShapeDtypeStruct((side, side), F32),
            ],
            compiler_params=params(),
            name="gram",
        )(*chunks)
        grams = [gram] + [swap(gram, "dst", k) for k in range(1, n_dst)]
    return pl.pallas_call(
        functools.partial(basis_kernel, box_total, n_dst),
        in_specs=[VMEM] * (1 + n_dst),
        out_specs=VMEM,
        out_shape=jax.ShapeDtypeStruct((side, col_blocks * box), F32),
        compiler_params=params(),
        name="basis",
    )(w_full, *grams)


def solution(mesh):
    return jax.shard_map(
        per_device,
        mesh=mesh,
        in_specs=(
            P(("groups", "src", "dst"), None, None),
            P(("groups", "src", "dst")),
            P(("groups", "src", "dst")),
            P(("groups", "src")),
            P(("groups", "dst")),
            P(None, ("groups", "dst")),
        ),
        out_specs=P(None, ("groups", "dst")),
        check_vma=False,
    )
```

profile of v0, /device:TPU:0, one launch (start us, length us, event | category | flops | bytes accessed | tf_op | source)
XLA Modules:
  0.0 129.3 jit_solution(11491919226689296524)
XLA Ops:
  0.0 1.0 copy-done.3
  1.0 0.7 copy-done.4
  1.8 0.7 copy-done.6
  2.5 0.7 copy-done.8
  3.1 10.9 %first_forward.1 = (f32[32,32,128]{2,1,0:T(8,128)S(1)}, bf16[32,32,128]{2,1,0:T(8,128)(2,1)S(1)}, bf16[640,128,128]{2,1,0:T(8,128)(2,1)S(1)}) custom-call(s32[640]{0:T(1024)S(1)} %copy-done.6, s32[640]{0:T(1024)S(1)} %copy-done.8, f32[32,4096]{1,0:T(8,128)S(1)} %copy-done.3, s32[1,4096]{1,0:T(1,128)S(1)} %bitcast.5, bf16[640,128,128]{2,1,0:T(8,128)(2,1)} %hbm_ref.1), custom_call_target="tpu_custom_call" | custom-call | tf_op jit(solution)/shard_map/first_forward/pallas_call | solution.py:264
  14.1 7.0 %copy-done = bf16[640,128,128]{2,1,0:T(8,128)(2,1)} copy-done((bf16[640,128,128]{2,1,0:T(8,128)(2,1)}, bf16[640,128,128]{2,1,0:T(8,128)(2,1)S(1)}, u32[]{:S(2)}) %copy-start) | copy-done | bytes 20971544
  21.0 0.4 collective-permute-start
  21.5 1.2 collective-permute-done
  22.7 2.9 %collective-permute-start.1 = (bf16[32,32,128]{2,1,0:T(8,128)(2,1)S(1)}, bf16[32,32,128]{2,1,0:T(8,128)(2,1)S(1)}, u32[]{:S(2)}, u32[]{:S(2)}) collective-permute-start(bf16[32,32,128]{2,1,0:T(8,128)(2,1)S(1)} %fusion), channel_id=1, source_target_pairs={{0,2},{1,3},{2,0},{3,1},{4,6},{5,7},{6,4},{7,5},{8,10},{9,11},{10,... | collective-permute-start | bytes 786440 | tf_op jit(solution)/shard_map/ppermute | solution.py:235
  25.6 6.6 %collective-permute-done.1 = bf16[32,32,128]{2,1,0:T(8,128)(2,1)S(1)} collective-permute-done((bf16[32,32,128]{2,1,0:T(8,128)(2,1)S(1)}, bf16[32,32,128]{2,1,0:T(8,128)(2,1)S(1)}, u32[]{:S(2)}, u32[]{:S(2)}) %collective-permute-start.1) | collective-permute-done | bytes 262176 | tf_op jit(solution)/shard_map/ppermute | solution.py:235
  32.4 1.5 %collective-permute-done.2.other_ref = bf16[32,32,128]{2,1,0:T(8,128)(2,1)S(1)} collective-permute-done((bf16[32,32,128]{2,1,0:T(8,128)(2,1)S(1)}, bf16[32,32,128]{2,1,0:T(8,128)(2,1)S(1)}, u32[]{:S(2)}, u32[]{:S(2)}) %collective-permute-start.2) | collective-permute-done | bytes 262176 | tf_op jit(solution)/shard_map/ppermute | solution.py:235
  34.0 7.0 %copy-done.1 = bf16[640,128,128]{2,1,0:T(8,128)(2,1)S(1)} copy-done((bf16[640,128,128]{2,1,0:T(8,128)(2,1)S(1)}, bf16[640,128,128]{2,1,0:T(8,128)(2,1)}, u32[]{:S(2)}) %copy-start.1) | copy-done | bytes 20971544
  40.9 5.2 %adjoint.2 = (f32[8,32,128]{2,1,0:T(8,128)S(1)}, bf16[8,32,128]{2,1,0:T(8,128)(2,1)S(1)}, bf16[8,32,128]{2,1,0:T(8,128)(2,1)S(1)}, bf16[8,32,128]{2,1,0:T(8,128)(2,1)S(1)}) custom-call(s32[640]{0:T(1024)S(1)} %copy-done.7, s32[640]{0:T(1024)S(1)} %copy-done.9, s32[32,1,128]{2,1,0:T(1,128)S(1)} %bitcast.6, bf16[640,128,128]{2,1,0:T(8,128)(2,1)S(1)} %copy-done.1, ...), custom_call_target="tpu_custom_call" | custom-call | tf_op jit(solution)/shard_map/adjoint/pallas_call | solution.py:292
  46.2 2.0 %collective-permute-start.3 = (bf16[8,32,128]{2,1,0:T(8,128)(2,1)S(1)}, bf16[8,32,128]{2,1,0:T(8,128)(2,1)S(1)}, u32[]{:S(2)}, u32[]{:S(2)}) collective-permute-start(bf16[8,32,128]{2,1,0:T(8,128)(2,1)S(1)} %get-tuple-element.26), channel_id=1, source_target_pairs={{0,4},{4,0},{8,12},{12,8},{1,5},{5,1},{9,13},{13,9},{2,6},{6,2},{1... | collective-permute-start | bytes 196616 | tf_op jit(solution)/shard_map/ppermute | solution.py:235
  48.1 2.6 %collective-permute-start.4 = (bf16[8,32,128]{2,1,0:T(8,128)(2,1)S(1)}, bf16[8,32,128]{2,1,0:T(8,128)(2,1)S(1)}, u32[]{:S(2)}, u32[]{:S(2)}) collective-permute-start(bf16[8,32,128]{2,1,0:T(8,128)(2,1)S(1)} %get-tuple-element.27), channel_id=1, source_target_pairs={{0,8},{4,12},{8,0},{12,4},{1,9},{5,13},{9,1},{13,5},{2,10},{6,14},... | collective-permute-start | bytes 196616 | tf_op jit(solution)/shard_map/ppermute | solution.py:235
  50.7 4.9 %collective-permute-done.4 = bf16[8,32,128]{2,1,0:T(8,128)(2,1)S(1)} collective-permute-done((bf16[8,32,128]{2,1,0:T(8,128)(2,1)S(1)}, bf16[8,32,128]{2,1,0:T(8,128)(2,1)S(1)}, u32[]{:S(2)}, u32[]{:S(2)}) %collective-permute-start.4) | collective-permute-done | bytes 65568 | tf_op jit(solution)/shard_map/ppermute | solution.py:235
  55.7 1.2 collective-permute-done.5
  56.9 2.0 %collective-permute-start.8 = (bf16[8,32,128]{2,1,0:T(8,128)(2,1)S(1)}, bf16[8,32,128]{2,1,0:T(8,128)(2,1)S(1)}, u32[]{:S(2)}, u32[]{:S(2)}) collective-permute-start(bf16[8,32,128]{2,1,0:T(8,128)(2,1)S(1)} %add_convert_fusion.1.refs_0_), channel_id=1, source_target_pairs={{0,12},{4,8},{8,4},{12,0},{1,13},{5,9},{9,5},{13,1},{2,14},{6,10},... | collective-permute-start | bytes 196616 | tf_op jit(solution)/shard_map/ppermute | solution.py:235
  58.9 0.3 collective-permute-start.7
  59.3 2.1 %collective-permute-start.6 = (bf16[8,32,128]{2,1,0:T(8,128)(2,1)S(1)}, bf16[8,32,128]{2,1,0:T(8,128)(2,1)S(1)}, u32[]{:S(2)}, u32[]{:S(2)}) collective-permute-start(bf16[8,32,128]{2,1,0:T(8,128)(2,1)S(1)} %add_convert_fusion.1.refs_0_), channel_id=1, source_target_pairs={{0,4},{4,0},{8,12},{12,8},{1,5},{5,1},{9,13},{13,9},{2,6},{6,2},{1... | collective-permute-start | bytes 196616 | tf_op jit(solution)/shard_map/ppermute | solution.py:235
  61.4 1.8 %collective-permute-done.8.refs_3_ = bf16[8,32,128]{2,1,0:T(8,128)(2,1)S(1)} collective-permute-done((bf16[8,32,128]{2,1,0:T(8,128)(2,1)S(1)}, bf16[8,32,128]{2,1,0:T(8,128)(2,1)S(1)}, u32[]{:S(2)}, u32[]{:S(2)}) %collective-permute-start.8) | collective-permute-done | bytes 65568 | tf_op jit(solution)/shard_map/ppermute | solution.py:235
  63.2 1.5 %collective-permute-done.7.refs_2_ = bf16[8,32,128]{2,1,0:T(8,128)(2,1)S(1)} collective-permute-done((bf16[8,32,128]{2,1,0:T(8,128)(2,1)S(1)}, bf16[8,32,128]{2,1,0:T(8,128)(2,1)S(1)}, u32[]{:S(2)}, u32[]{:S(2)}) %collective-permute-start.7) | collective-permute-done | bytes 65568 | tf_op jit(solution)/shard_map/ppermute | solution.py:235
  64.7 0.2 gram.2
  64.9 1.6 %collective-permute-start.10 = (f32[32,32]{1,0:T(8,128)S(1)}, f32[32,32]{1,0:T(8,128)S(1)}, u32[]{:S(2)}, u32[]{:S(2)}) collective-permute-start(f32[32,32]{1,0:T(8,128)S(1)} %get-tuple-element.30.refs_0_), channel_id=1, source_target_pairs={{0,2},{1,3},{2,0},{3,1},{4,6},{5,7},{6,4},{7,5},{8,10},{9,11},{10,... | collective-permute-start | bytes 12296 | tf_op jit(solution)/shard_map/ppermute | solution.py:235
  66.5 0.3 collective-permute-start.9
  66.8 1.4 %collective-permute-done.11.refs_3_ = f32[32,32]{1,0:T(8,128)S(1)} collective-permute-done((f32[32,32]{1,0:T(8,128)S(1)}, f32[32,32]{1,0:T(8,128)S(1)}, u32[]{:S(2)}, u32[]{:S(2)}) %collective-permute-start.11) | collective-permute-done | bytes 4128 | tf_op jit(solution)/shard_map/ppermute | solution.py:235
  68.2 0.5 collective-permute-done.10.refs_2_
  68.7 14.9 %forward.1 = (f32[32,32,128]{2,1,0:T(8,128)S(1)}, bf16[32,32,128]{2,1,0:T(8,128)(2,1)S(1)}) custom-call(s32[640]{0:T(1024)S(1)} %copy-done.7, s32[640]{0:T(1024)S(1)} %copy-done.9, s32[1,4096]{1,0:T(1,128)S(1)} %bitcast.7, bf16[640,128,128]{2,1,0:T(8,128)(2,1)S(1)} %copy-done.2, bf16[32,32,128]{2,1,0:T(8,128)(2,1)S(1)} %get-tuple-element.29.w_ref, ...), custom_call_target="tpu_custom_call" | custom-call | tf_op jit(solution)/shard_map/forward/pallas_call | solution.py:274
  83.6 0.5 collective-permute-start.12
  84.1 1.2 collective-permute-done.12
  85.3 1.5 %collective-permute-start.13 = (bf16[32,32,128]{2,1,0:T(8,128)(2,1)S(1)}, bf16[32,32,128]{2,1,0:T(8,128)(2,1)S(1)}, u32[]{:S(2)}, u32[]{:S(2)}) collective-permute-start(bf16[32,32,128]{2,1,0:T(8,128)(2,1)S(1)} %fusion.1), channel_id=1, source_target_pairs={{0,2},{1,3},{2,0},{3,1},{4,6},{5,7},{6,4},{7,5},{8,10},{9,11},{10,... | collective-permute-start | bytes 786440 | tf_op jit(solution)/shard_map/ppermute | solution.py:235
  86.9 7.1 %collective-permute-done.13 = bf16[32,32,128]{2,1,0:T(8,128)(2,1)S(1)} collective-permute-done((bf16[32,32,128]{2,1,0:T(8,128)(2,1)S(1)}, bf16[32,32,128]{2,1,0:T(8,128)(2,1)S(1)}, u32[]{:S(2)}, u32[]{:S(2)}) %collective-permute-start.13) | collective-permute-done | bytes 262176 | tf_op jit(solution)/shard_map/ppermute | solution.py:235
  94.2 1.5 %collective-permute-done.14.other_ref = bf16[32,32,128]{2,1,0:T(8,128)(2,1)S(1)} collective-permute-done((bf16[32,32,128]{2,1,0:T(8,128)(2,1)S(1)}, bf16[32,32,128]{2,1,0:T(8,128)(2,1)S(1)}, u32[]{:S(2)}, u32[]{:S(2)}) %collective-permute-start.14) | collective-permute-done | bytes 262176 | tf_op jit(solution)/shard_map/ppermute | solution.py:235
  95.7 5.2 %adjoint.3 = (f32[8,32,128]{2,1,0:T(8,128)S(1)}, bf16[8,32,128]{2,1,0:T(8,128)(2,1)S(1)}, bf16[8,32,128]{2,1,0:T(8,128)(2,1)S(1)}, bf16[8,32,128]{2,1,0:T(8,128)(2,1)S(1)}) custom-call(s32[640]{0:T(1024)S(1)} %copy-done.7, s32[640]{0:T(1024)S(1)} %copy-done.9, s32[32,1,128]{2,1,0:T(1,128)S(1)} %bitcast.8, bf16[640,128,128]{2,1,0:T(8,128)(2,1)S(1)} %copy-done.2, ...), custom_call_target="tpu_custom_call" | custom-call | tf_op jit(solution)/shard_map/adjoint/pallas_call | solution.py:292
  101.0 1.0 collective-permute-start.15
  102.0 1.6 %collective-permute-start.16 = (bf16[8,32,128]{2,1,0:T(8,128)(2,1)S(1)}, bf16[8,32,128]{2,1,0:T(8,128)(2,1)S(1)}, u32[]{:S(2)}, u32[]{:S(2)}) collective-permute-start(bf16[8,32,128]{2,1,0:T(8,128)(2,1)S(1)} %get-tuple-element.35), channel_id=1, source_target_pairs={{0,8},{4,12},{8,0},{12,4},{1,9},{5,13},{9,1},{13,5},{2,10},{6,14},... | collective-permute-start | bytes 196616 | tf_op jit(solution)/shard_map/ppermute | solution.py:235
  103.6 1.8 %collective-permute-start.17 = (bf16[8,32,128]{2,1,0:T(8,128)(2,1)S(1)}, bf16[8,32,128]{2,1,0:T(8,128)(2,1)S(1)}, u32[]{:S(2)}, u32[]{:S(2)}) collective-permute-start(bf16[8,32,128]{2,1,0:T(8,128)(2,1)S(1)} %get-tuple-element.36), channel_id=1, source_target_pairs={{0,12},{4,8},{8,4},{12,0},{1,13},{5,9},{9,5},{13,1},{2,14},{6,10},... | collective-permute-start | bytes 196616 | tf_op jit(solution)/shard_map/ppermute | solution.py:235
  105.4 4.8 %collective-permute-done.16 = bf16[8,32,128]{2,1,0:T(8,128)(2,1)S(1)} collective-permute-done((bf16[8,32,128]{2,1,0:T(8,128)(2,1)S(1)}, bf16[8,32,128]{2,1,0:T(8,128)(2,1)S(1)}, u32[]{:S(2)}, u32[]{:S(2)}) %collective-permute-start.16) | collective-permute-done | bytes 65568 | tf_op jit(solution)/shard_map/ppermute | solution.py:235
  110.3 2.0 %collective-permute-start.20 = (bf16[8,32,128]{2,1,0:T(8,128)(2,1)S(1)}, bf16[8,32,128]{2,1,0:T(8,128)(2,1)S(1)}, u32[]{:S(2)}, u32[]{:S(2)}) collective-permute-start(bf16[8,32,128]{2,1,0:T(8,128)(2,1)S(1)} %add_convert_fusion.refs_0_), channel_id=1, source_target_pairs={{0,12},{4,8},{8,4},{12,0},{1,13},{5,9},{9,5},{13,1},{2,14},{6,10},... | collective-permute-start | bytes 196616 | tf_op jit(solution)/shard_map/ppermute | solution.py:235
  112.3 0.7 collective-permute-start.19
  113.1 1.7 %collective-permute-start.18 = (bf16[8,32,128]{2,1,0:T(8,128)(2,1)S(1)}, bf16[8,32,128]{2,1,0:T(8,128)(2,1)S(1)}, u32[]{:S(2)}, u32[]{:S(2)}) collective-permute-start(bf16[8,32,128]{2,1,0:T(8,128)(2,1)S(1)} %add_convert_fusion.refs_0_), channel_id=1, source_target_pairs={{0,4},{4,0},{8,12},{12,8},{1,5},{5,1},{9,13},{13,9},{2,6},{6,2},{1... | collective-permute-start | bytes 196616 | tf_op jit(solution)/shard_map/ppermute | solution.py:235
  114.8 1.9 %collective-permute-done.20.refs_3_ = bf16[8,32,128]{2,1,0:T(8,128)(2,1)S(1)} collective-permute-done((bf16[8,32,128]{2,1,0:T(8,128)(2,1)S(1)}, bf16[8,32,128]{2,1,0:T(8,128)(2,1)S(1)}, u32[]{:S(2)}, u32[]{:S(2)}) %collective-permute-start.20) | collective-permute-done | bytes 65568 | tf_op jit(solution)/shard_map/ppermute | solution.py:235
  116.6 1.7 %collective-permute-done.19.refs_2_ = bf16[8,32,128]{2,1,0:T(8,128)(2,1)S(1)} collective-permute-done((bf16[8,32,128]{2,1,0:T(8,128)(2,1)S(1)}, bf16[8,32,128]{2,1,0:T(8,128)(2,1)S(1)}, u32[]{:S(2)}, u32[]{:S(2)}) %collective-permute-start.19) | collective-permute-done | bytes 65568 | tf_op jit(solution)/shard_map/ppermute | solution.py:235
  118.5 1.2 collective-permute-start.22
  119.8 0.6 collective-permute-start.21
  120.4 1.3 %collective-permute-done.23.refs_3_ = f32[32,32]{1,0:T(8,128)S(1)} collective-permute-done((f32[32,32]{1,0:T(8,128)S(1)}, f32[32,32]{1,0:T(8,128)S(1)}, u32[]{:S(2)}, u32[]{:S(2)}) %collective-permute-start.23) | collective-permute-done | bytes 4128 | tf_op jit(solution)/shard_map/ppermute | solution.py:235
  121.7 0.6 collective-permute-done.22.refs_2_
  122.3 7.0 %basis.1 = f32[32,4096]{1,0:T(8,128)} custom-call(bf16[32,32,128]{2,1,0:T(8,128)(2,1)S(1)} %get-tuple-element.37.w_ref, f32[32,32]{1,0:T(8,128)S(1)} %get-tuple-element.38.refs_0_, f32[32,32]{1,0:T(8,128)S(1)} %collective-permute-done.21.refs_1_, f32[32,32]{1,0:T(8,128)S(1)} %collective-permute-done.22.refs_2_, f32[32,32]{1,0:T(8,128)S(1)} %collective-permute-done.23.refs_3_), custom_call_target="tpu_custom_call" | custom-call | tf_op jit(solution)/shard_map/basis/pallas_call | solution.py:321
  (36 shorter events, 0.9 us)
Async XLA Ops:
  0.0 1.0 copy-start.3
  1.0 0.7 copy-start.4
  1.8 0.7 copy-start.6
  2.4 0.7 copy-start.8
  3.1 22.5 %copy-start.10 = (s32[8192]{0:T(1024)S(1)}, s32[8192]{0:T(1024)}, u32[]{:S(2)}) copy-start(s32[8192]{0:T(1024)} %param.9) | copy-start | bytes 98308
  3.1 30.8 %copy-start.5 = (s32[4096]{0:T(1024)S(1)}, s32[4096]{0:T(1024)}, u32[]{:S(2)}) copy-start(s32[4096]{0:T(1024)} %param.10) | copy-start | bytes 49156
  3.1 30.8 %copy-start.7 = (s32[640]{0:T(1024)S(1)}, s32[640]{0:T(1024)}, u32[]{:S(2)}) copy-start(s32[640]{0:T(1024)} %rows_ref.7) | copy-start | bytes 7684
  3.1 30.8 %copy-start.9 = (s32[640]{0:T(1024)S(1)}, s32[640]{0:T(1024)}, u32[]{:S(2)}) copy-start(s32[640]{0:T(1024)} %cols_ref.7) | copy-start | bytes 7684
  14.0 7.0 %copy-start = (bf16[640,128,128]{2,1,0:T(8,128)(2,1)}, bf16[640,128,128]{2,1,0:T(8,128)(2,1)S(1)}, u32[]{:S(2)}) copy-start(bf16[640,128,128]{2,1,0:T(8,128)(2,1)S(1)} %get-tuple-element.22.blocks_ref) | copy-start | bytes 62914564
  21.0 1.6 %collective-permute-start = (bf16[32,32,128]{2,1,0:T(8,128)(2,1)S(1)}, bf16[32,32,128]{2,1,0:T(8,128)(2,1)S(1)}, u32[]{:S(2)}, u32[]{:S(2)}) collective-permute-start(bf16[32,32,128]{2,1,0:T(8,128)(2,1)S(1)} %get-tuple-element.24), channel_id=1, source_target_pairs={{0,1},{1,0},{2,3},{3,2},{4,5},{5,4},{6,7},{7,6},{8,9},{9,8},{10,11... | collective-permute-start | bytes 786440 | tf_op jit(solution)/shard_map/ppermute | solution.py:235
  22.7 9.5 %collective-permute-start.1 = (bf16[32,32,128]{2,1,0:T(8,128)(2,1)S(1)}, bf16[32,32,128]{2,1,0:T(8,128)(2,1)S(1)}, u32[]{:S(2)}, u32[]{:S(2)}) collective-permute-start(bf16[32,32,128]{2,1,0:T(8,128)(2,1)S(1)} %fusion), channel_id=1, source_target_pairs={{0,2},{1,3},{2,0},{3,1},{4,6},{5,7},{6,4},{7,5},{8,10},{9,11},{10,... | collective-permute-start | bytes 786440 | tf_op jit(solution)/shard_map/ppermute | solution.py:235
  32.4 1.6 %collective-permute-start.2 = (bf16[32,32,128]{2,1,0:T(8,128)(2,1)S(1)}, bf16[32,32,128]{2,1,0:T(8,128)(2,1)S(1)}, u32[]{:S(2)}, u32[]{:S(2)}) collective-permute-start(bf16[32,32,128]{2,1,0:T(8,128)(2,1)S(1)} %divide_convert_fusion.1.mine_ref), channel_id=1, source_target_pairs={{0,1},{1,0},{2,3},{3,2},{4,5},{5,4},{6,7},{7,6},{8,9},{9,8},{10,11... | collective-permute-start | bytes 786440 | tf_op jit(solution)/shard_map/ppermute | solution.py:235
  34.0 7.0 %copy-start.1 = (bf16[640,128,128]{2,1,0:T(8,128)(2,1)S(1)}, bf16[640,128,128]{2,1,0:T(8,128)(2,1)}, u32[]{:S(2)}) copy-start(bf16[640,128,128]{2,1,0:T(8,128)(2,1)} %copy-done) | copy-start | bytes 62914564
  40.9 27.8 %copy-start.2 = (bf16[640,128,128]{2,1,0:T(8,128)(2,1)S(1)}, bf16[640,128,128]{2,1,0:T(8,128)(2,1)}, u32[]{:S(2)}) copy-start(bf16[640,128,128]{2,1,0:T(8,128)(2,1)} %copy-done) | copy-start | bytes 62914564
  46.2 4.6 %collective-permute-start.3 = (bf16[8,32,128]{2,1,0:T(8,128)(2,1)S(1)}, bf16[8,32,128]{2,1,0:T(8,128)(2,1)S(1)}, u32[]{:S(2)}, u32[]{:S(2)}) collective-permute-start(bf16[8,32,128]{2,1,0:T(8,128)(2,1)S(1)} %get-tuple-element.26), channel_id=1, source_target_pairs={{0,4},{4,0},{8,12},{12,8},{1,5},{5,1},{9,13},{13,9},{2,6},{6,2},{1... | collective-permute-start | bytes 196616 | tf_op jit(solution)/shard_map/ppermute | solution.py:235
  48.1 7.5 %collective-permute-start.4 = (bf16[8,32,128]{2,1,0:T(8,128)(2,1)S(1)}, bf16[8,32,128]{2,1,0:T(8,128)(2,1)S(1)}, u32[]{:S(2)}, u32[]{:S(2)}) collective-permute-start(bf16[8,32,128]{2,1,0:T(8,128)(2,1)S(1)} %get-tuple-element.27), channel_id=1, source_target_pairs={{0,8},{4,12},{8,0},{12,4},{1,9},{5,13},{9,1},{13,5},{2,10},{6,14},... | collective-permute-start | bytes 196616 | tf_op jit(solution)/shard_map/ppermute | solution.py:235
  50.7 6.2 %collective-permute-start.5 = (bf16[8,32,128]{2,1,0:T(8,128)(2,1)S(1)}, bf16[8,32,128]{2,1,0:T(8,128)(2,1)S(1)}, u32[]{:S(2)}, u32[]{:S(2)}) collective-permute-start(bf16[8,32,128]{2,1,0:T(8,128)(2,1)S(1)} %get-tuple-element.28), channel_id=1, source_target_pairs={{0,12},{4,8},{8,4},{12,0},{1,13},{5,9},{9,5},{13,1},{2,14},{6,10},... | collective-permute-start | bytes 196616 | tf_op jit(solution)/shard_map/ppermute | solution.py:235
  56.9 6.3 %collective-permute-start.8 = (bf16[8,32,128]{2,1,0:T(8,128)(2,1)S(1)}, bf16[8,32,128]{2,1,0:T(8,128)(2,1)S(1)}, u32[]{:S(2)}, u32[]{:S(2)}) collective-permute-start(bf16[8,32,128]{2,1,0:T(8,128)(2,1)S(1)} %add_convert_fusion.1.refs_0_), channel_id=1, source_target_pairs={{0,12},{4,8},{8,4},{12,0},{1,13},{5,9},{9,5},{13,1},{2,14},{6,10},... | collective-permute-start | bytes 196616 | tf_op jit(solution)/shard_map/ppermute | solution.py:235
  58.9 5.8 %collective-permute-start.7 = (bf16[8,32,128]{2,1,0:T(8,128)(2,1)S(1)}, bf16[8,32,128]{2,1,0:T(8,128)(2,1)S(1)}, u32[]{:S(2)}, u32[]{:S(2)}) collective-permute-start(bf16[8,32,128]{2,1,0:T(8,128)(2,1)S(1)} %add_convert_fusion.1.refs_0_), channel_id=1, source_target_pairs={{0,8},{4,12},{8,0},{12,4},{1,9},{5,13},{9,1},{13,5},{2,10},{6,14},... | collective-permute-start | bytes 196616 | tf_op jit(solution)/shard_map/ppermute | solution.py:235
  59.3 5.4 %collective-permute-start.6 = (bf16[8,32,128]{2,1,0:T(8,128)(2,1)S(1)}, bf16[8,32,128]{2,1,0:T(8,128)(2,1)S(1)}, u32[]{:S(2)}, u32[]{:S(2)}) collective-permute-start(bf16[8,32,128]{2,1,0:T(8,128)(2,1)S(1)} %add_convert_fusion.1.refs_0_), channel_id=1, source_target_pairs={{0,4},{4,0},{8,12},{12,8},{1,5},{5,1},{9,13},{13,9},{2,6},{6,2},{1... | collective-permute-start | bytes 196616 | tf_op jit(solution)/shard_map/ppermute | solution.py:235
  64.9 3.3 %collective-permute-start.11 = (f32[32,32]{1,0:T(8,128)S(1)}, f32[32,32]{1,0:T(8,128)S(1)}, u32[]{:S(2)}, u32[]{:S(2)}) collective-permute-start(f32[32,32]{1,0:T(8,128)S(1)} %get-tuple-element.30.refs_0_), channel_id=1, source_target_pairs={{0,3},{1,2},{2,1},{3,0},{4,7},{5,6},{6,5},{7,4},{8,11},{9,10},{10,... | collective-permute-start | bytes 12296 | tf_op jit(solution)/shard_map/ppermute | solution.py:235
  64.9 3.8 %collective-permute-start.10 = (f32[32,32]{1,0:T(8,128)S(1)}, f32[32,32]{1,0:T(8,128)S(1)}, u32[]{:S(2)}, u32[]{:S(2)}) collective-permute-start(f32[32,32]{1,0:T(8,128)S(1)} %get-tuple-element.30.refs_0_), channel_id=1, source_target_pairs={{0,2},{1,3},{2,0},{3,1},{4,6},{5,7},{6,4},{7,5},{8,10},{9,11},{10,... | collective-permute-start | bytes 12296 | tf_op jit(solution)/shard_map/ppermute | solution.py:235
  66.5 2.2 %collective-permute-start.9 = (f32[32,32]{1,0:T(8,128)S(1)}, f32[32,32]{1,0:T(8,128)S(1)}, u32[]{:S(2)}, u32[]{:S(2)}) collective-permute-start(f32[32,32]{1,0:T(8,128)S(1)} %get-tuple-element.30.refs_0_), channel_id=1, source_target_pairs={{0,1},{1,0},{2,3},{3,2},{4,5},{5,4},{6,7},{7,6},{8,9},{9,8},{10,11... | collective-permute-start | bytes 12296 | tf_op jit(solution)/shard_map/ppermute | solution.py:235
  83.6 1.6 %collective-permute-start.12 = (bf16[32,32,128]{2,1,0:T(8,128)(2,1)S(1)}, bf16[32,32,128]{2,1,0:T(8,128)(2,1)S(1)}, u32[]{:S(2)}, u32[]{:S(2)}) collective-permute-start(bf16[32,32,128]{2,1,0:T(8,128)(2,1)S(1)} %get-tuple-element.32), channel_id=1, source_target_pairs={{0,1},{1,0},{2,3},{3,2},{4,5},{5,4},{6,7},{7,6},{8,9},{9,8},{10,11... | collective-permute-start | bytes 786440 | tf_op jit(solution)/shard_map/ppermute | solution.py:235
  85.3 8.7 %collective-permute-start.13 = (bf16[32,32,128]{2,1,0:T(8,128)(2,1)S(1)}, bf16[32,32,128]{2,1,0:T(8,128)(2,1)S(1)}, u32[]{:S(2)}, u32[]{:S(2)}) collective-permute-start(bf16[32,32,128]{2,1,0:T(8,128)(2,1)S(1)} %fusion.1), channel_id=1, source_target_pairs={{0,2},{1,3},{2,0},{3,1},{4,6},{5,7},{6,4},{7,5},{8,10},{9,11},{10,... | collective-permute-start | bytes 786440 | tf_op jit(solution)/shard_map/ppermute | solution.py:235
  94.1 1.6 %collective-permute-start.14 = (bf16[32,32,128]{2,1,0:T(8,128)(2,1)S(1)}, bf16[32,32,128]{2,1,0:T(8,128)(2,1)S(1)}, u32[]{:S(2)}, u32[]{:S(2)}) collective-permute-start(bf16[32,32,128]{2,1,0:T(8,128)(2,1)S(1)} %divide_convert_fusion.mine_ref), channel_id=1, source_target_pairs={{0,1},{1,0},{2,3},{3,2},{4,5},{5,4},{6,7},{7,6},{8,9},{9,8},{10,11... | collective-permute-start | bytes 786440 | tf_op jit(solution)/shard_map/ppermute | solution.py:235
  101.0 4.5 %collective-permute-start.15 = (bf16[8,32,128]{2,1,0:T(8,128)(2,1)S(1)}, bf16[8,32,128]{2,1,0:T(8,128)(2,1)S(1)}, u32[]{:S(2)}, u32[]{:S(2)}) collective-permute-start(bf16[8,32,128]{2,1,0:T(8,128)(2,1)S(1)} %get-tuple-element.34), channel_id=1, source_target_pairs={{0,4},{4,0},{8,12},{12,8},{1,5},{5,1},{9,13},{13,9},{2,6},{6,2},{1... | collective-permute-start | bytes 196616 | tf_op jit(solution)/shard_map/ppermute | solution.py:235
  102.0 8.3 %collective-permute-start.16 = (bf16[8,32,128]{2,1,0:T(8,128)(2,1)S(1)}, bf16[8,32,128]{2,1,0:T(8,128)(2,1)S(1)}, u32[]{:S(2)}, u32[]{:S(2)}) collective-permute-start(bf16[8,32,128]{2,1,0:T(8,128)(2,1)S(1)} %get-tuple-element.35), channel_id=1, source_target_pairs={{0,8},{4,12},{8,0},{12,4},{1,9},{5,13},{9,1},{13,5},{2,10},{6,14},... | collective-permute-start | bytes 196616 | tf_op jit(solution)/shard_map/ppermute | solution.py:235
  103.6 6.7 %collective-permute-start.17 = (bf16[8,32,128]{2,1,0:T(8,128)(2,1)S(1)}, bf16[8,32,128]{2,1,0:T(8,128)(2,1)S(1)}, u32[]{:S(2)}, u32[]{:S(2)}) collective-permute-start(bf16[8,32,128]{2,1,0:T(8,128)(2,1)S(1)} %get-tuple-element.36), channel_id=1, source_target_pairs={{0,12},{4,8},{8,4},{12,0},{1,13},{5,9},{9,5},{13,1},{2,14},{6,10},... | collective-permute-start | bytes 196616 | tf_op jit(solution)/shard_map/ppermute | solution.py:235
  110.3 6.3 %collective-permute-start.20 = (bf16[8,32,128]{2,1,0:T(8,128)(2,1)S(1)}, bf16[8,32,128]{2,1,0:T(8,128)(2,1)S(1)}, u32[]{:S(2)}, u32[]{:S(2)}) collective-permute-start(bf16[8,32,128]{2,1,0:T(8,128)(2,1)S(1)} %add_convert_fusion.refs_0_), channel_id=1, source_target_pairs={{0,12},{4,8},{8,4},{12,0},{1,13},{5,9},{9,5},{13,1},{2,14},{6,10},... | collective-permute-start | bytes 196616 | tf_op jit(solution)/shard_map/ppermute | solution.py:235
  112.3 5.9 %collective-permute-start.19 = (bf16[8,32,128]{2,1,0:T(8,128)(2,1)S(1)}, bf16[8,32,128]{2,1,0:T(8,128)(2,1)S(1)}, u32[]{:S(2)}, u32[]{:S(2)}) collective-permute-start(bf16[8,32,128]{2,1,0:T(8,128)(2,1)S(1)} %add_convert_fusion.refs_0_), channel_id=1, source_target_pairs={{0,8},{4,12},{8,0},{12,4},{1,9},{5,13},{9,1},{13,5},{2,10},{6,14},... | collective-permute-start | bytes 196616 | tf_op jit(solution)/shard_map/ppermute | solution.py:235
  113.1 5.2 %collective-permute-start.18 = (bf16[8,32,128]{2,1,0:T(8,128)(2,1)S(1)}, bf16[8,32,128]{2,1,0:T(8,128)(2,1)S(1)}, u32[]{:S(2)}, u32[]{:S(2)}) collective-permute-start(bf16[8,32,128]{2,1,0:T(8,128)(2,1)S(1)} %add_convert_fusion.refs_0_), channel_id=1, source_target_pairs={{0,4},{4,0},{8,12},{12,8},{1,5},{5,1},{9,13},{13,9},{2,6},{6,2},{1... | collective-permute-start | bytes 196616 | tf_op jit(solution)/shard_map/ppermute | solution.py:235
  118.5 3.2 %collective-permute-start.23 = (f32[32,32]{1,0:T(8,128)S(1)}, f32[32,32]{1,0:T(8,128)S(1)}, u32[]{:S(2)}, u32[]{:S(2)}) collective-permute-start(f32[32,32]{1,0:T(8,128)S(1)} %get-tuple-element.38.refs_0_), channel_id=1, source_target_pairs={{0,3},{1,2},{2,1},{3,0},{4,7},{5,6},{6,5},{7,4},{8,11},{9,10},{10,... | collective-permute-start | bytes 12296 | tf_op jit(solution)/shard_map/ppermute | solution.py:235
  118.5 3.8 %collective-permute-start.22 = (f32[32,32]{1,0:T(8,128)S(1)}, f32[32,32]{1,0:T(8,128)S(1)}, u32[]{:S(2)}, u32[]{:S(2)}) collective-permute-start(f32[32,32]{1,0:T(8,128)S(1)} %get-tuple-element.38.refs_0_), channel_id=1, source_target_pairs={{0,2},{1,3},{2,0},{3,1},{4,6},{5,7},{6,4},{7,5},{8,10},{9,11},{10,... | collective-permute-start | bytes 12296 | tf_op jit(solution)/shard_map/ppermute | solution.py:235
  119.8 2.6 %collective-permute-start.21 = (f32[32,32]{1,0:T(8,128)S(1)}, f32[32,32]{1,0:T(8,128)S(1)}, u32[]{:S(2)}, u32[]{:S(2)}) collective-permute-start(f32[32,32]{1,0:T(8,128)S(1)} %get-tuple-element.38.refs_0_), channel_id=1, source_target_pairs={{0,1},{1,0},{2,3},{3,2},{4,5},{5,4},{6,7},{7,6},{8,9},{9,8},{10,11... | collective-permute-start | bytes 12296 | tf_op jit(solution)/shard_map/ppermute | solution.py:235
where the time goes:
time: 130 us; the launch traced here: 129 us
  Pallas kernels  43.7 us (34%)
  waiting for transfers between devices  40.8 us (31%)
  starting transfers between devices  27.2 us (21%)
  local copies, waits for them, and re-layouts  17.1 us (13%)
    ppermute x24, waiting for transfers between devices, swap(): return lax.ppermute(x, axis, [(i, i ^ bits) for i in range(size)])  40.8 us
    ppermute x24, starting transfers between devices, swap(): return lax.ppermute(x, axis, [(i, i ^ bits) for i in range(size)])  27.2 us
    unnamed x22, local copies, waits for them, and re-layouts  17.1 us
    pallas_call x1, Pallas kernels, per_device(): pl.pallas_call(functools.partial(forward_kernel, unroll, box_total, n_dst...  14.9 us
    pallas_call x1, Pallas kernels, per_device(): pl.pallas_call(functools.partial(first_forward_kernel, unroll), in_specs=...  10.9 us
    pallas_call x2, Pallas kernels, per_device(): pl.pallas_call(functools.partial(adjoint_kernel, unroll, n_src), in_specs...  10.5 us
    pallas_call x1, Pallas kernels, per_device(): pl.pallas_call(functools.partial(basis_kernel, box_total, n_dst), in_spec...  7.01 us
  transfers between devices with their start and end apart: 24, of which 17 were waited for; matrix products, arithmetic and copies ran while one was open for 0% of the time, Pallas kernels for 0%

commit v1 on v0

--- a/solution.py
+++ b/solution.py
@@ -12,12 +12,15 @@
 BF16 = jnp.bfloat16
 VMEM = pl.BlockSpec(memory_space=pltpu.VMEM)
 SMEM = pl.BlockSpec(memory_space=pltpu.SMEM)
-ANY = pl.BlockSpec(memory_space=pl.ANY)
-LIMIT = 20 << 20
-
-
-def params():
-    return pltpu.CompilerParams(vmem_limit_bytes=LIMIT)
+HBM = pl.BlockSpec(memory_space=pltpu.HBM)
+
+
+def cost(flops, moved=0):
+    return pl.CostEstimate(flops=flops, bytes_accessed=moved, transcendentals=0)
+
+
+def params(mebibytes=6):
+    return pltpu.CompilerParams(vmem_limit_bytes=mebibytes << 20)
 
 
 def dot_nn(a, b, precision=None):
@@ -46,7 +49,7 @@
         acc[place] += piece
 
 
-def forward_group(panel_ref, cols_ref, col_base, blocks_ref, first, size):
+def forward_group(panel_ref, cols_ref, col_base, blocks_ref, first, start, size):
     pieces = []
     side = panel_ref.shape[1]
     for t in range(0, size, 2):
@@ -56,7 +59,7 @@
         left = jnp.concatenate(
             [jnp.concatenate([one, zero], 1), jnp.concatenate([zero, two], 1)], 0
         )
-        right = jnp.concatenate([blocks_ref[first + t], blocks_ref[first + t + 1]], 1)
+        right = jnp.concatenate([blocks_ref[start + t], blocks_ref[start + t + 1]], 1)
         out = dot_nt(left, right)
         pieces += [out[:side], out[side:]]
     return pieces
@@ -107,17 +110,15 @@
     return parts[0]
 
 
-def basis_of(w_ref, gram_refs, box_total):
-    gram = tree_sum([g[...] for g in gram_refs]) / box_total
-    matrix = orth_matrix(gram)
-    top = matrix.astype(BF16)
-    rest = matrix - top.astype(F32)
+def split3(x):
+    top = x.astype(BF16)
+    rest = x - top.astype(F32)
     mid = rest.astype(BF16)
-    low = (rest - mid.astype(F32)).astype(BF16)
-    side = matrix.shape[0]
-    wide = jnp.concatenate([w_ref[c] for c in range(w_ref.shape[0])], 1)
-    out = dot_nn(jnp.concatenate([top, mid, low], 0), wide)
-    return out[:side] + out[side : 2 * side] + out[2 * side :]
+    return top, mid, (rest - mid.astype(F32)).astype(BF16)
+
+
+def orth_of(gram_refs, box_total):
+    return orth_matrix(tree_sum([g[...] for g in gram_refs]) / box_total)
 
 
 def store_scaled(basis, counts_ref, panel_ref):
@@ -136,53 +137,77 @@
 
 
 def first_forward_kernel(
-    unroll, rows_ref, cols_ref, start_ref, counts_ref, hbm_ref,
-    keep_ref, send_ref, blocks_ref, panel_ref, acc_a, acc_b, sems,
+    unroll, rows_hbm, cols_hbm, start_hbm, counts_hbm, blocks_hbm,
+    keep_ref, send_ref,
+    rows_ref, cols_ref, start_ref, counts_ref, blocks_ref, panel_ref, acc_a, acc_b, sems, small_sems,
 ):
-    total = blocks_ref.shape[0]
-
-    def part(i):
-        span = pl.ds(i * unroll, unroll)
-        return pltpu.make_async_copy(hbm_ref.at[span], blocks_ref.at[span], sems.at[i])
-
-    for i in range(total // unroll):
-        part(i).start()
-    core = lax.axis_index("dst") % 2
+    steps = blocks_hbm.shape[0] // unroll
+    slots = blocks_ref.shape[0]
+
+    def part(i, slot):
+        return pltpu.make_async_copy(
+            blocks_hbm.at[pl.ds(i * unroll, unroll)], blocks_ref.at[slot], sems.at[slot]
+        )
+
+    small = [
+        pltpu.make_async_copy(source, target, small_sems.at[i])
+        for i, (source, target) in enumerate(
+            (
+                (start_hbm, start_ref),
+                (counts_hbm, counts_ref),
+                (rows_hbm, rows_ref),
+                (cols_hbm, cols_ref),
+            )
+        )
+    ]
+    for copy in small:
+        copy.start()
+    for i in range(min(slots, steps)):
+        part(i, i).start()
     row_base = lax.axis_index("src") * acc_a.shape[0]
     col_base = lax.axis_index("dst") * panel_ref.shape[0]
-    store_scaled(start_ref[...], counts_ref, panel_ref)
     acc_a[...] = jnp.zeros_like(acc_a)
     acc_b[...] = jnp.zeros_like(acc_b)
+    for copy in small:
+        copy.wait()
+    store_scaled(start_ref[...], counts_ref, panel_ref)
 
     def step(i, carry):
-        part(i).wait()
+        slot = lax.rem(i, slots)
+        part(i, slot).wait()
+        pieces = forward_group(panel_ref, cols_ref, col_base, blocks_ref.at[slot], i * unroll, 0, unroll)
+        add_group(pieces, rows_ref, i * unroll, row_base, (acc_a, acc_b))
+
+        @pl.when(i + slots < steps)
+        def _():
+            part(i + slots, slot).start()
+
+        return carry
+
+    lax.fori_loop(0, steps, step, 0)
+    split_halves((acc_a, acc_b), lax.axis_index("dst") % 2, keep_ref, send_ref)
+
+
+def load_kernel(hbm_ref, held_ref, sem):
+    copy = pltpu.make_async_copy(hbm_ref, held_ref, sem)
+    copy.start()
+    copy.wait()
+
+
+def forward_kernel(unroll, rows_ref, cols_ref, blocks_ref, panel_ref, keep_ref, send_ref, acc_a, acc_b):
+    row_base = lax.axis_index("src") * acc_a.shape[0]
+    col_base = lax.axis_index("dst") * panel_ref.shape[0]
+    acc_a[...] = jnp.zeros_like(acc_a)
+    acc_b[...] = jnp.zeros_like(acc_b)
+
+    def step(i, carry):
         first = i * unroll
-        pieces = forward_group(panel_ref, cols_ref, col_base, blocks_ref, first, unroll)
+        pieces = forward_group(panel_ref, cols_ref, col_base, blocks_ref, first, first, unroll)
         add_group(pieces, rows_ref, first, row_base, (acc_a, acc_b))
         return carry
 
-    lax.fori_loop(0, total // unroll, step, 0)
-    split_halves((acc_a, acc_b), core, keep_ref, send_ref)
-
-
-def forward_kernel(unroll, box_total, n_gram, rows_ref, cols_ref, counts_ref, blocks_ref, w_ref, *refs):
-    gram_refs = refs[:n_gram]
-    keep_ref, send_ref, panel_ref, acc_a, acc_b = refs[n_gram:]
-    core = lax.axis_index("dst") % 2
-    row_base = lax.axis_index("src") * acc_a.shape[0]
-    col_base = lax.axis_index("dst") * panel_ref.shape[0]
-    store_scaled(basis_of(w_ref, gram_refs, box_total), counts_ref, panel_ref)
-    acc_a[...] = jnp.zeros_like(acc_a)
-    acc_b[...] = jnp.zeros_like(acc_b)
-
-    def step(i, carry):
-        first = i * unroll
-        pieces = forward_group(panel_ref, cols_ref, col_base, blocks_ref, first, unroll)
-        add_group(pieces, rows_ref, first, row_base, (acc_a, acc_b))
-        return carry
-
     lax.fori_loop(0, blocks_ref.shape[0] // unroll, step, 0)
-    split_halves((acc_a, acc_b), core, keep_ref, send_ref)
+    split_halves((acc_a, acc_b), lax.axis_index("dst") % 2, keep_ref, send_ref)
 
 
 def adjoint_kernel(unroll, n_src, rows_ref, cols_ref, counts_ref, blocks_ref, mine_ref, other_ref, *refs):
@@ -216,7 +241,7 @@
             send_refs[k - 1][...] = value.astype(BF16)
 
 
-def gram_kernel(n_src, *refs):
+def gram_kernel(n_src, last, counts_ref, *refs):
     chunk_refs, (w_ref, gram_ref) = refs[:n_src], refs[n_src:]
     source = lax.axis_index("src")
     size = chunk_refs[0].shape[0]
@@ -224,10 +249,37 @@
         w_ref[pl.ds((source ^ k) * size, size)] = chunk_refs[k][...]
     wide = jnp.concatenate([w_ref[c] for c in range(w_ref.shape[0])], 1)
     gram_ref[...] = dot_nt(wide, wide)
-
-
-def basis_kernel(box_total, n_gram, w_ref, *refs):
-    refs[n_gram][...] = basis_of(w_ref, refs[:n_gram], box_total)
+    if not last:
+        w_ref[...] = (w_ref[...].astype(F32) / jnp.sqrt(counts_ref[...].astype(F32))).astype(BF16)
+
+
+def orth_kernel(box_total, *refs):
+    refs[-1][...] = orth_of(refs[:-1], box_total)
+
+
+def basis_kernel(box_total, w_ref, *refs):
+    matrix = orth_of(refs[:-1], box_total)
+    side = matrix.shape[0]
+    wide = jnp.concatenate([w_ref[c] for c in range(w_ref.shape[0])], 1)
+    out = dot_nn(jnp.concatenate(split3(matrix), 0), wide)
+    refs[-1][...] = out[:side] + out[side : 2 * side] + out[2 * side :]
+
+
+def mix_kernel(matrix_ref, scale_ref, keep_ref, core_ref, *refs):
+    out_ref = refs[-1]
+    half, side, box = out_ref.shape
+    total = keep_ref[...] + core_ref[...].astype(F32)
+    for ref in refs[:-1]:
+        total = total + ref[...].astype(F32)
+    wide = jnp.concatenate([total[c] for c in range(half)], 1)
+    top, mid, low = split3(wide)
+    left = split3(matrix_ref[...])
+    one = dot_nn(jnp.concatenate(left, 0), top)
+    two = dot_nn(jnp.concatenate(left[:2], 0), mid)
+    three = dot_nn(left[0], low)
+    mixed = one[:side] + (one[side : 2 * side] + two[:side]) + (one[2 * side :] + two[side:] + three)
+    for c in range(half):
+        out_ref[c] = (mixed[:, c * box : (c + 1) * box] / scale_ref[c].astype(F32)).astype(BF16)
 
 
 def swap(x, axis, bits):
@@ -248,45 +300,96 @@
     wide_counts = col_counts.reshape(1, col_blocks * box)
     tall_counts = col_counts.reshape(col_blocks, 1, box)
     core = lax.axis_index("dst") % 2
-    row_scale = row_counts.reshape(2, half, 1, box)[core].astype(F32)
+    row_scale = row_counts.reshape(2, half, 1, box)[core]
+    forward_cost = cost(2 * total * box * box * 512)
+    adjoint_cost = cost(2 * total * box * box * 256)
+    small_cost = cost(1 << 28)
+    orth_cost = cost(1 << 32)
 
     keep_out = jax.ShapeDtypeStruct((half, side, box), F32)
     send_out = jax.ShapeDtypeStruct((half, side, box), BF16)
-    forward_scratch = [
-        pltpu.VMEM((col_blocks, side, box), BF16),
-        pltpu.VMEM((row_blocks, side, box), F32),
-        pltpu.VMEM((row_blocks, side, box), F32),
-    ]
-    held = None
+    square = jax.ShapeDtypeStruct((side, side), F32)
+    accs = [pltpu.VMEM((row_blocks, side, box), F32)] * 2
     w_full, grams = None, None
     for sweep in range(ITERS):
         if sweep == 0:
-            keep, send, held = pl.pallas_call(
+            slots = min(total // unroll, 3)
+            keep, send = pl.pallas_call(
                 functools.partial(first_forward_kernel, unroll),
-                in_specs=[SMEM, SMEM, VMEM, VMEM, ANY],
-                out_specs=[VMEM, VMEM, VMEM],
-                out_shape=[keep_out, send_out, pltpu.VMEM(blocks.shape, BF16)],
-                scratch_shapes=forward_scratch + [pltpu.SemaphoreType.DMA((total // unroll,))],
-                compiler_params=params(),
+                in_specs=[HBM] * 5,
+                out_specs=[VMEM, VMEM],
+                out_shape=[keep_out, send_out],
+                scratch_shapes=[
+                    pltpu.SMEM(block_rows.shape, jnp.int32),
+                    pltpu.SMEM(block_cols.shape, jnp.int32),
+                    pltpu.VMEM(start_panel.shape, F32),
+                    pltpu.VMEM(wide_counts.shape, jnp.int32),
+                    pltpu.VMEM((slots, unroll, box, box), BF16),
+                    pltpu.VMEM((col_blocks, side, box), BF16),
+                    *accs,
+                    pltpu.SemaphoreType.DMA((slots,)),
+                    pltpu.SemaphoreType.DMA((4,)),
+                ],
+                compiler_params=params(18),
                 name="first_forward",
-            )(block_rows, block_cols, start_panel, wide_counts, blocks)
+                cost_estimate=forward_cost,
+            )(*[
+                pltpu.with_memory_space_constraint(x, pltpu.HBM)
+                for x in (block_rows, block_cols, start_panel, wide_counts, blocks)
+            ])
         else:
             keep, send = pl.pallas_call(
-                functools.partial(forward_kernel, unroll, box_total, n_dst),
-                in_specs=[SMEM, SMEM] + [VMEM] * (3 + n_dst),
+                functools.partial(forward_kernel, unroll),
+                in_specs=[SMEM, SMEM, VMEM, VMEM],
                 out_specs=[VMEM, VMEM],
                 out_shape=[keep_out, send_out],
-                scratch_shapes=forward_scratch,
+                scratch_shapes=accs,
                 compiler_params=params(),
                 name="forward",
-            )(block_rows, block_cols, wide_counts, held, w_full, *grams)
-        held = pltpu.with_memory_space_constraint(held, pltpu.VMEM)
-        summed = keep + swap(send, "dst", 1).astype(F32)
+                cost_estimate=forward_cost,
+            )(block_rows, block_cols, held, w_full)
+        core_got = swap(send, "dst", 1)
+        if sweep == 0:
+            again, core_got = lax.optimization_barrier((blocks, core_got))
+            held = pl.pallas_call(
+                load_kernel,
+                in_specs=[HBM],
+                out_specs=VMEM,
+                out_shape=pltpu.VMEM(blocks.shape, BF16),
+                scratch_shapes=[pltpu.SemaphoreType.DMA],
+                compiler_params=params(2),
+                name="load",
+                cost_estimate=cost(0, 2 * total * box * box * 2),
+            )(pltpu.with_memory_space_constraint(again, pltpu.HBM))
+        summed = keep + core_got.astype(F32)
+        x_got = []
         bits = 2
         while bits < n_dst:
-            summed = summed + swap(summed.astype(BF16), "dst", bits).astype(F32)
+            x_got.append(swap(summed.astype(BF16), "dst", bits))
+            summed = summed + x_got[-1].astype(F32)
             bits *= 2
-        mine = (summed / row_scale).astype(BF16)
+        if sweep == 0:
+            summed, held = lax.optimization_barrier((summed, held))
+            mine = (summed / row_scale.astype(F32)).astype(BF16)
+        else:
+            matrix = pl.pallas_call(
+                functools.partial(orth_kernel, box_total),
+                in_specs=[VMEM] * n_dst,
+                out_specs=VMEM,
+                out_shape=square,
+                compiler_params=params(),
+                name="orth",
+                cost_estimate=orth_cost,
+            )(*grams)
+            mine = pl.pallas_call(
+                mix_kernel,
+                in_specs=[VMEM] * (4 + len(x_got)),
+                out_specs=VMEM,
+                out_shape=send_out,
+                compiler_params=params(),
+                name="mix",
+                cost_estimate=small_cost,
+            )(matrix, row_scale, keep, core_got, *x_got)
         other = swap(mine, "dst", 1)
         chunk = (size, side, box)
         outs = pl.pallas_call(
@@ -302,29 +405,29 @@
             ],
             compiler_params=params(),
             name="adjoint",
+                cost_estimate=adjoint_cost,
         )(block_rows, block_cols, tall_counts, held, mine, other)
         got = [swap(outs[k], "src", k) for k in range(1, n_src)]
         own = tree_sum([outs[0]] + [g.astype(F32) for g in got]).astype(BF16)
         chunks = [own] + [swap(own, "src", k) for k in range(1, n_src)]
         w_full, gram = pl.pallas_call(
-            functools.partial(gram_kernel, n_src),
-            in_specs=[VMEM] * n_src,
+            functools.partial(gram_kernel, n_src, sweep == ITERS - 1),
+            in_specs=[VMEM] * (1 + n_src),
             out_specs=[VMEM, VMEM],
-            out_shape=[
-                jax.ShapeDtypeStruct((col_blocks, side, box), BF16),
-                jax.ShapeDtypeStruct((side, side), F32),
-            ],
+            out_shape=[jax.ShapeDtypeStruct((col_blocks, side, box), BF16), square],
             compiler_params=params(),
             name="gram",
-        )(*chunks)
+                cost_estimate=small_cost,
+        )(tall_counts, *chunks)
         grams = [gram] + [swap(gram, "dst", k) for k in range(1, n_dst)]
     return pl.pallas_call(
-        functools.partial(basis_kernel, box_total, n_dst),
+        functools.partial(basis_kernel, box_total),
         in_specs=[VMEM] * (1 + n_dst),
         out_specs=VMEM,
         out_shape=jax.ShapeDtypeStruct((side, col_blocks * box), F32),
         compiler_params=params(),
         name="basis",
+                cost_estimate=orth_cost,
     )(w_full, *grams)
 
 

time: 130 us -> 104 us (0.80)
  local copies, waits for them, and re-layouts: 17.1 us -> 0.02 us
  waiting for transfers between devices: 40.8 us -> 25.4 us
  Pallas kernels: 43.7 us -> 50.6 us
    unnamed x22 -> x8, local copies, waits for them, and re-layouts: 17.1 us -> 0.02 us
    ppermute x24, waiting for transfers between devices: 40.8 us -> 25.4 us  [swap(): return lax.ppermute(x, axis, [(i, i ^ bits) for i in range(size)])]
    pallas_call x4 -> x7, Pallas kernels: 22.3 us -> 29.7 us  [the longest x1 8.81 us: per_device(): pl.pallas_call(functools.partial(forward_kernel, unroll), in_specs=[SMEM,...]
  transfers between devices with their start and end apart: 24 -> 24, of which waited for: 17 -> 13; matrix products, arithmetic and copies ran while one was open for 0% -> 0% of each run, Pallas kernels for 0% -> 12%
where the time goes in v1:
time: 104 us; the launch traced here: 103 us
  Pallas kernels  50.6 us (49%)
  starting transfers between devices  26.9 us (26%)
  waiting for transfers between devices  25.4 us (24%)
    ppermute x24, starting transfers between devices, swap(): return lax.ppermute(x, axis, [(i, i ^ bits) for i in range(size)])  26.9 us
    ppermute x24, waiting for transfers between devices, swap(): return lax.ppermute(x, axis, [(i, i ^ bits) for i in range(size)])  25.4 us
    pallas_call x2, Pallas kernels, per_device(): pl.pallas_call(functools.partial(adjoint_kernel, unroll, n_src), in_specs...  10.5 us
    pallas_call x1, Pallas kernels, per_device(): pl.pallas_call(functools.partial(first_forward_kernel, unroll), in_specs=...  10.4 us
    pallas_call x1, Pallas kernels, per_device(): pl.pallas_call(functools.partial(forward_kernel, unroll), in_specs=[SMEM,...  8.81 us
    pallas_call x1, Pallas kernels, per_device(): pl.pallas_call(functools.partial(basis_kernel, box_total), in_specs=[VMEM...  7.01 us
    pallas_call x1, Pallas kernels, per_device(): pl.pallas_call(load_kernel, in_specs=[HBM], out_specs=VMEM, out_shape=plt...  6.99 us
    pallas_call x1, Pallas kernels, per_device(): pl.pallas_call(functools.partial(orth_kernel, box_total), in_specs=[VMEM]...  5.84 us
  transfers between devices with their start and end apart: 24, of which 13 were waited for; matrix products, arithmetic and copies ran while one was open for 0% of the time, Pallas kernels for 12%

profile of v1, /device:TPU:0, one launch (start us, length us, event | category | flops | bytes accessed | tf_op | source)
XLA Modules:
  0.0 103.4 jit_solution(13128306137100414015)
XLA Ops:
  0.0 10.4 %first_forward.1 = (f32[32,32,128]{2,1,0:T(8,128)S(1)}, bf16[32,32,128]{2,1,0:T(8,128)(2,1)S(1)}) custom-call(s32[640]{0:T(1024)} %rows_ref.5, s32[640]{0:T(1024)} %cols_ref.5, f32[32,4096]{1,0:T(8,128)} %start_hbm.1, s32[1,4096]{1,0:T(1,128)} %bitcast.7, bf16[640,128,128]{2,1,0:T(8,128)(2,1)} %hbm_ref), custom_call_target="tpu_custom_call" | custom-call | flops 10737418240 | tf_op jit(solution)/shard_map/first_forward/pallas_call | solution.py:317
  10.4 0.5 collective-permute-start
  11.0 1.2 %collective-permute-done = bf16[32,32,128]{2,1,0:T(8,128)(2,1)S(1)} collective-permute-done((bf16[32,32,128]{2,1,0:T(8,128)(2,1)S(1)}, bf16[32,32,128]{2,1,0:T(8,128)(2,1)S(1)}, u32[]{:S(2)}, u32[]{:S(2)}) %collective-permute-start) | collective-permute-done | bytes 262176 | tf_op jit(solution)/shard_map/ppermute | solution.py:287
  12.1 0.1 fusion
  12.2 2.9 %collective-permute-start.1 = (bf16[32,32,128]{2,1,0:T(8,128)(2,1)S(1)}, bf16[32,32,128]{2,1,0:T(8,128)(2,1)S(1)}, u32[]{:S(2)}, u32[]{:S(2)}) collective-permute-start(bf16[32,32,128]{2,1,0:T(8,128)(2,1)S(1)} %fusion), channel_id=1, source_target_pairs={{0,2},{1,3},{2,0},{3,1},{4,6},{5,7},{6,4},{7,5},{8,10},{9,11},{10,... | collective-permute-start | bytes 786440 | tf_op jit(solution)/shard_map/ppermute | solution.py:287
  15.2 7.0 %load.1.blocks_ref = bf16[640,128,128]{2,1,0:T(8,128)(2,1)S(1)} custom-call(bf16[640,128,128]{2,1,0:T(8,128)(2,1)} %hbm_ref), custom_call_target="tpu_custom_call" | custom-call | bytes 41943040 | tf_op jit(solution)/shard_map/load/pallas_call | solution.py:354
  22.2 0.1 convert_add_fusion
  22.3 0.1 collective-permute-start.2
  22.4 1.5 %collective-permute-done.2.other_ref = bf16[32,32,128]{2,1,0:T(8,128)(2,1)S(1)} collective-permute-done((bf16[32,32,128]{2,1,0:T(8,128)(2,1)S(1)}, bf16[32,32,128]{2,1,0:T(8,128)(2,1)S(1)}, u32[]{:S(2)}, u32[]{:S(2)}) %collective-permute-start.2) | collective-permute-done | bytes 262176 | tf_op jit(solution)/shard_map/ppermute | solution.py:287
  23.9 5.2 %adjoint.2 = (f32[8,32,128]{2,1,0:T(8,128)S(1)}, bf16[8,32,128]{2,1,0:T(8,128)(2,1)S(1)}, bf16[8,32,128]{2,1,0:T(8,128)(2,1)S(1)}, bf16[8,32,128]{2,1,0:T(8,128)(2,1)S(1)}) custom-call(s32[640]{0:T(1024)S(1)} %copy-done.1, s32[640]{0:T(1024)S(1)} %copy-done.2, s32[32,1,128]{2,1,0:T(1,128)S(1)} %bitcast.8, bf16[640,128,128]{2,1,0:T(8,128)(2,1)S(1)} %load.1.blocks_ref, ...), custom_call_target="tpu_custom_call" | custom-call | flops 5368709120 | tf_op jit(solution)/shard_map/adjoint/pallas_call | solution.py:395
  29.2 1.7 %collective-permute-start.3 = (bf16[8,32,128]{2,1,0:T(8,128)(2,1)S(1)}, bf16[8,32,128]{2,1,0:T(8,128)(2,1)S(1)}, u32[]{:S(2)}, u32[]{:S(2)}) collective-permute-start(bf16[8,32,128]{2,1,0:T(8,128)(2,1)S(1)} %get-tuple-element.32), channel_id=1, source_target_pairs={{0,4},{4,0},{8,12},{12,8},{1,5},{5,1},{9,13},{13,9},{2,6},{6,2},{1... | collective-permute-start | bytes 196616 | tf_op jit(solution)/shard_map/ppermute | solution.py:287
  30.8 2.6 %collective-permute-start.4 = (bf16[8,32,128]{2,1,0:T(8,128)(2,1)S(1)}, bf16[8,32,128]{2,1,0:T(8,128)(2,1)S(1)}, u32[]{:S(2)}, u32[]{:S(2)}) collective-permute-start(bf16[8,32,128]{2,1,0:T(8,128)(2,1)S(1)} %get-tuple-element.33), channel_id=1, source_target_pairs={{0,8},{4,12},{8,0},{12,4},{1,9},{5,13},{9,1},{13,5},{2,10},{6,14},... | collective-permute-start | bytes 196616 | tf_op jit(solution)/shard_map/ppermute | solution.py:287
  33.4 0.2 collective-permute-start.5
  33.6 4.7 %collective-permute-done.4 = bf16[8,32,128]{2,1,0:T(8,128)(2,1)S(1)} collective-permute-done((bf16[8,32,128]{2,1,0:T(8,128)(2,1)S(1)}, bf16[8,32,128]{2,1,0:T(8,128)(2,1)S(1)}, u32[]{:S(2)}, u32[]{:S(2)}) %collective-permute-start.4) | collective-permute-done | bytes 65568 | tf_op jit(solution)/shard_map/ppermute | solution.py:287
  38.4 1.2 %collective-permute-done.5 = bf16[8,32,128]{2,1,0:T(8,128)(2,1)S(1)} collective-permute-done((bf16[8,32,128]{2,1,0:T(8,128)(2,1)S(1)}, bf16[8,32,128]{2,1,0:T(8,128)(2,1)S(1)}, u32[]{:S(2)}, u32[]{:S(2)}) %collective-permute-start.5) | collective-permute-done | bytes 65568 | tf_op jit(solution)/shard_map/ppermute | solution.py:287
  39.6 2.1 %collective-permute-start.8 = (bf16[8,32,128]{2,1,0:T(8,128)(2,1)S(1)}, bf16[8,32,128]{2,1,0:T(8,128)(2,1)S(1)}, u32[]{:S(2)}, u32[]{:S(2)}) collective-permute-start(bf16[8,32,128]{2,1,0:T(8,128)(2,1)S(1)} %add_convert_fusion.2.refs_0_), channel_id=1, source_target_pairs={{0,12},{4,8},{8,4},{12,0},{1,13},{5,9},{9,5},{13,1},{2,14},{6,10},... | collective-permute-start | bytes 196616 | tf_op jit(solution)/shard_map/ppermute | solution.py:287
  41.7 0.3 collective-permute-start.7
  42.0 2.1 %collective-permute-start.6 = (bf16[8,32,128]{2,1,0:T(8,128)(2,1)S(1)}, bf16[8,32,128]{2,1,0:T(8,128)(2,1)S(1)}, u32[]{:S(2)}, u32[]{:S(2)}) collective-permute-start(bf16[8,32,128]{2,1,0:T(8,128)(2,1)S(1)} %add_convert_fusion.2.refs_0_), channel_id=1, source_target_pairs={{0,4},{4,0},{8,12},{12,8},{1,5},{5,1},{9,13},{13,9},{2,6},{6,2},{1... | collective-permute-start | bytes 196616 | tf_op jit(solution)/shard_map/ppermute | solution.py:287
  44.1 1.8 %collective-permute-done.8.refs_3_ = bf16[8,32,128]{2,1,0:T(8,128)(2,1)S(1)} collective-permute-done((bf16[8,32,128]{2,1,0:T(8,128)(2,1)S(1)}, bf16[8,32,128]{2,1,0:T(8,128)(2,1)S(1)}, u32[]{:S(2)}, u32[]{:S(2)}) %collective-permute-start.8) | collective-permute-done | bytes 65568 | tf_op jit(solution)/shard_map/ppermute | solution.py:287
  45.9 1.5 %collective-permute-done.7.refs_2_ = bf16[8,32,128]{2,1,0:T(8,128)(2,1)S(1)} collective-permute-done((bf16[8,32,128]{2,1,0:T(8,128)(2,1)S(1)}, bf16[8,32,128]{2,1,0:T(8,128)(2,1)S(1)}, u32[]{:S(2)}, u32[]{:S(2)}) %collective-permute-start.7) | collective-permute-done | bytes 65568 | tf_op jit(solution)/shard_map/ppermute | solution.py:287
  47.4 0.2 gram.2
  47.7 8.8 %forward.1 = (f32[32,32,128]{2,1,0:T(8,128)S(1)}, bf16[32,32,128]{2,1,0:T(8,128)(2,1)S(1)}) custom-call(s32[640]{0:T(1024)S(1)} %copy-done.1, s32[640]{0:T(1024)S(1)} %copy-done.2, bf16[640,128,128]{2,1,0:T(8,128)(2,1)S(1)} %load.1.blocks_ref, bf16[32,32,128]{2,1,0:T(8,128)(2,1)S(1)} %get-tuple-element.36.panel_ref), custom_call_target="tpu_custom_call" | custom-call | flops 10737418240 | tf_op jit(solution)/shard_map/forward/pallas_call | solution.py:341
  56.5 0.1 collective-permute-start.12
  56.6 1.4 %collective-permute-start.11 = (f32[32,32]{1,0:T(8,128)S(1)}, f32[32,32]{1,0:T(8,128)S(1)}, u32[]{:S(2)}, u32[]{:S(2)}) collective-permute-start(f32[32,32]{1,0:T(8,128)S(1)} %get-tuple-element.35.refs_0_), channel_id=1, source_target_pairs={{0,3},{1,2},{2,1},{3,0},{4,7},{5,6},{6,5},{7,4},{8,11},{9,10},{10,... | collective-permute-start | bytes 12296 | tf_op jit(solution)/shard_map/ppermute | solution.py:287
  58.0 0.7 collective-permute-start.10
  58.7 0.1 add_convert_fusion
  58.8 1.4 %collective-permute-start.13 = (bf16[32,32,128]{2,1,0:T(8,128)(2,1)S(1)}, bf16[32,32,128]{2,1,0:T(8,128)(2,1)S(1)}, u32[]{:S(2)}, u32[]{:S(2)}) collective-permute-start(bf16[32,32,128]{2,1,0:T(8,128)(2,1)S(1)} %add_convert_fusion), channel_id=1, source_target_pairs={{0,2},{1,3},{2,0},{3,1},{4,6},{5,7},{6,4},{7,5},{8,10},{9,11},{10,... | collective-permute-start | bytes 786440 | tf_op jit(solution)/shard_map/ppermute | solution.py:287
  60.2 1.6 %collective-permute-done.10.refs_2_ = f32[32,32]{1,0:T(8,128)S(1)} collective-permute-done((f32[32,32]{1,0:T(8,128)S(1)}, f32[32,32]{1,0:T(8,128)S(1)}, u32[]{:S(2)}, u32[]{:S(2)}) %collective-permute-start.10) | collective-permute-done | bytes 4128 | tf_op jit(solution)/shard_map/ppermute | solution.py:287
  61.8 5.8 %orth.1.matrix_ref = f32[32,32]{1,0:T(8,128)S(1)} custom-call(f32[32,32]{1,0:T(8,128)S(1)} %get-tuple-element.35.refs_0_, f32[32,32]{1,0:T(8,128)S(1)} %collective-permute-done.9.refs_1_, f32[32,32]{1,0:T(8,128)S(1)} %collective-permute-done.10.refs_2_, f32[32,32]{1,0:T(8,128)S(1)} %collective-permute-done.11.refs_3_), custom_call_target="tpu_custom_call" | custom-call | flops 4294967296 | tf_op jit(solution)/shard_map/orth/pallas_call | solution.py:375
  67.6 0.6 mix.1.mine_ref
  68.2 0.1 collective-permute-start.14
  68.3 1.5 %collective-permute-done.14.other_ref = bf16[32,32,128]{2,1,0:T(8,128)(2,1)S(1)} collective-permute-done((bf16[32,32,128]{2,1,0:T(8,128)(2,1)S(1)}, bf16[32,32,128]{2,1,0:T(8,128)(2,1)S(1)}, u32[]{:S(2)}, u32[]{:S(2)}) %collective-permute-start.14) | collective-permute-done | bytes 262176 | tf_op jit(solution)/shard_map/ppermute | solution.py:287
  69.8 5.2 %adjoint.3 = (f32[8,32,128]{2,1,0:T(8,128)S(1)}, bf16[8,32,128]{2,1,0:T(8,128)(2,1)S(1)}, bf16[8,32,128]{2,1,0:T(8,128)(2,1)S(1)}, bf16[8,32,128]{2,1,0:T(8,128)(2,1)S(1)}) custom-call(s32[640]{0:T(1024)S(1)} %copy-done.1, s32[640]{0:T(1024)S(1)} %copy-done.2, s32[32,1,128]{2,1,0:T(1,128)S(1)} %bitcast.10, bf16[640,128,128]{2,1,0:T(8,128)(2,1)S(1)} %load.1.blocks_ref, ...), custom_call_target="tpu_custom_call" | custom-call | flops 5368709120 | tf_op jit(solution)/shard_map/adjoint/pallas_call | solution.py:395
  75.1 1.0 collective-permute-start.15
  76.0 1.6 %collective-permute-start.16 = (bf16[8,32,128]{2,1,0:T(8,128)(2,1)S(1)}, bf16[8,32,128]{2,1,0:T(8,128)(2,1)S(1)}, u32[]{:S(2)}, u32[]{:S(2)}) collective-permute-start(bf16[8,32,128]{2,1,0:T(8,128)(2,1)S(1)} %get-tuple-element.41), channel_id=1, source_target_pairs={{0,8},{4,12},{8,0},{12,4},{1,9},{5,13},{9,1},{13,5},{2,10},{6,14},... | collective-permute-start | bytes 196616 | tf_op jit(solution)/shard_map/ppermute | solution.py:287
  77.6 1.9 %collective-permute-start.17 = (bf16[8,32,128]{2,1,0:T(8,128)(2,1)S(1)}, bf16[8,32,128]{2,1,0:T(8,128)(2,1)S(1)}, u32[]{:S(2)}, u32[]{:S(2)}) collective-permute-start(bf16[8,32,128]{2,1,0:T(8,128)(2,1)S(1)} %get-tuple-element.42), channel_id=1, source_target_pairs={{0,12},{4,8},{8,4},{12,0},{1,13},{5,9},{9,5},{13,1},{2,14},{6,10},... | collective-permute-start | bytes 196616 | tf_op jit(solution)/shard_map/ppermute | solution.py:287
  79.5 4.8 %collective-permute-done.16 = bf16[8,32,128]{2,1,0:T(8,128)(2,1)S(1)} collective-permute-done((bf16[8,32,128]{2,1,0:T(8,128)(2,1)S(1)}, bf16[8,32,128]{2,1,0:T(8,128)(2,1)S(1)}, u32[]{:S(2)}, u32[]{:S(2)}) %collective-permute-start.16) | collective-permute-done | bytes 65568 | tf_op jit(solution)/shard_map/ppermute | solution.py:287
  84.3 2.1 %collective-permute-start.20 = (bf16[8,32,128]{2,1,0:T(8,128)(2,1)S(1)}, bf16[8,32,128]{2,1,0:T(8,128)(2,1)S(1)}, u32[]{:S(2)}, u32[]{:S(2)}) collective-permute-start(bf16[8,32,128]{2,1,0:T(8,128)(2,1)S(1)} %add_convert_fusion.1.refs_0_), channel_id=1, source_target_pairs={{0,12},{4,8},{8,4},{12,0},{1,13},{5,9},{9,5},{13,1},{2,14},{6,10},... | collective-permute-start | bytes 196616 | tf_op jit(solution)/shard_map/ppermute | solution.py:287
  86.4 0.7 collective-permute-start.19
  87.1 1.7 %collective-permute-start.18 = (bf16[8,32,128]{2,1,0:T(8,128)(2,1)S(1)}, bf16[8,32,128]{2,1,0:T(8,128)(2,1)S(1)}, u32[]{:S(2)}, u32[]{:S(2)}) collective-permute-start(bf16[8,32,128]{2,1,0:T(8,128)(2,1)S(1)} %add_convert_fusion.1.refs_0_), channel_id=1, source_target_pairs={{0,4},{4,0},{8,12},{12,8},{1,5},{5,1},{9,13},{13,9},{2,6},{6,2},{1... | collective-permute-start | bytes 196616 | tf_op jit(solution)/shard_map/ppermute | solution.py:287
  88.8 2.0 %collective-permute-done.20.refs_3_ = bf16[8,32,128]{2,1,0:T(8,128)(2,1)S(1)} collective-permute-done((bf16[8,32,128]{2,1,0:T(8,128)(2,1)S(1)}, bf16[8,32,128]{2,1,0:T(8,128)(2,1)S(1)}, u32[]{:S(2)}, u32[]{:S(2)}) %collective-permute-start.20) | collective-permute-done | bytes 65568 | tf_op jit(solution)/shard_map/ppermute | solution.py:287
  90.8 1.6 %collective-permute-done.19.refs_2_ = bf16[8,32,128]{2,1,0:T(8,128)(2,1)S(1)} collective-permute-done((bf16[8,32,128]{2,1,0:T(8,128)(2,1)S(1)}, bf16[8,32,128]{2,1,0:T(8,128)(2,1)S(1)}, u32[]{:S(2)}, u32[]{:S(2)}) %collective-permute-start.19) | collective-permute-done | bytes 65568 | tf_op jit(solution)/shard_map/ppermute | solution.py:287
  92.3 0.2 gram.3
  92.6 1.3 %collective-permute-start.22 = (f32[32,32]{1,0:T(8,128)S(1)}, f32[32,32]{1,0:T(8,128)S(1)}, u32[]{:S(2)}, u32[]{:S(2)}) collective-permute-start(f32[32,32]{1,0:T(8,128)S(1)} %get-tuple-element.44.refs_0_), channel_id=1, source_target_pairs={{0,2},{1,3},{2,0},{3,1},{4,6},{5,7},{6,4},{7,5},{8,10},{9,11},{10,... | collective-permute-start | bytes 12296 | tf_op jit(solution)/shard_map/ppermute | solution.py:287
  93.9 0.5 collective-permute-start.21
  94.4 1.3 %collective-permute-done.23.refs_3_ = f32[32,32]{1,0:T(8,128)S(1)} collective-permute-done((f32[32,32]{1,0:T(8,128)S(1)}, f32[32,32]{1,0:T(8,128)S(1)}, u32[]{:S(2)}, u32[]{:S(2)}) %collective-permute-start.23) | collective-permute-done | bytes 4128 | tf_op jit(solution)/shard_map/ppermute | solution.py:287
  95.8 0.6 collective-permute-done.22.refs_2_
  96.4 7.0 %basis.1 = f32[32,4096]{1,0:T(8,128)} custom-call(bf16[32,32,128]{2,1,0:T(8,128)(2,1)S(1)} %get-tuple-element.43.w_ref, f32[32,32]{1,0:T(8,128)S(1)} %get-tuple-element.44.refs_0_, f32[32,32]{1,0:T(8,128)S(1)} %collective-permute-done.21.refs_1_, f32[32,32]{1,0:T(8,128)S(1)} %collective-permute-done.22.refs_2_, f32[32,32]{1,0:T(8,128)S(1)} %collective-permute-done.23.refs_3_), custom_call_target="tpu_custom_call" | custom-call | flops 4294967296 | tf_op jit(solution)/shard_map/basis/pallas_call | solution.py:423
  (25 shorter events, 0.2 us)
Async XLA Ops:
  0.0 15.1 %copy-start.3 = (s32[8192]{0:T(1024)S(1)}, s32[8192]{0:T(1024)}, u32[]{:S(2)}) copy-start(s32[8192]{0:T(1024)} %param.9) | copy-start | bytes 98308
  10.4 1.7 %collective-permute-start = (bf16[32,32,128]{2,1,0:T(8,128)(2,1)S(1)}, bf16[32,32,128]{2,1,0:T(8,128)(2,1)S(1)}, u32[]{:S(2)}, u32[]{:S(2)}) collective-permute-start(bf16[32,32,128]{2,1,0:T(8,128)(2,1)S(1)} %get-tuple-element.26), channel_id=1, source_target_pairs={{0,1},{1,0},{2,3},{3,2},{4,5},{5,4},{6,7},{7,6},{8,9},{9,8},{10,11... | collective-permute-start | bytes 786440 | tf_op jit(solution)/shard_map/ppermute | solution.py:287
  12.2 10.0 %collective-permute-start.1 = (bf16[32,32,128]{2,1,0:T(8,128)(2,1)S(1)}, bf16[32,32,128]{2,1,0:T(8,128)(2,1)S(1)}, u32[]{:S(2)}, u32[]{:S(2)}) collective-permute-start(bf16[32,32,128]{2,1,0:T(8,128)(2,1)S(1)} %fusion), channel_id=1, source_target_pairs={{0,2},{1,3},{2,0},{3,1},{4,6},{5,7},{6,4},{7,5},{8,10},{9,11},{10,... | collective-permute-start | bytes 786440 | tf_op jit(solution)/shard_map/ppermute | solution.py:287
  15.1 8.8 %copy-start = (s32[4096]{0:T(1024)S(1)}, s32[4096]{0:T(1024)}, u32[]{:S(2)}) copy-start(s32[4096]{0:T(1024)} %param.10) | copy-start | bytes 49156
  15.1 8.8 %copy-start.1 = (s32[640]{0:T(1024)S(1)}, s32[640]{0:T(1024)}, u32[]{:S(2)}) copy-start(s32[640]{0:T(1024)} %rows_ref.5) | copy-start | bytes 7684
  15.1 8.8 %copy-start.2 = (s32[640]{0:T(1024)S(1)}, s32[640]{0:T(1024)}, u32[]{:S(2)}) copy-start(s32[640]{0:T(1024)} %cols_ref.5) | copy-start | bytes 7684
  22.3 1.6 %collective-permute-start.2 = (bf16[32,32,128]{2,1,0:T(8,128)(2,1)S(1)}, bf16[32,32,128]{2,1,0:T(8,128)(2,1)S(1)}, u32[]{:S(2)}, u32[]{:S(2)}) collective-permute-start(bf16[32,32,128]{2,1,0:T(8,128)(2,1)S(1)} %divide_convert_fusion.mine_ref), channel_id=1, source_target_pairs={{0,1},{1,0},{2,3},{3,2},{4,5},{5,4},{6,7},{7,6},{8,9},{9,8},{10,11... | collective-permute-start | bytes 786440 | tf_op jit(solution)/shard_map/ppermute | solution.py:287
  29.2 4.5 %collective-permute-start.3 = (bf16[8,32,128]{2,1,0:T(8,128)(2,1)S(1)}, bf16[8,32,128]{2,1,0:T(8,128)(2,1)S(1)}, u32[]{:S(2)}, u32[]{:S(2)}) collective-permute-start(bf16[8,32,128]{2,1,0:T(8,128)(2,1)S(1)} %get-tuple-element.32), channel_id=1, source_target_pairs={{0,4},{4,0},{8,12},{12,8},{1,5},{5,1},{9,13},{13,9},{2,6},{6,2},{1... | collective-permute-start | bytes 196616 | tf_op jit(solution)/shard_map/ppermute | solution.py:287
  30.8 7.5 %collective-permute-start.4 = (bf16[8,32,128]{2,1,0:T(8,128)(2,1)S(1)}, bf16[8,32,128]{2,1,0:T(8,128)(2,1)S(1)}, u32[]{:S(2)}, u32[]{:S(2)}) collective-permute-start(bf16[8,32,128]{2,1,0:T(8,128)(2,1)S(1)} %get-tuple-element.33), channel_id=1, source_target_pairs={{0,8},{4,12},{8,0},{12,4},{1,9},{5,13},{9,1},{13,5},{2,10},{6,14},... | collective-permute-start | bytes 196616 | tf_op jit(solution)/shard_map/ppermute | solution.py:287
  33.4 6.2 %collective-permute-start.5 = (bf16[8,32,128]{2,1,0:T(8,128)(2,1)S(1)}, bf16[8,32,128]{2,1,0:T(8,128)(2,1)S(1)}, u32[]{:S(2)}, u32[]{:S(2)}) collective-permute-start(bf16[8,32,128]{2,1,0:T(8,128)(2,1)S(1)} %get-tuple-element.34), channel_id=1, source_target_pairs={{0,12},{4,8},{8,4},{12,0},{1,13},{5,9},{9,5},{13,1},{2,14},{6,10},... | collective-permute-start | bytes 196616 | tf_op jit(solution)/shard_map/ppermute | solution.py:287
  39.6 6.3 %collective-permute-start.8 = (bf16[8,32,128]{2,1,0:T(8,128)(2,1)S(1)}, bf16[8,32,128]{2,1,0:T(8,128)(2,1)S(1)}, u32[]{:S(2)}, u32[]{:S(2)}) collective-permute-start(bf16[8,32,128]{2,1,0:T(8,128)(2,1)S(1)} %add_convert_fusion.2.refs_0_), channel_id=1, source_target_pairs={{0,12},{4,8},{8,4},{12,0},{1,13},{5,9},{9,5},{13,1},{2,14},{6,10},... | collective-permute-start | bytes 196616 | tf_op jit(solution)/shard_map/ppermute | solution.py:287
  41.7 5.7 %collective-permute-start.7 = (bf16[8,32,128]{2,1,0:T(8,128)(2,1)S(1)}, bf16[8,32,128]{2,1,0:T(8,128)(2,1)S(1)}, u32[]{:S(2)}, u32[]{:S(2)}) collective-permute-start(bf16[8,32,128]{2,1,0:T(8,128)(2,1)S(1)} %add_convert_fusion.2.refs_0_), channel_id=1, source_target_pairs={{0,8},{4,12},{8,0},{12,4},{1,9},{5,13},{9,1},{13,5},{2,10},{6,14},... | collective-permute-start | bytes 196616 | tf_op jit(solution)/shard_map/ppermute | solution.py:287
  42.0 5.4 %collective-permute-start.6 = (bf16[8,32,128]{2,1,0:T(8,128)(2,1)S(1)}, bf16[8,32,128]{2,1,0:T(8,128)(2,1)S(1)}, u32[]{:S(2)}, u32[]{:S(2)}) collective-permute-start(bf16[8,32,128]{2,1,0:T(8,128)(2,1)S(1)} %add_convert_fusion.2.refs_0_), channel_id=1, source_target_pairs={{0,4},{4,0},{8,12},{12,8},{1,5},{5,1},{9,13},{13,9},{2,6},{6,2},{1... | collective-permute-start | bytes 196616 | tf_op jit(solution)/shard_map/ppermute | solution.py:287
  56.5 2.2 %collective-permute-start.12 = (bf16[32,32,128]{2,1,0:T(8,128)(2,1)S(1)}, bf16[32,32,128]{2,1,0:T(8,128)(2,1)S(1)}, u32[]{:S(2)}, u32[]{:S(2)}) collective-permute-start(bf16[32,32,128]{2,1,0:T(8,128)(2,1)S(1)} %get-tuple-element.38), channel_id=1, source_target_pairs={{0,1},{1,0},{2,3},{3,2},{4,5},{5,4},{6,7},{7,6},{8,9},{9,8},{10,11... | collective-permute-start | bytes 786440 | tf_op jit(solution)/shard_map/ppermute | solution.py:287
  56.6 3.6 %collective-permute-start.11 = (f32[32,32]{1,0:T(8,128)S(1)}, f32[32,32]{1,0:T(8,128)S(1)}, u32[]{:S(2)}, u32[]{:S(2)}) collective-permute-start(f32[32,32]{1,0:T(8,128)S(1)} %get-tuple-element.35.refs_0_), channel_id=1, source_target_pairs={{0,3},{1,2},{2,1},{3,0},{4,7},{5,6},{6,5},{7,4},{8,11},{9,10},{10,... | collective-permute-start | bytes 12296 | tf_op jit(solution)/shard_map/ppermute | solution.py:287
  58.0 3.7 %collective-permute-start.10 = (f32[32,32]{1,0:T(8,128)S(1)}, f32[32,32]{1,0:T(8,128)S(1)}, u32[]{:S(2)}, u32[]{:S(2)}) collective-permute-start(f32[32,32]{1,0:T(8,128)S(1)} %get-tuple-element.35.refs_0_), channel_id=1, source_target_pairs={{0,2},{1,3},{2,0},{3,1},{4,6},{5,7},{6,4},{7,5},{8,10},{9,11},{10,... | collective-permute-start | bytes 12296 | tf_op jit(solution)/shard_map/ppermute | solution.py:287
  58.7 3.0 %collective-permute-start.9 = (f32[32,32]{1,0:T(8,128)S(1)}, f32[32,32]{1,0:T(8,128)S(1)}, u32[]{:S(2)}, u32[]{:S(2)}) collective-permute-start(f32[32,32]{1,0:T(8,128)S(1)} %get-tuple-element.35.refs_0_), channel_id=1, source_target_pairs={{0,1},{1,0},{2,3},{3,2},{4,5},{5,4},{6,7},{7,6},{8,9},{9,8},{10,11... | collective-permute-start | bytes 12296 | tf_op jit(solution)/shard_map/ppermute | solution.py:287
  58.8 8.8 %collective-permute-start.13 = (bf16[32,32,128]{2,1,0:T(8,128)(2,1)S(1)}, bf16[32,32,128]{2,1,0:T(8,128)(2,1)S(1)}, u32[]{:S(2)}, u32[]{:S(2)}) collective-permute-start(bf16[32,32,128]{2,1,0:T(8,128)(2,1)S(1)} %add_convert_fusion), channel_id=1, source_target_pairs={{0,2},{1,3},{2,0},{3,1},{4,6},{5,7},{6,4},{7,5},{8,10},{9,11},{10,... | collective-permute-start | bytes 786440 | tf_op jit(solution)/shard_map/ppermute | solution.py:287
  68.2 1.6 %collective-permute-start.14 = (bf16[32,32,128]{2,1,0:T(8,128)(2,1)S(1)}, bf16[32,32,128]{2,1,0:T(8,128)(2,1)S(1)}, u32[]{:S(2)}, u32[]{:S(2)}) collective-permute-start(bf16[32,32,128]{2,1,0:T(8,128)(2,1)S(1)} %mix.1.mine_ref), channel_id=1, source_target_pairs={{0,1},{1,0},{2,3},{3,2},{4,5},{5,4},{6,7},{7,6},{8,9},{9,8},{10,11... | collective-permute-start | bytes 786440 | tf_op jit(solution)/shard_map/ppermute | solution.py:287
  75.1 4.5 %collective-permute-start.15 = (bf16[8,32,128]{2,1,0:T(8,128)(2,1)S(1)}, bf16[8,32,128]{2,1,0:T(8,128)(2,1)S(1)}, u32[]{:S(2)}, u32[]{:S(2)}) collective-permute-start(bf16[8,32,128]{2,1,0:T(8,128)(2,1)S(1)} %get-tuple-element.40), channel_id=1, source_target_pairs={{0,4},{4,0},{8,12},{12,8},{1,5},{5,1},{9,13},{13,9},{2,6},{6,2},{1... | collective-permute-start | bytes 196616 | tf_op jit(solution)/shard_map/ppermute | solution.py:287
  76.0 8.3 %collective-permute-start.16 = (bf16[8,32,128]{2,1,0:T(8,128)(2,1)S(1)}, bf16[8,32,128]{2,1,0:T(8,128)(2,1)S(1)}, u32[]{:S(2)}, u32[]{:S(2)}) collective-permute-start(bf16[8,32,128]{2,1,0:T(8,128)(2,1)S(1)} %get-tuple-element.41), channel_id=1, source_target_pairs={{0,8},{4,12},{8,0},{12,4},{1,9},{5,13},{9,1},{13,5},{2,10},{6,14},... | collective-permute-start | bytes 196616 | tf_op jit(solution)/shard_map/ppermute | solution.py:287
  77.6 6.7 %collective-permute-start.17 = (bf16[8,32,128]{2,1,0:T(8,128)(2,1)S(1)}, bf16[8,32,128]{2,1,0:T(8,128)(2,1)S(1)}, u32[]{:S(2)}, u32[]{:S(2)}) collective-permute-start(bf16[8,32,128]{2,1,0:T(8,128)(2,1)S(1)} %get-tuple-element.42), channel_id=1, source_target_pairs={{0,12},{4,8},{8,4},{12,0},{1,13},{5,9},{9,5},{13,1},{2,14},{6,10},... | collective-permute-start | bytes 196616 | tf_op jit(solution)/shard_map/ppermute | solution.py:287
  84.3 6.4 %collective-permute-start.20 = (bf16[8,32,128]{2,1,0:T(8,128)(2,1)S(1)}, bf16[8,32,128]{2,1,0:T(8,128)(2,1)S(1)}, u32[]{:S(2)}, u32[]{:S(2)}) collective-permute-start(bf16[8,32,128]{2,1,0:T(8,128)(2,1)S(1)} %add_convert_fusion.1.refs_0_), channel_id=1, source_target_pairs={{0,12},{4,8},{8,4},{12,0},{1,13},{5,9},{9,5},{13,1},{2,14},{6,10},... | collective-permute-start | bytes 196616 | tf_op jit(solution)/shard_map/ppermute | solution.py:287
  86.4 5.9 %collective-permute-start.19 = (bf16[8,32,128]{2,1,0:T(8,128)(2,1)S(1)}, bf16[8,32,128]{2,1,0:T(8,128)(2,1)S(1)}, u32[]{:S(2)}, u32[]{:S(2)}) collective-permute-start(bf16[8,32,128]{2,1,0:T(8,128)(2,1)S(1)} %add_convert_fusion.1.refs_0_), channel_id=1, source_target_pairs={{0,8},{4,12},{8,0},{12,4},{1,9},{5,13},{9,1},{13,5},{2,10},{6,14},... | collective-permute-start | bytes 196616 | tf_op jit(solution)/shard_map/ppermute | solution.py:287
  87.1 5.2 %collective-permute-start.18 = (bf16[8,32,128]{2,1,0:T(8,128)(2,1)S(1)}, bf16[8,32,128]{2,1,0:T(8,128)(2,1)S(1)}, u32[]{:S(2)}, u32[]{:S(2)}) collective-permute-start(bf16[8,32,128]{2,1,0:T(8,128)(2,1)S(1)} %add_convert_fusion.1.refs_0_), channel_id=1, source_target_pairs={{0,4},{4,0},{8,12},{12,8},{1,5},{5,1},{9,13},{13,9},{2,6},{6,2},{1... | collective-permute-start | bytes 196616 | tf_op jit(solution)/shard_map/ppermute | solution.py:287
  92.6 3.2 %collective-permute-start.23 = (f32[32,32]{1,0:T(8,128)S(1)}, f32[32,32]{1,0:T(8,128)S(1)}, u32[]{:S(2)}, u32[]{:S(2)}) collective-permute-start(f32[32,32]{1,0:T(8,128)S(1)} %get-tuple-element.44.refs_0_), channel_id=1, source_target_pairs={{0,3},{1,2},{2,1},{3,0},{4,7},{5,6},{6,5},{7,4},{8,11},{9,10},{10,... | collective-permute-start | bytes 12296 | tf_op jit(solution)/shard_map/ppermute | solution.py:287
  92.6 3.8 %collective-permute-start.22 = (f32[32,32]{1,0:T(8,128)S(1)}, f32[32,32]{1,0:T(8,128)S(1)}, u32[]{:S(2)}, u32[]{:S(2)}) collective-permute-start(f32[32,32]{1,0:T(8,128)S(1)} %get-tuple-element.44.refs_0_), channel_id=1, source_target_pairs={{0,2},{1,3},{2,0},{3,1},{4,6},{5,7},{6,4},{7,5},{8,10},{9,11},{10,... | collective-permute-start | bytes 12296 | tf_op jit(solution)/shard_map/ppermute | solution.py:287
  93.9 2.5 %collective-permute-start.21 = (f32[32,32]{1,0:T(8,128)S(1)}, f32[32,32]{1,0:T(8,128)S(1)}, u32[]{:S(2)}, u32[]{:S(2)}) collective-permute-start(f32[32,32]{1,0:T(8,128)S(1)} %get-tuple-element.44.refs_0_), channel_id=1, source_target_pairs={{0,1},{1,0},{2,3},{3,2},{4,5},{5,4},{6,7},{7,6},{8,9},{9,8},{10,11... | collective-permute-start | bytes 12296 | tf_op jit(solution)/shard_map/ppermute | solution.py:287

commit v2 on v1

--- a/solution.py
+++ b/solution.py
@@ -8,6 +8,7 @@
 from jax.sharding import PartitionSpec as P
 
 ITERS = 2
+TURNED = 3
 F32 = jnp.float32
 BF16 = jnp.bfloat16
 VMEM = pl.BlockSpec(memory_space=pltpu.VMEM)
@@ -35,11 +36,10 @@
     )
 
 
-def unroll_of(total):
-    for size in (128, 64, 32, 16, 8, 4, 2, 1):
-        if total % size == 0:
-            return size
-    return 1
+def unroll_of(total, most):
+    while total % most:
+        most //= 2
+    return most
 
 
 def add_group(pieces, ids_ref, first, base, accs):
@@ -49,23 +49,23 @@
         acc[place] += piece
 
 
-def forward_group(panel_ref, cols_ref, col_base, blocks_ref, first, start, size):
+def forward_group(panel_ref, cols_ref, col_base, block_at, first, size):
     pieces = []
-    side = panel_ref.shape[1]
+    side, box = panel_ref.shape[1:]
     for t in range(0, size, 2):
-        one = panel_ref[cols_ref[first + t] - col_base]
-        two = panel_ref[cols_ref[first + t + 1] - col_base]
-        zero = jnp.zeros_like(one)
         left = jnp.concatenate(
-            [jnp.concatenate([one, zero], 1), jnp.concatenate([zero, two], 1)], 0
+            [
+                panel_ref[cols_ref[first + t] - col_base],
+                panel_ref[cols_ref[first + t + 1] - col_base],
+            ],
+            0,
         )
-        right = jnp.concatenate([blocks_ref[start + t], blocks_ref[start + t + 1]], 1)
-        out = dot_nt(left, right)
-        pieces += [out[:side], out[side:]]
+        out = dot_nn(left, jnp.concatenate([block_at(t), block_at(t + 1)], 1))
+        pieces += [out[:side, :box], out[side:, box:]]
     return pieces
 
 
-def adjoint_group(panel_ref, rows_ref, row_base, blocks_ref, first, size):
+def adjoint_group(panel_ref, rows_ref, row_base, held_ref, first, size):
     pieces = []
     side, box = panel_ref.shape[1:]
     for t in range(0, size, 2):
@@ -76,7 +76,7 @@
             ],
             0,
         )
-        right = jnp.concatenate([blocks_ref[first + t], blocks_ref[first + t + 1]], 1)
+        right = jnp.concatenate([held_ref[first + t], held_ref[first + t + 1]], 1)
         out = dot_nn(left, right)
         pieces += [out[:side, :box], out[side:, box:]]
     return pieces
@@ -84,16 +84,34 @@
 
 def inverse_factor(gram):
     side = gram.shape[0]
-    row_ids = lax.broadcasted_iota(jnp.int32, (side, 2 * side), 0)
-    col_ids = lax.broadcasted_iota(jnp.int32, (side, 2 * side), 1)
-    eye = (col_ids == row_ids + side).astype(F32)
-    work = jnp.concatenate([gram, jnp.zeros_like(gram)], 1) + eye
-    for j in range(side - 1):
-        pivot_row = work[j : j + 1, :]
-        scaled_row = pivot_row / work[j : j + 1, j : j + 1]
-        column = jnp.where(row_ids[:, :1] > j, work[:, j : j + 1], 0.0)
-        work = work - column * scaled_row
-    diag = jnp.sum(jnp.where(col_ids == row_ids, work, 0.0), axis=1, keepdims=True)
+    row = lax.broadcasted_iota(jnp.int32, (side, 2 * side), 0)
+    col = lax.broadcasted_iota(jnp.int32, (side, 2 * side), 1)
+    work = jnp.concatenate([gram, jnp.zeros_like(gram)], 1) + (col == row + side).astype(F32)
+    for j in range(0, side, 4):
+        column = [jnp.broadcast_to(work[:, j + k : j + k + 1], work.shape) for k in range(4)]
+        r0, r1, r2, r3 = [work[j + k : j + k + 1, :] for k in range(4)]
+        at = [[column[k][j + i : j + i + 1, :] for k in range(4)] for i in range(4)]
+        a, b, c = at[0][0], at[1][0], at[1][1]
+        inv = 1.0 / (a * c - b * b)
+        ia, ib, ic = c * inv, -b * inv, a * inv
+        t0, t1 = ia * r0 + ib * r1, ib * r0 + ic * r1
+        p0, p1, q0, q1 = at[2][0], at[2][1], at[3][0], at[3][1]
+        gp0, gp1 = ia * p0 + ib * p1, ib * p0 + ic * p1
+        gq0, gq1 = ia * q0 + ib * q1, ib * q0 + ic * q1
+        sa = at[2][2] - (p0 * gp0 + p1 * gp1)
+        sb = at[3][2] - (q0 * gp0 + q1 * gp1)
+        sc = at[3][3] - (q0 * gq0 + q1 * gq1)
+        n1 = r1 - (b / a) * r0
+        n2 = r2 - (p0 * t0 + p1 * t1)
+        n3 = r3 - (q0 * t0 + q1 * t1)
+        inv_s = 1.0 / (sa * sc - sb * sb)
+        u0, u1 = (sc * n2 - sb * n3) * inv_s, (sa * n3 - sb * n2) * inv_s
+        v0, v1 = t0 - (gp0 * u0 + gq0 * u1), t1 - (gp1 * u0 + gq1 * u1)
+        below = work - ((column[0] * v0 + column[1] * v1) + (column[2] * u0 + column[3] * u1))
+        work = jnp.where(row > j + 3, below, work)
+        for k, new in ((1, n1), (2, n2), (3, n3 - (sb / sa) * n2)):
+            work = jnp.where(row == j + k, new, work)
+    diag = jnp.sum(jnp.where(col == row, work, 0.0), axis=1, keepdims=True)
     return work[:, side:] / jnp.sqrt(diag)
 
 
@@ -175,7 +193,9 @@
     def step(i, carry):
         slot = lax.rem(i, slots)
         part(i, slot).wait()
-        pieces = forward_group(panel_ref, cols_ref, col_base, blocks_ref.at[slot], i * unroll, 0, unroll)
+        pieces = forward_group(
+            panel_ref, cols_ref, col_base, lambda t: blocks_ref[slot, t].T, i * unroll, unroll
+        )
         add_group(pieces, rows_ref, i * unroll, row_base, (acc_a, acc_b))
 
         @pl.when(i + slots < steps)
@@ -188,13 +208,25 @@
     split_halves((acc_a, acc_b), lax.axis_index("dst") % 2, keep_ref, send_ref)
 
 
-def load_kernel(hbm_ref, held_ref, sem):
-    copy = pltpu.make_async_copy(hbm_ref, held_ref, sem)
-    copy.start()
-    copy.wait()
-
-
-def forward_kernel(unroll, rows_ref, cols_ref, blocks_ref, panel_ref, keep_ref, send_ref, acc_a, acc_b):
+def load_kernel(unroll, turned, hbm_ref, held_ref, sems):
+    total = hbm_ref.shape[0]
+    steps = total // unroll
+
+    def part(i):
+        span = pl.ds(i * unroll, unroll)
+        return pltpu.make_async_copy(hbm_ref.at[span], held_ref.at[span], sems.at[i])
+
+    for i in range(steps):
+        part(i).start()
+
+    for i in range(steps):
+        part(i).wait()
+        for t in range(turned):
+            held_ref[total + i * turned + t] = held_ref[i * unroll + t].T
+
+
+def forward_kernel(unroll, turned, rows_ref, cols_ref, held_ref, panel_ref, keep_ref, send_ref, acc_a, acc_b):
+    total = rows_ref.shape[0]
     row_base = lax.axis_index("src") * acc_a.shape[0]
     col_base = lax.axis_index("dst") * panel_ref.shape[0]
     acc_a[...] = jnp.zeros_like(acc_a)
@@ -202,15 +234,21 @@
 
     def step(i, carry):
         first = i * unroll
-        pieces = forward_group(panel_ref, cols_ref, col_base, blocks_ref, first, first, unroll)
+
+        def block_at(t):
+            if t < turned:
+                return held_ref[total + i * turned + t]
+            return held_ref[first + t].T
+
+        pieces = forward_group(panel_ref, cols_ref, col_base, block_at, first, unroll)
         add_group(pieces, rows_ref, first, row_base, (acc_a, acc_b))
         return carry
 
-    lax.fori_loop(0, blocks_ref.shape[0] // unroll, step, 0)
+    lax.fori_loop(0, total // unroll, step, 0)
     split_halves((acc_a, acc_b), lax.axis_index("dst") % 2, keep_ref, send_ref)
 
 
-def adjoint_kernel(unroll, n_src, rows_ref, cols_ref, counts_ref, blocks_ref, mine_ref, other_ref, *refs):
+def adjoint_kernel(unroll, n_src, rows_ref, cols_ref, counts_ref, held_ref, mine_ref, other_ref, *refs):
     keep_ref, send_refs = refs[0], refs[1:n_src]
     panel_ref, acc_a, acc_b = refs[n_src:]
     core = lax.axis_index("dst") % 2
@@ -225,11 +263,11 @@
 
     def step(i, carry):
         first = i * unroll
-        pieces = adjoint_group(panel_ref, rows_ref, row_base, blocks_ref, first, unroll)
+        pieces = adjoint_group(panel_ref, rows_ref, row_base, held_ref, first, unroll)
         add_group(pieces, cols_ref, first, col_base, (acc_a, acc_b))
         return carry
 
-    lax.fori_loop(0, blocks_ref.shape[0] // unroll, step, 0)
+    lax.fori_loop(0, rows_ref.shape[0] // unroll, step, 0)
     size = keep_ref.shape[0]
     for k in range(n_src):
         span = pl.ds((source ^ k) * size, size)
@@ -294,7 +332,8 @@
     col_blocks = col_counts.shape[0] // box
     n_src, n_dst = lax.axis_size("src"), lax.axis_size("dst")
     box_total = float(col_blocks * box * n_dst)
-    unroll = unroll_of(total)
+    unroll = unroll_of(total, 128)
+    turned = unroll * TURNED // 8
     half = row_blocks // 2
     size = col_blocks // n_src
     wide_counts = col_counts.reshape(1, col_blocks * box)
@@ -339,7 +378,7 @@
             ])
         else:
             keep, send = pl.pallas_call(
-                functools.partial(forward_kernel, unroll),
+                functools.partial(forward_kernel, unroll, turned),
                 in_specs=[SMEM, SMEM, VMEM, VMEM],
                 out_specs=[VMEM, VMEM],
                 out_shape=[keep_out, send_out],
@@ -352,11 +391,11 @@
         if sweep == 0:
             again, core_got = lax.optimization_barrier((blocks, core_got))
             held = pl.pallas_call(
-                load_kernel,
+                functools.partial(load_kernel, unroll, turned),
                 in_specs=[HBM],
                 out_specs=VMEM,
-                out_shape=pltpu.VMEM(blocks.shape, BF16),
-                scratch_shapes=[pltpu.SemaphoreType.DMA],
+                out_shape=pltpu.VMEM((total + total // unroll * turned, box, box), BF16),
+                scratch_shapes=[pltpu.SemaphoreType.DMA((total // unroll,))],
                 compiler_params=params(2),
                 name="load",
                 cost_estimate=cost(0, 2 * total * box * box * 2),

time: 104 us -> 96.6 us (0.929)
  Pallas kernels: 50.6 us -> 40.4 us
  waiting for transfers between devices: 25.4 us -> 29.1 us
    ppermute x24, waiting for transfers between devices: 25.4 us -> 29.1 us  [swap(): return lax.ppermute(x, axis, [(i, i ^ bits) for i in range(size)])]
    pallas_call x1, Pallas kernels: 7.01 us -> 3.8 us  [per_device(): pl.pallas_call(functools.partial(basis_kernel, box_total), in_specs=[VMEM...]
    pallas_call x1, Pallas kernels: 5.84 us -> 2.64 us  [per_device(): pl.pallas_call(functools.partial(orth_kernel, box_total), in_specs=[VMEM]...]
    pallas_call x2, Pallas kernels: 15.8 us -> 13.4 us  [the longest x1 7.55 us: per_device(): pl.pallas_call(functools.partial(load_kernel, unroll, turned), in_specs=[...]
    pallas_call x1, Pallas kernels: 10.4 us -> 8.99 us  [per_device(): pl.pallas_call(functools.partial(first_forward_kernel, unroll), in_specs=...]
  transfers between devices with their start and end apart: 24 -> 24, of which waited for: 13 -> 15; matrix products, arithmetic and copies ran while one was open for 0% -> 0% of each run, Pallas kernels for 12% -> 11%
where the time goes in v2:
time: 96.6 us; the launch traced here: 96.4 us
  Pallas kernels  40.4 us (42%)
  waiting for transfers between devices  29.1 us (30%)
  starting transfers between devices  26.3 us (27%)
    ppermute x24, waiting for transfers between devices, swap(): return lax.ppermute(x, axis, [(i, i ^ bits) for i in range(size)])  29.1 us
    ppermute x24, starting transfers between devices, swap(): return lax.ppermute(x, axis, [(i, i ^ bits) for i in range(size)])  26.3 us
    pallas_call x2, Pallas kernels, per_device(): pl.pallas_call(functools.partial(adjoint_kernel, unroll, n_src), in_specs...  10.5 us
    pallas_call x1, Pallas kernels, per_device(): pl.pallas_call(functools.partial(first_forward_kernel, unroll), in_specs=...  8.99 us
    pallas_call x1, Pallas kernels, per_device(): pl.pallas_call(functools.partial(load_kernel, unroll, turned), in_specs=[...  7.55 us
    pallas_call x1, Pallas kernels, per_device(): pl.pallas_call(functools.partial(forward_kernel, unroll, turned), in_spec...  5.86 us
    pallas_call x1, Pallas kernels, per_device(): pl.pallas_call(functools.partial(basis_kernel, box_total), in_specs=[VMEM...  3.8 us
    pallas_call x1, Pallas kernels, per_device(): pl.pallas_call(functools.partial(orth_kernel, box_total), in_specs=[VMEM]...  2.64 us
  transfers between devices with their start and end apart: 24, of which 15 were waited for; matrix products, arithmetic and copies ran while one was open for 0% of the time, Pallas kernels for 11%

profile of v2, /device:TPU:0, one launch (start us, length us, event | category | flops | bytes accessed | tf_op | source)
XLA Modules:
  0.0 96.4 jit_solution(17550757393260463803)
XLA Ops:
  0.0 9.0 %first_forward.1 = (f32[32,32,128]{2,1,0:T(8,128)S(1)}, bf16[32,32,128]{2,1,0:T(8,128)(2,1)S(1)}) custom-call(s32[640]{0:T(1024)} %rows_ref.5, s32[640]{0:T(1024)} %cols_ref.5, f32[32,4096]{1,0:T(8,128)} %start_hbm.1, s32[1,4096]{1,0:T(1,128)} %bitcast.6, bf16[640,128,128]{2,1,0:T(8,128)(2,1)} %hbm_ref), custom_call_target="tpu_custom_call" | custom-call | flops 10737418240 | tf_op jit(solution)/shard_map/first_forward/pallas_call | solution.py:356
  9.0 0.5 collective-permute-start
  9.6 1.2 %collective-permute-done = bf16[32,32,128]{2,1,0:T(8,128)(2,1)S(1)} collective-permute-done((bf16[32,32,128]{2,1,0:T(8,128)(2,1)S(1)}, bf16[32,32,128]{2,1,0:T(8,128)(2,1)S(1)}, u32[]{:S(2)}, u32[]{:S(2)}) %collective-permute-start) | collective-permute-done | bytes 262176 | tf_op jit(solution)/shard_map/ppermute | solution.py:325
  10.7 0.1 fusion
  10.8 2.9 %collective-permute-start.1 = (bf16[32,32,128]{2,1,0:T(8,128)(2,1)S(1)}, bf16[32,32,128]{2,1,0:T(8,128)(2,1)S(1)}, u32[]{:S(2)}, u32[]{:S(2)}) collective-permute-start(bf16[32,32,128]{2,1,0:T(8,128)(2,1)S(1)} %fusion), channel_id=1, source_target_pairs={{0,2},{1,3},{2,0},{3,1},{4,6},{5,7},{6,4},{7,5},{8,10},{9,11},{10,... | collective-permute-start | bytes 786440 | tf_op jit(solution)/shard_map/ppermute | solution.py:325
  13.7 7.5 %load.1.held_ref = bf16[880,128,128]{2,1,0:T(8,128)(2,1)S(1)} custom-call(bf16[640,128,128]{2,1,0:T(8,128)(2,1)} %hbm_ref), custom_call_target="tpu_custom_call" | custom-call | bytes 41943040 | tf_op jit(solution)/shard_map/load/pallas_call | solution.py:393
  21.3 0.1 convert_add_fusion
  21.5 0.1 collective-permute-start.2
  21.6 1.5 %collective-permute-done.2.other_ref = bf16[32,32,128]{2,1,0:T(8,128)(2,1)S(1)} collective-permute-done((bf16[32,32,128]{2,1,0:T(8,128)(2,1)S(1)}, bf16[32,32,128]{2,1,0:T(8,128)(2,1)S(1)}, u32[]{:S(2)}, u32[]{:S(2)}) %collective-permute-start.2) | collective-permute-done | bytes 262176 | tf_op jit(solution)/shard_map/ppermute | solution.py:325
  23.1 5.3 %adjoint.2 = (f32[8,32,128]{2,1,0:T(8,128)S(1)}, bf16[8,32,128]{2,1,0:T(8,128)(2,1)S(1)}, bf16[8,32,128]{2,1,0:T(8,128)(2,1)S(1)}, bf16[8,32,128]{2,1,0:T(8,128)(2,1)S(1)}) custom-call(s32[640]{0:T(1024)S(1)} %copy-done.1, s32[640]{0:T(1024)S(1)} %copy-done.2, s32[32,1,128]{2,1,0:T(1,128)S(1)} %bitcast.7, bf16[880,128,128]{2,1,0:T(8,128)(2,1)S(1)} %load.1.held_ref, ...), custom_call_target="tpu_custom_call" | custom-call | flops 5368709120 | tf_op jit(solution)/shard_map/adjoint/pallas_call | solution.py:434
  28.4 1.6 %collective-permute-start.3 = (bf16[8,32,128]{2,1,0:T(8,128)(2,1)S(1)}, bf16[8,32,128]{2,1,0:T(8,128)(2,1)S(1)}, u32[]{:S(2)}, u32[]{:S(2)}) collective-permute-start(bf16[8,32,128]{2,1,0:T(8,128)(2,1)S(1)} %get-tuple-element.32), channel_id=1, source_target_pairs={{0,4},{4,0},{8,12},{12,8},{1,5},{5,1},{9,13},{13,9},{2,6},{6,2},{1... | collective-permute-start | bytes 196616 | tf_op jit(solution)/shard_map/ppermute | solution.py:325
  30.0 2.6 %collective-permute-start.4 = (bf16[8,32,128]{2,1,0:T(8,128)(2,1)S(1)}, bf16[8,32,128]{2,1,0:T(8,128)(2,1)S(1)}, u32[]{:S(2)}, u32[]{:S(2)}) collective-permute-start(bf16[8,32,128]{2,1,0:T(8,128)(2,1)S(1)} %get-tuple-element.33), channel_id=1, source_target_pairs={{0,8},{4,12},{8,0},{12,4},{1,9},{5,13},{9,1},{13,5},{2,10},{6,14},... | collective-permute-start | bytes 196616 | tf_op jit(solution)/shard_map/ppermute | solution.py:325
  32.6 0.2 collective-permute-start.5
  32.8 4.7 %collective-permute-done.4 = bf16[8,32,128]{2,1,0:T(8,128)(2,1)S(1)} collective-permute-done((bf16[8,32,128]{2,1,0:T(8,128)(2,1)S(1)}, bf16[8,32,128]{2,1,0:T(8,128)(2,1)S(1)}, u32[]{:S(2)}, u32[]{:S(2)}) %collective-permute-start.4) | collective-permute-done | bytes 65568 | tf_op jit(solution)/shard_map/ppermute | solution.py:325
  37.5 1.2 %collective-permute-done.5 = bf16[8,32,128]{2,1,0:T(8,128)(2,1)S(1)} collective-permute-done((bf16[8,32,128]{2,1,0:T(8,128)(2,1)S(1)}, bf16[8,32,128]{2,1,0:T(8,128)(2,1)S(1)}, u32[]{:S(2)}, u32[]{:S(2)}) %collective-permute-start.5) | collective-permute-done | bytes 65568 | tf_op jit(solution)/shard_map/ppermute | solution.py:325
  38.8 2.0 %collective-permute-start.8 = (bf16[8,32,128]{2,1,0:T(8,128)(2,1)S(1)}, bf16[8,32,128]{2,1,0:T(8,128)(2,1)S(1)}, u32[]{:S(2)}, u32[]{:S(2)}) collective-permute-start(bf16[8,32,128]{2,1,0:T(8,128)(2,1)S(1)} %add_convert_fusion.2.refs_0_), channel_id=1, source_target_pairs={{0,12},{4,8},{8,4},{12,0},{1,13},{5,9},{9,5},{13,1},{2,14},{6,10},... | collective-permute-start | bytes 196616 | tf_op jit(solution)/shard_map/ppermute | solution.py:325
  40.8 0.3 collective-permute-start.7
  41.1 2.1 %collective-permute-start.6 = (bf16[8,32,128]{2,1,0:T(8,128)(2,1)S(1)}, bf16[8,32,128]{2,1,0:T(8,128)(2,1)S(1)}, u32[]{:S(2)}, u32[]{:S(2)}) collective-permute-start(bf16[8,32,128]{2,1,0:T(8,128)(2,1)S(1)} %add_convert_fusion.2.refs_0_), channel_id=1, source_target_pairs={{0,4},{4,0},{8,12},{12,8},{1,5},{5,1},{9,13},{13,9},{2,6},{6,2},{1... | collective-permute-start | bytes 196616 | tf_op jit(solution)/shard_map/ppermute | solution.py:325
  43.2 1.8 %collective-permute-done.8.refs_3_ = bf16[8,32,128]{2,1,0:T(8,128)(2,1)S(1)} collective-permute-done((bf16[8,32,128]{2,1,0:T(8,128)(2,1)S(1)}, bf16[8,32,128]{2,1,0:T(8,128)(2,1)S(1)}, u32[]{:S(2)}, u32[]{:S(2)}) %collective-permute-start.8) | collective-permute-done | bytes 65568 | tf_op jit(solution)/shard_map/ppermute | solution.py:325
  45.0 1.5 %collective-permute-done.7.refs_2_ = bf16[8,32,128]{2,1,0:T(8,128)(2,1)S(1)} collective-permute-done((bf16[8,32,128]{2,1,0:T(8,128)(2,1)S(1)}, bf16[8,32,128]{2,1,0:T(8,128)(2,1)S(1)}, u32[]{:S(2)}, u32[]{:S(2)}) %collective-permute-start.7) | collective-permute-done | bytes 65568 | tf_op jit(solution)/shard_map/ppermute | solution.py:325
  46.6 0.2 gram.2
  46.8 5.9 %forward.1 = (f32[32,32,128]{2,1,0:T(8,128)S(1)}, bf16[32,32,128]{2,1,0:T(8,128)(2,1)S(1)}) custom-call(s32[640]{0:T(1024)S(1)} %copy-done.1, s32[640]{0:T(1024)S(1)} %copy-done.2, bf16[880,128,128]{2,1,0:T(8,128)(2,1)S(1)} %load.1.held_ref, bf16[32,32,128]{2,1,0:T(8,128)(2,1)S(1)} %get-tuple-element.36.panel_ref), custom_call_target="tpu_custom_call" | custom-call | flops 10737418240 | tf_op jit(solution)/shard_map/forward/pallas_call | solution.py:380
  52.7 0.1 collective-permute-start.12
  52.8 0.9 collective-permute-start.11
  53.7 1.2 %collective-permute-start.10 = (f32[32,32]{1,0:T(8,128)S(1)}, f32[32,32]{1,0:T(8,128)S(1)}, u32[]{:S(2)}, u32[]{:S(2)}) collective-permute-start(f32[32,32]{1,0:T(8,128)S(1)} %get-tuple-element.35.refs_0_), channel_id=1, source_target_pairs={{0,2},{1,3},{2,0},{3,1},{4,6},{5,7},{6,4},{7,5},{8,10},{9,11},{10,... | collective-permute-start | bytes 12296 | tf_op jit(solution)/shard_map/ppermute | solution.py:325
  55.0 0.8 collective-permute-start.13
  55.8 0.2 collective-permute-done.11.refs_3_
  56.0 1.4 %collective-permute-done.10.refs_2_ = f32[32,32]{1,0:T(8,128)S(1)} collective-permute-done((f32[32,32]{1,0:T(8,128)S(1)}, f32[32,32]{1,0:T(8,128)S(1)}, u32[]{:S(2)}, u32[]{:S(2)}) %collective-permute-start.10) | collective-permute-done | bytes 4128 | tf_op jit(solution)/shard_map/ppermute | solution.py:325
  57.4 2.6 %orth.1.matrix_ref = f32[32,32]{1,0:T(8,128)S(1)} custom-call(f32[32,32]{1,0:T(8,128)S(1)} %get-tuple-element.35.refs_0_, f32[32,32]{1,0:T(8,128)S(1)} %collective-permute-done.9.refs_1_, f32[32,32]{1,0:T(8,128)S(1)} %collective-permute-done.10.refs_2_, f32[32,32]{1,0:T(8,128)S(1)} %collective-permute-done.11.refs_3_), custom_call_target="tpu_custom_call" | custom-call | flops 4294967296 | tf_op jit(solution)/shard_map/orth/pallas_call | solution.py:414
  60.0 3.7 %collective-permute-done.13.refs_0_ = bf16[32,32,128]{2,1,0:T(8,128)(2,1)S(1)} collective-permute-done((bf16[32,32,128]{2,1,0:T(8,128)(2,1)S(1)}, bf16[32,32,128]{2,1,0:T(8,128)(2,1)S(1)}, u32[]{:S(2)}, u32[]{:S(2)}) %collective-permute-start.13) | collective-permute-done | bytes 262176 | tf_op jit(solution)/shard_map/ppermute | solution.py:325
  63.8 0.6 mix.1.mine_ref
  64.4 1.5 %collective-permute-done.14.other_ref = bf16[32,32,128]{2,1,0:T(8,128)(2,1)S(1)} collective-permute-done((bf16[32,32,128]{2,1,0:T(8,128)(2,1)S(1)}, bf16[32,32,128]{2,1,0:T(8,128)(2,1)S(1)}, u32[]{:S(2)}, u32[]{:S(2)}) %collective-permute-start.14) | collective-permute-done | bytes 262176 | tf_op jit(solution)/shard_map/ppermute | solution.py:325
  65.9 5.3 %adjoint.3 = (f32[8,32,128]{2,1,0:T(8,128)S(1)}, bf16[8,32,128]{2,1,0:T(8,128)(2,1)S(1)}, bf16[8,32,128]{2,1,0:T(8,128)(2,1)S(1)}, bf16[8,32,128]{2,1,0:T(8,128)(2,1)S(1)}) custom-call(s32[640]{0:T(1024)S(1)} %copy-done.1, s32[640]{0:T(1024)S(1)} %copy-done.2, s32[32,1,128]{2,1,0:T(1,128)S(1)} %bitcast.9, bf16[880,128,128]{2,1,0:T(8,128)(2,1)S(1)} %load.1.held_ref, ...), custom_call_target="tpu_custom_call" | custom-call | flops 5368709120 | tf_op jit(solution)/shard_map/adjoint/pallas_call | solution.py:434
  71.2 1.0 %collective-permute-start.15 = (bf16[8,32,128]{2,1,0:T(8,128)(2,1)S(1)}, bf16[8,32,128]{2,1,0:T(8,128)(2,1)S(1)}, u32[]{:S(2)}, u32[]{:S(2)}) collective-permute-start(bf16[8,32,128]{2,1,0:T(8,128)(2,1)S(1)} %get-tuple-element.40), channel_id=1, source_target_pairs={{0,4},{4,0},{8,12},{12,8},{1,5},{5,1},{9,13},{13,9},{2,6},{6,2},{1... | collective-permute-start | bytes 196616 | tf_op jit(solution)/shard_map/ppermute | solution.py:325
  72.2 1.6 %collective-permute-start.16 = (bf16[8,32,128]{2,1,0:T(8,128)(2,1)S(1)}, bf16[8,32,128]{2,1,0:T(8,128)(2,1)S(1)}, u32[]{:S(2)}, u32[]{:S(2)}) collective-permute-start(bf16[8,32,128]{2,1,0:T(8,128)(2,1)S(1)} %get-tuple-element.41), channel_id=1, source_target_pairs={{0,8},{4,12},{8,0},{12,4},{1,9},{5,13},{9,1},{13,5},{2,10},{6,14},... | collective-permute-start | bytes 196616 | tf_op jit(solution)/shard_map/ppermute | solution.py:325
  73.8 1.9 %collective-permute-start.17 = (bf16[8,32,128]{2,1,0:T(8,128)(2,1)S(1)}, bf16[8,32,128]{2,1,0:T(8,128)(2,1)S(1)}, u32[]{:S(2)}, u32[]{:S(2)}) collective-permute-start(bf16[8,32,128]{2,1,0:T(8,128)(2,1)S(1)} %get-tuple-element.42), channel_id=1, source_target_pairs={{0,12},{4,8},{8,4},{12,0},{1,13},{5,9},{9,5},{13,1},{2,14},{6,10},... | collective-permute-start | bytes 196616 | tf_op jit(solution)/shard_map/ppermute | solution.py:325
  75.7 4.8 %collective-permute-done.16 = bf16[8,32,128]{2,1,0:T(8,128)(2,1)S(1)} collective-permute-done((bf16[8,32,128]{2,1,0:T(8,128)(2,1)S(1)}, bf16[8,32,128]{2,1,0:T(8,128)(2,1)S(1)}, u32[]{:S(2)}, u32[]{:S(2)}) %collective-permute-start.16) | collective-permute-done | bytes 65568 | tf_op jit(solution)/shard_map/ppermute | solution.py:325
  80.5 2.1 %collective-permute-start.20 = (bf16[8,32,128]{2,1,0:T(8,128)(2,1)S(1)}, bf16[8,32,128]{2,1,0:T(8,128)(2,1)S(1)}, u32[]{:S(2)}, u32[]{:S(2)}) collective-permute-start(bf16[8,32,128]{2,1,0:T(8,128)(2,1)S(1)} %add_convert_fusion.1.refs_0_), channel_id=1, source_target_pairs={{0,12},{4,8},{8,4},{12,0},{1,13},{5,9},{9,5},{13,1},{2,14},{6,10},... | collective-permute-start | bytes 196616 | tf_op jit(solution)/shard_map/ppermute | solution.py:325
  82.6 0.7 collective-permute-start.19
  83.3 1.7 %collective-permute-start.18 = (bf16[8,32,128]{2,1,0:T(8,128)(2,1)S(1)}, bf16[8,32,128]{2,1,0:T(8,128)(2,1)S(1)}, u32[]{:S(2)}, u32[]{:S(2)}) collective-permute-start(bf16[8,32,128]{2,1,0:T(8,128)(2,1)S(1)} %add_convert_fusion.1.refs_0_), channel_id=1, source_target_pairs={{0,4},{4,0},{8,12},{12,8},{1,5},{5,1},{9,13},{13,9},{2,6},{6,2},{1... | collective-permute-start | bytes 196616 | tf_op jit(solution)/shard_map/ppermute | solution.py:325
  85.0 1.9 %collective-permute-done.20.refs_3_ = bf16[8,32,128]{2,1,0:T(8,128)(2,1)S(1)} collective-permute-done((bf16[8,32,128]{2,1,0:T(8,128)(2,1)S(1)}, bf16[8,32,128]{2,1,0:T(8,128)(2,1)S(1)}, u32[]{:S(2)}, u32[]{:S(2)}) %collective-permute-start.20) | collective-permute-done | bytes 65568 | tf_op jit(solution)/shard_map/ppermute | solution.py:325
  86.9 1.6 %collective-permute-done.19.refs_2_ = bf16[8,32,128]{2,1,0:T(8,128)(2,1)S(1)} collective-permute-done((bf16[8,32,128]{2,1,0:T(8,128)(2,1)S(1)}, bf16[8,32,128]{2,1,0:T(8,128)(2,1)S(1)}, u32[]{:S(2)}, u32[]{:S(2)}) %collective-permute-start.19) | collective-permute-done | bytes 65568 | tf_op jit(solution)/shard_map/ppermute | solution.py:325
  88.5 0.2 gram.3
  88.7 0.9 collective-permute-start.22
  89.6 1.0 %collective-permute-start.21 = (f32[32,32]{1,0:T(8,128)S(1)}, f32[32,32]{1,0:T(8,128)S(1)}, u32[]{:S(2)}, u32[]{:S(2)}) collective-permute-start(f32[32,32]{1,0:T(8,128)S(1)} %get-tuple-element.44.refs_0_), channel_id=1, source_target_pairs={{0,1},{1,0},{2,3},{3,2},{4,5},{5,4},{6,7},{7,6},{8,9},{9,8},{10,11... | collective-permute-start | bytes 12296 | tf_op jit(solution)/shard_map/ppermute | solution.py:325
  90.6 1.3 %collective-permute-done.23.refs_3_ = f32[32,32]{1,0:T(8,128)S(1)} collective-permute-done((f32[32,32]{1,0:T(8,128)S(1)}, f32[32,32]{1,0:T(8,128)S(1)}, u32[]{:S(2)}, u32[]{:S(2)}) %collective-permute-start.23) | collective-permute-done | bytes 4128 | tf_op jit(solution)/shard_map/ppermute | solution.py:325
  91.9 0.7 collective-permute-done.22.refs_2_
  92.6 3.8 %basis.1 = f32[32,4096]{1,0:T(8,128)} custom-call(bf16[32,32,128]{2,1,0:T(8,128)(2,1)S(1)} %get-tuple-element.43.w_ref, f32[32,32]{1,0:T(8,128)S(1)} %get-tuple-element.44.refs_0_, f32[32,32]{1,0:T(8,128)S(1)} %collective-permute-done.21.refs_1_, f32[32,32]{1,0:T(8,128)S(1)} %collective-permute-done.22.refs_2_, f32[32,32]{1,0:T(8,128)S(1)} %collective-permute-done.23.refs_3_), custom_call_target="tpu_custom_call" | custom-call | flops 4294967296 | tf_op jit(solution)/shard_map/basis/pallas_call | solution.py:462
  (25 shorter events, 0.3 us)
Async XLA Ops:
  0.0 13.7 %copy-start.3 = (s32[8192]{0:T(1024)S(1)}, s32[8192]{0:T(1024)}, u32[]{:S(2)}) copy-start(s32[8192]{0:T(1024)} %param.9) | copy-start | bytes 98308
  9.0 14.1 %copy-start = (s32[4096]{0:T(1024)S(1)}, s32[4096]{0:T(1024)}, u32[]{:S(2)}) copy-start(s32[4096]{0:T(1024)} %param.10) | copy-start | bytes 49156
  9.0 14.1 %copy-start.1 = (s32[640]{0:T(1024)S(1)}, s32[640]{0:T(1024)}, u32[]{:S(2)}) copy-start(s32[640]{0:T(1024)} %rows_ref.5) | copy-start | bytes 7684
  9.0 14.1 %copy-start.2 = (s32[640]{0:T(1024)S(1)}, s32[640]{0:T(1024)}, u32[]{:S(2)}) copy-start(s32[640]{0:T(1024)} %cols_ref.5) | copy-start | bytes 7684
  9.0 1.7 %collective-permute-start = (bf16[32,32,128]{2,1,0:T(8,128)(2,1)S(1)}, bf16[32,32,128]{2,1,0:T(8,128)(2,1)S(1)}, u32[]{:S(2)}, u32[]{:S(2)}) collective-permute-start(bf16[32,32,128]{2,1,0:T(8,128)(2,1)S(1)} %get-tuple-element.26), channel_id=1, source_target_pairs={{0,1},{1,0},{2,3},{3,2},{4,5},{5,4},{6,7},{7,6},{8,9},{9,8},{10,11... | collective-permute-start | bytes 786440 | tf_op jit(solution)/shard_map/ppermute | solution.py:325
  10.8 10.5 %collective-permute-start.1 = (bf16[32,32,128]{2,1,0:T(8,128)(2,1)S(1)}, bf16[32,32,128]{2,1,0:T(8,128)(2,1)S(1)}, u32[]{:S(2)}, u32[]{:S(2)}) collective-permute-start(bf16[32,32,128]{2,1,0:T(8,128)(2,1)S(1)} %fusion), channel_id=1, source_target_pairs={{0,2},{1,3},{2,0},{3,1},{4,6},{5,7},{6,4},{7,5},{8,10},{9,11},{10,... | collective-permute-start | bytes 786440 | tf_op jit(solution)/shard_map/ppermute | solution.py:325
  21.5 1.6 %collective-permute-start.2 = (bf16[32,32,128]{2,1,0:T(8,128)(2,1)S(1)}, bf16[32,32,128]{2,1,0:T(8,128)(2,1)S(1)}, u32[]{:S(2)}, u32[]{:S(2)}) collective-permute-start(bf16[32,32,128]{2,1,0:T(8,128)(2,1)S(1)} %divide_convert_fusion.mine_ref), channel_id=1, source_target_pairs={{0,1},{1,0},{2,3},{3,2},{4,5},{5,4},{6,7},{7,6},{8,9},{9,8},{10,11... | collective-permute-start | bytes 786440 | tf_op jit(solution)/shard_map/ppermute | solution.py:325
  28.4 4.5 %collective-permute-start.3 = (bf16[8,32,128]{2,1,0:T(8,128)(2,1)S(1)}, bf16[8,32,128]{2,1,0:T(8,128)(2,1)S(1)}, u32[]{:S(2)}, u32[]{:S(2)}) collective-permute-start(bf16[8,32,128]{2,1,0:T(8,128)(2,1)S(1)} %get-tuple-element.32), channel_id=1, source_target_pairs={{0,4},{4,0},{8,12},{12,8},{1,5},{5,1},{9,13},{13,9},{2,6},{6,2},{1... | collective-permute-start | bytes 196616 | tf_op jit(solution)/shard_map/ppermute | solution.py:325
  30.0 7.5 %collective-permute-start.4 = (bf16[8,32,128]{2,1,0:T(8,128)(2,1)S(1)}, bf16[8,32,128]{2,1,0:T(8,128)(2,1)S(1)}, u32[]{:S(2)}, u32[]{:S(2)}) collective-permute-start(bf16[8,32,128]{2,1,0:T(8,128)(2,1)S(1)} %get-tuple-element.33), channel_id=1, source_target_pairs={{0,8},{4,12},{8,0},{12,4},{1,9},{5,13},{9,1},{13,5},{2,10},{6,14},... | collective-permute-start | bytes 196616 | tf_op jit(solution)/shard_map/ppermute | solution.py:325
  32.6 6.2 %collective-permute-start.5 = (bf16[8,32,128]{2,1,0:T(8,128)(2,1)S(1)}, bf16[8,32,128]{2,1,0:T(8,128)(2,1)S(1)}, u32[]{:S(2)}, u32[]{:S(2)}) collective-permute-start(bf16[8,32,128]{2,1,0:T(8,128)(2,1)S(1)} %get-tuple-element.34), channel_id=1, source_target_pairs={{0,12},{4,8},{8,4},{12,0},{1,13},{5,9},{9,5},{13,1},{2,14},{6,10},... | collective-permute-start | bytes 196616 | tf_op jit(solution)/shard_map/ppermute | solution.py:325
  38.8 6.3 %collective-permute-start.8 = (bf16[8,32,128]{2,1,0:T(8,128)(2,1)S(1)}, bf16[8,32,128]{2,1,0:T(8,128)(2,1)S(1)}, u32[]{:S(2)}, u32[]{:S(2)}) collective-permute-start(bf16[8,32,128]{2,1,0:T(8,128)(2,1)S(1)} %add_convert_fusion.2.refs_0_), channel_id=1, source_target_pairs={{0,12},{4,8},{8,4},{12,0},{1,13},{5,9},{9,5},{13,1},{2,14},{6,10},... | collective-permute-start | bytes 196616 | tf_op jit(solution)/shard_map/ppermute | solution.py:325
  40.8 5.7 %collective-permute-start.7 = (bf16[8,32,128]{2,1,0:T(8,128)(2,1)S(1)}, bf16[8,32,128]{2,1,0:T(8,128)(2,1)S(1)}, u32[]{:S(2)}, u32[]{:S(2)}) collective-permute-start(bf16[8,32,128]{2,1,0:T(8,128)(2,1)S(1)} %add_convert_fusion.2.refs_0_), channel_id=1, source_target_pairs={{0,8},{4,12},{8,0},{12,4},{1,9},{5,13},{9,1},{13,5},{2,10},{6,14},... | collective-permute-start | bytes 196616 | tf_op jit(solution)/shard_map/ppermute | solution.py:325
  41.1 5.4 %collective-permute-start.6 = (bf16[8,32,128]{2,1,0:T(8,128)(2,1)S(1)}, bf16[8,32,128]{2,1,0:T(8,128)(2,1)S(1)}, u32[]{:S(2)}, u32[]{:S(2)}) collective-permute-start(bf16[8,32,128]{2,1,0:T(8,128)(2,1)S(1)} %add_convert_fusion.2.refs_0_), channel_id=1, source_target_pairs={{0,4},{4,0},{8,12},{12,8},{1,5},{5,1},{9,13},{13,9},{2,6},{6,2},{1... | collective-permute-start | bytes 196616 | tf_op jit(solution)/shard_map/ppermute | solution.py:325
  52.7 2.2 %collective-permute-start.12 = (bf16[32,32,128]{2,1,0:T(8,128)(2,1)S(1)}, bf16[32,32,128]{2,1,0:T(8,128)(2,1)S(1)}, u32[]{:S(2)}, u32[]{:S(2)}) collective-permute-start(bf16[32,32,128]{2,1,0:T(8,128)(2,1)S(1)} %get-tuple-element.38), channel_id=1, source_target_pairs={{0,1},{1,0},{2,3},{3,2},{4,5},{5,4},{6,7},{7,6},{8,9},{9,8},{10,11... | collective-permute-start | bytes 786440 | tf_op jit(solution)/shard_map/ppermute | solution.py:325
  52.8 3.2 %collective-permute-start.11 = (f32[32,32]{1,0:T(8,128)S(1)}, f32[32,32]{1,0:T(8,128)S(1)}, u32[]{:S(2)}, u32[]{:S(2)}) collective-permute-start(f32[32,32]{1,0:T(8,128)S(1)} %get-tuple-element.35.refs_0_), channel_id=1, source_target_pairs={{0,3},{1,2},{2,1},{3,0},{4,7},{5,6},{6,5},{7,4},{8,11},{9,10},{10,... | collective-permute-start | bytes 12296 | tf_op jit(solution)/shard_map/ppermute | solution.py:325
  53.7 3.7 %collective-permute-start.10 = (f32[32,32]{1,0:T(8,128)S(1)}, f32[32,32]{1,0:T(8,128)S(1)}, u32[]{:S(2)}, u32[]{:S(2)}) collective-permute-start(f32[32,32]{1,0:T(8,128)S(1)} %get-tuple-element.35.refs_0_), channel_id=1, source_target_pairs={{0,2},{1,3},{2,0},{3,1},{4,6},{5,7},{6,4},{7,5},{8,10},{9,11},{10,... | collective-permute-start | bytes 12296 | tf_op jit(solution)/shard_map/ppermute | solution.py:325
  54.9 2.5 %collective-permute-start.9 = (f32[32,32]{1,0:T(8,128)S(1)}, f32[32,32]{1,0:T(8,128)S(1)}, u32[]{:S(2)}, u32[]{:S(2)}) collective-permute-start(f32[32,32]{1,0:T(8,128)S(1)} %get-tuple-element.35.refs_0_), channel_id=1, source_target_pairs={{0,1},{1,0},{2,3},{3,2},{4,5},{5,4},{6,7},{7,6},{8,9},{9,8},{10,11... | collective-permute-start | bytes 12296 | tf_op jit(solution)/shard_map/ppermute | solution.py:325
  55.0 8.8 %collective-permute-start.13 = (bf16[32,32,128]{2,1,0:T(8,128)(2,1)S(1)}, bf16[32,32,128]{2,1,0:T(8,128)(2,1)S(1)}, u32[]{:S(2)}, u32[]{:S(2)}) collective-permute-start(bf16[32,32,128]{2,1,0:T(8,128)(2,1)S(1)} %add_convert_fusion), channel_id=1, source_target_pairs={{0,2},{1,3},{2,0},{3,1},{4,6},{5,7},{6,4},{7,5},{8,10},{9,11},{10,... | collective-permute-start | bytes 786440 | tf_op jit(solution)/shard_map/ppermute | solution.py:325
  64.3 1.6 %collective-permute-start.14 = (bf16[32,32,128]{2,1,0:T(8,128)(2,1)S(1)}, bf16[32,32,128]{2,1,0:T(8,128)(2,1)S(1)}, u32[]{:S(2)}, u32[]{:S(2)}) collective-permute-start(bf16[32,32,128]{2,1,0:T(8,128)(2,1)S(1)} %mix.1.mine_ref), channel_id=1, source_target_pairs={{0,1},{1,0},{2,3},{3,2},{4,5},{5,4},{6,7},{7,6},{8,9},{9,8},{10,11... | collective-permute-start | bytes 786440 | tf_op jit(solution)/shard_map/ppermute | solution.py:325
  71.2 4.5 %collective-permute-start.15 = (bf16[8,32,128]{2,1,0:T(8,128)(2,1)S(1)}, bf16[8,32,128]{2,1,0:T(8,128)(2,1)S(1)}, u32[]{:S(2)}, u32[]{:S(2)}) collective-permute-start(bf16[8,32,128]{2,1,0:T(8,128)(2,1)S(1)} %get-tuple-element.40), channel_id=1, source_target_pairs={{0,4},{4,0},{8,12},{12,8},{1,5},{5,1},{9,13},{13,9},{2,6},{6,2},{1... | collective-permute-start | bytes 196616 | tf_op jit(solution)/shard_map/ppermute | solution.py:325
  72.2 8.3 %collective-permute-start.16 = (bf16[8,32,128]{2,1,0:T(8,128)(2,1)S(1)}, bf16[8,32,128]{2,1,0:T(8,128)(2,1)S(1)}, u32[]{:S(2)}, u32[]{:S(2)}) collective-permute-start(bf16[8,32,128]{2,1,0:T(8,128)(2,1)S(1)} %get-tuple-element.41), channel_id=1, source_target_pairs={{0,8},{4,12},{8,0},{12,4},{1,9},{5,13},{9,1},{13,5},{2,10},{6,14},... | collective-permute-start | bytes 196616 | tf_op jit(solution)/shard_map/ppermute | solution.py:325
  73.8 6.7 %collective-permute-start.17 = (bf16[8,32,128]{2,1,0:T(8,128)(2,1)S(1)}, bf16[8,32,128]{2,1,0:T(8,128)(2,1)S(1)}, u32[]{:S(2)}, u32[]{:S(2)}) collective-permute-start(bf16[8,32,128]{2,1,0:T(8,128)(2,1)S(1)} %get-tuple-element.42), channel_id=1, source_target_pairs={{0,12},{4,8},{8,4},{12,0},{1,13},{5,9},{9,5},{13,1},{2,14},{6,10},... | collective-permute-start | bytes 196616 | tf_op jit(solution)/shard_map/ppermute | solution.py:325
  80.5 6.4 %collective-permute-start.20 = (bf16[8,32,128]{2,1,0:T(8,128)(2,1)S(1)}, bf16[8,32,128]{2,1,0:T(8,128)(2,1)S(1)}, u32[]{:S(2)}, u32[]{:S(2)}) collective-permute-start(bf16[8,32,128]{2,1,0:T(8,128)(2,1)S(1)} %add_convert_fusion.1.refs_0_), channel_id=1, source_target_pairs={{0,12},{4,8},{8,4},{12,0},{1,13},{5,9},{9,5},{13,1},{2,14},{6,10},... | collective-permute-start | bytes 196616 | tf_op jit(solution)/shard_map/ppermute | solution.py:325
  82.6 5.9 %collective-permute-start.19 = (bf16[8,32,128]{2,1,0:T(8,128)(2,1)S(1)}, bf16[8,32,128]{2,1,0:T(8,128)(2,1)S(1)}, u32[]{:S(2)}, u32[]{:S(2)}) collective-permute-start(bf16[8,32,128]{2,1,0:T(8,128)(2,1)S(1)} %add_convert_fusion.1.refs_0_), channel_id=1, source_target_pairs={{0,8},{4,12},{8,0},{12,4},{1,9},{5,13},{9,1},{13,5},{2,10},{6,14},... | collective-permute-start | bytes 196616 | tf_op jit(solution)/shard_map/ppermute | solution.py:325
  83.3 5.2 %collective-permute-start.18 = (bf16[8,32,128]{2,1,0:T(8,128)(2,1)S(1)}, bf16[8,32,128]{2,1,0:T(8,128)(2,1)S(1)}, u32[]{:S(2)}, u32[]{:S(2)}) collective-permute-start(bf16[8,32,128]{2,1,0:T(8,128)(2,1)S(1)} %add_convert_fusion.1.refs_0_), channel_id=1, source_target_pairs={{0,4},{4,0},{8,12},{12,8},{1,5},{5,1},{9,13},{13,9},{2,6},{6,2},{1... | collective-permute-start | bytes 196616 | tf_op jit(solution)/shard_map/ppermute | solution.py:325
  88.7 3.2 %collective-permute-start.23 = (f32[32,32]{1,0:T(8,128)S(1)}, f32[32,32]{1,0:T(8,128)S(1)}, u32[]{:S(2)}, u32[]{:S(2)}) collective-permute-start(f32[32,32]{1,0:T(8,128)S(1)} %get-tuple-element.44.refs_0_), channel_id=1, source_target_pairs={{0,3},{1,2},{2,1},{3,0},{4,7},{5,6},{6,5},{7,4},{8,11},{9,10},{10,... | collective-permute-start | bytes 12296 | tf_op jit(solution)/shard_map/ppermute | solution.py:325
  88.7 3.9 %collective-permute-start.22 = (f32[32,32]{1,0:T(8,128)S(1)}, f32[32,32]{1,0:T(8,128)S(1)}, u32[]{:S(2)}, u32[]{:S(2)}) collective-permute-start(f32[32,32]{1,0:T(8,128)S(1)} %get-tuple-element.44.refs_0_), channel_id=1, source_target_pairs={{0,2},{1,3},{2,0},{3,1},{4,6},{5,7},{6,4},{7,5},{8,10},{9,11},{10,... | collective-permute-start | bytes 12296 | tf_op jit(solution)/shard_map/ppermute | solution.py:325
  89.6 3.0 %collective-permute-start.21 = (f32[32,32]{1,0:T(8,128)S(1)}, f32[32,32]{1,0:T(8,128)S(1)}, u32[]{:S(2)}, u32[]{:S(2)}) collective-permute-start(f32[32,32]{1,0:T(8,128)S(1)} %get-tuple-element.44.refs_0_), channel_id=1, source_target_pairs={{0,1},{1,0},{2,3},{3,2},{4,5},{5,4},{6,7},{7,6},{8,9},{9,8},{10,11... | collective-permute-start | bytes 12296 | tf_op jit(solution)/shard_map/ppermute | solution.py:325

commit v3 on v2

--- a/solution.py
+++ b/solution.py
@@ -9,6 +9,9 @@
 
 ITERS = 2
 TURNED = 3
+FIRST = 128
+SLOTS = 3
+MIX = 8
 F32 = jnp.float32
 BF16 = jnp.bfloat16
 VMEM = pl.BlockSpec(memory_space=pltpu.VMEM)
@@ -49,7 +52,7 @@
         acc[place] += piece
 
 
-def forward_group(panel_ref, cols_ref, col_base, block_at, first, size):
+def forward_group(panel_ref, cols_ref, col_base, block_at, plain, first, size):
     pieces = []
     side, box = panel_ref.shape[1:]
     for t in range(0, size, 2):
@@ -60,7 +63,11 @@
             ],
             0,
         )
-        out = dot_nn(left, jnp.concatenate([block_at(t), block_at(t + 1)], 1))
+        one, two = block_at(t), block_at(t + 1)
+        if plain(t):
+            out = dot_nt(left, jnp.concatenate([one, two], 0))
+        else:
+            out = dot_nn(left, jnp.concatenate([one, two], 1))
         pieces += [out[:side, :box], out[side:, box:]]
     return pieces
 
@@ -193,8 +200,16 @@
     def step(i, carry):
         slot = lax.rem(i, slots)
         part(i, slot).wait()
+
+        def plain(t):
+            return t % MIX == MIX - 2
+
+        def block_at(t):
+            block = blocks_ref[slot, t]
+            return block if plain(t // 2 * 2) else block.T
+
         pieces = forward_group(
-            panel_ref, cols_ref, col_base, lambda t: blocks_ref[slot, t].T, i * unroll, unroll
+            panel_ref, cols_ref, col_base, block_at, plain, i * unroll, unroll
         )
         add_group(pieces, rows_ref, i * unroll, row_base, (acc_a, acc_b))
 
@@ -208,24 +223,19 @@
     split_halves((acc_a, acc_b), lax.axis_index("dst") % 2, keep_ref, send_ref)
 
 
-def load_kernel(unroll, turned, hbm_ref, held_ref, sems):
-    total = hbm_ref.shape[0]
-    steps = total // unroll
-
-    def part(i):
-        span = pl.ds(i * unroll, unroll)
-        return pltpu.make_async_copy(hbm_ref.at[span], held_ref.at[span], sems.at[i])
-
-    for i in range(steps):
-        part(i).start()
-
-    for i in range(steps):
-        part(i).wait()
+def load_kernel(hbm_ref, held_ref, sem):
+    copy = pltpu.make_async_copy(hbm_ref, held_ref, sem)
+    copy.start()
+    copy.wait()
+
+
+def turn_kernel(unroll, turned, held_ref, turned_ref):
+    for i in range(turned_ref.shape[0] // turned):
         for t in range(turned):
-            held_ref[total + i * turned + t] = held_ref[i * unroll + t].T
-
-
-def forward_kernel(unroll, turned, rows_ref, cols_ref, held_ref, panel_ref, keep_ref, send_ref, acc_a, acc_b):
+            turned_ref[i * turned + t] = held_ref[i * unroll + t].T
+
+
+def forward_kernel(unroll, turned, rows_ref, cols_ref, held_ref, turned_ref, panel_ref, keep_ref, send_ref, acc_a, acc_b):
     total = rows_ref.shape[0]
     row_base = lax.axis_index("src") * acc_a.shape[0]
     col_base = lax.axis_index("dst") * panel_ref.shape[0]
@@ -237,10 +247,10 @@
 
         def block_at(t):
             if t < turned:
-                return held_ref[total + i * turned + t]
+                return turned_ref[i * turned + t]
             return held_ref[first + t].T
 
-        pieces = forward_group(panel_ref, cols_ref, col_base, block_at, first, unroll)
+        pieces = forward_group(panel_ref, cols_ref, col_base, block_at, lambda t: False, first, unroll)
         add_group(pieces, rows_ref, first, row_base, (acc_a, acc_b))
         return carry
 
@@ -333,6 +343,7 @@
     n_src, n_dst = lax.axis_size("src"), lax.axis_size("dst")
     box_total = float(col_blocks * box * n_dst)
     unroll = unroll_of(total, 128)
+    first_unroll = unroll_of(total, FIRST)
     turned = unroll * TURNED // 8
     half = row_blocks // 2
     size = col_blocks // n_src
@@ -352,9 +363,9 @@
     w_full, grams = None, None
     for sweep in range(ITERS):
         if sweep == 0:
-            slots = min(total // unroll, 3)
+            slots = min(total // first_unroll, SLOTS)
             keep, send = pl.pallas_call(
-                functools.partial(first_forward_kernel, unroll),
+                functools.partial(first_forward_kernel, first_unroll),
                 in_specs=[HBM] * 5,
                 out_specs=[VMEM, VMEM],
                 out_shape=[keep_out, send_out],
@@ -363,13 +374,13 @@
                     pltpu.SMEM(block_cols.shape, jnp.int32),
                     pltpu.VMEM(start_panel.shape, F32),
                     pltpu.VMEM(wide_counts.shape, jnp.int32),
-                    pltpu.VMEM((slots, unroll, box, box), BF16),
+                    pltpu.VMEM((slots, first_unroll, box, box), BF16),
                     pltpu.VMEM((col_blocks, side, box), BF16),
                     *accs,
                     pltpu.SemaphoreType.DMA((slots,)),
                     pltpu.SemaphoreType.DMA((4,)),
                 ],
-                compiler_params=params(18),
+                compiler_params=params(22),
                 name="first_forward",
                 cost_estimate=forward_cost,
             )(*[
@@ -379,23 +390,23 @@
         else:
             keep, send = pl.pallas_call(
                 functools.partial(forward_kernel, unroll, turned),
-                in_specs=[SMEM, SMEM, VMEM, VMEM],
+                in_specs=[SMEM, SMEM, VMEM, VMEM, VMEM],
                 out_specs=[VMEM, VMEM],
                 out_shape=[keep_out, send_out],
                 scratch_shapes=accs,
                 compiler_params=params(),
                 name="forward",
                 cost_estimate=forward_cost,
-            )(block_rows, block_cols, held, w_full)
+            )(block_rows, block_cols, held, flipped, w_full)
         core_got = swap(send, "dst", 1)
         if sweep == 0:
             again, core_got = lax.optimization_barrier((blocks, core_got))
             held = pl.pallas_call(
-                functools.partial(load_kernel, unroll, turned),
+                load_kernel,
                 in_specs=[HBM],
                 out_specs=VMEM,
-                out_shape=pltpu.VMEM((total + total // unroll * turned, box, box), BF16),
-                scratch_shapes=[pltpu.SemaphoreType.DMA((total // unroll,))],
+                out_shape=pltpu.VMEM(blocks.shape, BF16),
+                scratch_shapes=[pltpu.SemaphoreType.DMA],
                 compiler_params=params(2),
                 name="load",
                 cost_estimate=cost(0, 2 * total * box * box * 2),
@@ -446,7 +457,20 @@
             name="adjoint",
                 cost_estimate=adjoint_cost,
         )(block_rows, block_cols, tall_counts, held, mine, other)
+        outs = list(outs)
         got = [swap(outs[k], "src", k) for k in range(1, n_src)]
+        if sweep == 0:
+            outs[0], again = lax.optimization_barrier((outs[0], held))
+            flipped = pl.pallas_call(
+                functools.partial(turn_kernel, unroll, turned),
+                in_specs=[VMEM],
+                out_specs=VMEM,
+                out_shape=pltpu.VMEM((total // unroll * turned, box, box), BF16),
+                compiler_params=params(2),
+                name="turn",
+                cost_estimate=adjoint_cost,
+            )(again)
+            got, flipped = lax.optimization_barrier((got, flipped))
         own = tree_sum([outs[0]] + [g.astype(F32) for g in got]).astype(BF16)
         chunks = [own] + [swap(own, "src", k) for k in range(1, n_src)]
         w_full, gram = pl.pallas_call(

time: 96.6 us -> 95.5 us (0.989)
  waiting for transfers between devices: 29.1 us -> 26.4 us
  Pallas kernels: 40.4 us -> 41.6 us
    ppermute x24, waiting for transfers between devices: 29.1 us -> 26.4 us  [swap(): return lax.ppermute(x, axis, [(i, i ^ bits) for i in range(size)])]
    pallas_call x2 -> x3, Pallas kernels: 16.5 us -> 17.7 us  [the longest x1 8.64 us: per_device(): pl.pallas_call(functools.partial(first_forward_kernel, first_unroll), in_...]
  transfers between devices with their start and end apart: 24 -> 24, of which waited for: 15 -> 14; matrix products, arithmetic and copies ran while one was open for 0% -> 0% of each run, Pallas kernels for 11% -> 12%
where the time goes in v3:
time: 95.5 us; the launch traced here: 95.4 us
  Pallas kernels  41.6 us (44%)
  starting transfers between devices  26.9 us (28%)
  waiting for transfers between devices  26.4 us (28%)
    ppermute x24, starting transfers between devices, swap(): return lax.ppermute(x, axis, [(i, i ^ bits) for i in range(size)])  26.9 us
    ppermute x24, waiting for transfers between devices, swap(): return lax.ppermute(x, axis, [(i, i ^ bits) for i in range(size)])  26.4 us
    pallas_call x2, Pallas kernels, per_device(): pl.pallas_call(functools.partial(adjoint_kernel, unroll, n_src), in_specs...  10.5 us
    pallas_call x1, Pallas kernels, per_device(): pl.pallas_call(functools.partial(first_forward_kernel, first_unroll), in_...  8.64 us
    pallas_call x1, Pallas kernels, per_device(): pl.pallas_call(load_kernel, in_specs=[HBM], out_specs=VMEM, out_shape=plt...  6.99 us
    pallas_call x1, Pallas kernels, per_device(): pl.pallas_call(functools.partial(forward_kernel, unroll, turned), in_spec...  5.87 us
    pallas_call x1, Pallas kernels, per_device(): pl.pallas_call(functools.partial(basis_kernel, box_total), in_specs=[VMEM...  3.8 us
    pallas_call x1, Pallas kernels, per_device(): pl.pallas_call(functools.partial(orth_kernel, box_total), in_specs=[VMEM]...  2.64 us
  transfers between devices with their start and end apart: 24, of which 14 were waited for; matrix products, arithmetic and copies ran while one was open for 0% of the time, Pallas kernels for 12%

profile of v3, /device:TPU:0, one launch (start us, length us, event | category | flops | bytes accessed | tf_op | source)
XLA Modules:
  0.0 95.4 jit_solution(6657443985389750225)
XLA Ops:
  0.0 8.6 %first_forward.1 = (f32[32,32,128]{2,1,0:T(8,128)S(1)}, bf16[32,32,128]{2,1,0:T(8,128)(2,1)S(1)}) custom-call(s32[640]{0:T(1024)} %rows_ref.5, s32[640]{0:T(1024)} %cols_ref.5, f32[32,4096]{1,0:T(8,128)} %start_hbm.1, s32[1,4096]{1,0:T(1,128)} %bitcast.7, bf16[640,128,128]{2,1,0:T(8,128)(2,1)} %hbm_ref), custom_call_target="tpu_custom_call" | custom-call | flops 10737418240 | tf_op jit(solution)/shard_map/first_forward/pallas_call | solution.py:367
  8.7 0.5 collective-permute-start
  9.2 1.2 %collective-permute-done = bf16[32,32,128]{2,1,0:T(8,128)(2,1)S(1)} collective-permute-done((bf16[32,32,128]{2,1,0:T(8,128)(2,1)S(1)}, bf16[32,32,128]{2,1,0:T(8,128)(2,1)S(1)}, u32[]{:S(2)}, u32[]{:S(2)}) %collective-permute-start) | collective-permute-done | bytes 262176 | tf_op jit(solution)/shard_map/ppermute | solution.py:335
  10.4 2.9 %collective-permute-start.1 = (bf16[32,32,128]{2,1,0:T(8,128)(2,1)S(1)}, bf16[32,32,128]{2,1,0:T(8,128)(2,1)S(1)}, u32[]{:S(2)}, u32[]{:S(2)}) collective-permute-start(bf16[32,32,128]{2,1,0:T(8,128)(2,1)S(1)} %fusion), channel_id=1, source_target_pairs={{0,2},{1,3},{2,0},{3,1},{4,6},{5,7},{6,4},{7,5},{8,10},{9,11},{10,... | collective-permute-start | bytes 786440 | tf_op jit(solution)/shard_map/ppermute | solution.py:335
  13.4 7.0 %load.1.held_ref = bf16[640,128,128]{2,1,0:T(8,128)(2,1)S(1)} custom-call(bf16[640,128,128]{2,1,0:T(8,128)(2,1)} %hbm_ref), custom_call_target="tpu_custom_call" | custom-call | bytes 41943040 | tf_op jit(solution)/shard_map/load/pallas_call | solution.py:404
  20.4 0.1 convert_add_fusion
  20.5 0.1 collective-permute-start.2
  20.6 1.5 %collective-permute-done.2.other_ref = bf16[32,32,128]{2,1,0:T(8,128)(2,1)S(1)} collective-permute-done((bf16[32,32,128]{2,1,0:T(8,128)(2,1)S(1)}, bf16[32,32,128]{2,1,0:T(8,128)(2,1)S(1)}, u32[]{:S(2)}, u32[]{:S(2)}) %collective-permute-start.2) | collective-permute-done | bytes 262176 | tf_op jit(solution)/shard_map/ppermute | solution.py:335
  22.1 5.3 %adjoint.2 = (f32[8,32,128]{2,1,0:T(8,128)S(1)}, bf16[8,32,128]{2,1,0:T(8,128)(2,1)S(1)}, bf16[8,32,128]{2,1,0:T(8,128)(2,1)S(1)}, bf16[8,32,128]{2,1,0:T(8,128)(2,1)S(1)}) custom-call(s32[640]{0:T(1024)S(1)} %copy-done.1, s32[640]{0:T(1024)S(1)} %copy-done.2, s32[32,1,128]{2,1,0:T(1,128)S(1)} %bitcast.8, bf16[640,128,128]{2,1,0:T(8,128)(2,1)S(1)} %load.1.held_ref, ...), custom_call_target="tpu_custom_call" | custom-call | flops 5368709120 | tf_op jit(solution)/shard_map/adjoint/pallas_call | solution.py:445
  27.4 1.6 %collective-permute-start.3 = (bf16[8,32,128]{2,1,0:T(8,128)(2,1)S(1)}, bf16[8,32,128]{2,1,0:T(8,128)(2,1)S(1)}, u32[]{:S(2)}, u32[]{:S(2)}) collective-permute-start(bf16[8,32,128]{2,1,0:T(8,128)(2,1)S(1)} %get-tuple-element.39), channel_id=1, source_target_pairs={{0,4},{4,0},{8,12},{12,8},{1,5},{5,1},{9,13},{13,9},{2,6},{6,2},{1... | collective-permute-start | bytes 196616 | tf_op jit(solution)/shard_map/ppermute | solution.py:335
  29.0 2.6 %collective-permute-start.4 = (bf16[8,32,128]{2,1,0:T(8,128)(2,1)S(1)}, bf16[8,32,128]{2,1,0:T(8,128)(2,1)S(1)}, u32[]{:S(2)}, u32[]{:S(2)}) collective-permute-start(bf16[8,32,128]{2,1,0:T(8,128)(2,1)S(1)} %get-tuple-element.40), channel_id=1, source_target_pairs={{0,8},{4,12},{8,0},{12,4},{1,9},{5,13},{9,1},{13,5},{2,10},{6,14},... | collective-permute-start | bytes 196616 | tf_op jit(solution)/shard_map/ppermute | solution.py:335
  31.6 0.2 collective-permute-start.5
  31.9 2.1 %turn.1.turned_ref = bf16[240,128,128]{2,1,0:T(8,128)(2,1)S(1)} custom-call(bf16[640,128,128]{2,1,0:T(8,128)(2,1)S(1)} %load.1.held_ref), custom_call_target="tpu_custom_call" | custom-call | flops 5368709120 | tf_op jit(solution)/shard_map/turn/pallas_call | solution.py:464
  34.0 2.6 %collective-permute-done.4 = bf16[8,32,128]{2,1,0:T(8,128)(2,1)S(1)} collective-permute-done((bf16[8,32,128]{2,1,0:T(8,128)(2,1)S(1)}, bf16[8,32,128]{2,1,0:T(8,128)(2,1)S(1)}, u32[]{:S(2)}, u32[]{:S(2)}) %collective-permute-start.4) | collective-permute-done | bytes 65568 | tf_op jit(solution)/shard_map/ppermute | solution.py:335
  36.6 1.2 %collective-permute-done.5 = bf16[8,32,128]{2,1,0:T(8,128)(2,1)S(1)} collective-permute-done((bf16[8,32,128]{2,1,0:T(8,128)(2,1)S(1)}, bf16[8,32,128]{2,1,0:T(8,128)(2,1)S(1)}, u32[]{:S(2)}, u32[]{:S(2)}) %collective-permute-start.5) | collective-permute-done | bytes 65568 | tf_op jit(solution)/shard_map/ppermute | solution.py:335
  37.9 2.0 %collective-permute-start.8 = (bf16[8,32,128]{2,1,0:T(8,128)(2,1)S(1)}, bf16[8,32,128]{2,1,0:T(8,128)(2,1)S(1)}, u32[]{:S(2)}, u32[]{:S(2)}) collective-permute-start(bf16[8,32,128]{2,1,0:T(8,128)(2,1)S(1)} %add_convert_fusion.2.refs_0_), channel_id=1, source_target_pairs={{0,12},{4,8},{8,4},{12,0},{1,13},{5,9},{9,5},{13,1},{2,14},{6,10},... | collective-permute-start | bytes 196616 | tf_op jit(solution)/shard_map/ppermute | solution.py:335
  39.9 0.3 collective-permute-start.7
  40.2 2.1 %collective-permute-start.6 = (bf16[8,32,128]{2,1,0:T(8,128)(2,1)S(1)}, bf16[8,32,128]{2,1,0:T(8,128)(2,1)S(1)}, u32[]{:S(2)}, u32[]{:S(2)}) collective-permute-start(bf16[8,32,128]{2,1,0:T(8,128)(2,1)S(1)} %add_convert_fusion.2.refs_0_), channel_id=1, source_target_pairs={{0,4},{4,0},{8,12},{12,8},{1,5},{5,1},{9,13},{13,9},{2,6},{6,2},{1... | collective-permute-start | bytes 196616 | tf_op jit(solution)/shard_map/ppermute | solution.py:335
  42.3 1.8 %collective-permute-done.8.refs_3_ = bf16[8,32,128]{2,1,0:T(8,128)(2,1)S(1)} collective-permute-done((bf16[8,32,128]{2,1,0:T(8,128)(2,1)S(1)}, bf16[8,32,128]{2,1,0:T(8,128)(2,1)S(1)}, u32[]{:S(2)}, u32[]{:S(2)}) %collective-permute-start.8) | collective-permute-done | bytes 65568 | tf_op jit(solution)/shard_map/ppermute | solution.py:335
  44.1 1.5 %collective-permute-done.7.refs_2_ = bf16[8,32,128]{2,1,0:T(8,128)(2,1)S(1)} collective-permute-done((bf16[8,32,128]{2,1,0:T(8,128)(2,1)S(1)}, bf16[8,32,128]{2,1,0:T(8,128)(2,1)S(1)}, u32[]{:S(2)}, u32[]{:S(2)}) %collective-permute-start.7) | collective-permute-done | bytes 65568 | tf_op jit(solution)/shard_map/ppermute | solution.py:335
  45.6 0.2 gram.2
  45.9 5.9 %forward.1 = (f32[32,32,128]{2,1,0:T(8,128)S(1)}, bf16[32,32,128]{2,1,0:T(8,128)(2,1)S(1)}) custom-call(s32[640]{0:T(1024)S(1)} %copy-done.1, s32[640]{0:T(1024)S(1)} %copy-done.2, bf16[640,128,128]{2,1,0:T(8,128)(2,1)S(1)} %load.1.held_ref, bf16[240,128,128]{2,1,0:T(8,128)(2,1)S(1)} %turn.1.turned_ref, bf16[32,32,128]{2,1,0:T(8,128)(2,1)S(1)} %get-tuple-element.48.panel_ref), custom_call_target="tpu_custom_call" | custom-call | flops 10737418240 | tf_op jit(solution)/shard_map/forward/pallas_call | solution.py:391
  51.8 0.1 collective-permute-start.12
  51.8 1.4 %collective-permute-start.11 = (f32[32,32]{1,0:T(8,128)S(1)}, f32[32,32]{1,0:T(8,128)S(1)}, u32[]{:S(2)}, u32[]{:S(2)}) collective-permute-start(f32[32,32]{1,0:T(8,128)S(1)} %get-tuple-element.46.refs_0_), channel_id=1, source_target_pairs={{0,3},{1,2},{2,1},{3,0},{4,7},{5,6},{6,5},{7,4},{8,11},{9,10},{10,... | collective-permute-start | bytes 12296 | tf_op jit(solution)/shard_map/ppermute | solution.py:335
  53.3 0.7 collective-permute-start.10
  54.0 0.1 add_convert_fusion
  54.1 1.4 %collective-permute-start.13 = (bf16[32,32,128]{2,1,0:T(8,128)(2,1)S(1)}, bf16[32,32,128]{2,1,0:T(8,128)(2,1)S(1)}, u32[]{:S(2)}, u32[]{:S(2)}) collective-permute-start(bf16[32,32,128]{2,1,0:T(8,128)(2,1)S(1)} %add_convert_fusion), channel_id=1, source_target_pairs={{0,2},{1,3},{2,0},{3,1},{4,6},{5,7},{6,4},{7,5},{8,10},{9,11},{10,... | collective-permute-start | bytes 786440 | tf_op jit(solution)/shard_map/ppermute | solution.py:335
  55.4 1.6 %collective-permute-done.10.refs_2_ = f32[32,32]{1,0:T(8,128)S(1)} collective-permute-done((f32[32,32]{1,0:T(8,128)S(1)}, f32[32,32]{1,0:T(8,128)S(1)}, u32[]{:S(2)}, u32[]{:S(2)}) %collective-permute-start.10) | collective-permute-done | bytes 4128 | tf_op jit(solution)/shard_map/ppermute | solution.py:335
  57.0 2.6 %orth.1.matrix_ref = f32[32,32]{1,0:T(8,128)S(1)} custom-call(f32[32,32]{1,0:T(8,128)S(1)} %get-tuple-element.46.refs_0_, f32[32,32]{1,0:T(8,128)S(1)} %collective-permute-done.9.refs_1_, f32[32,32]{1,0:T(8,128)S(1)} %collective-permute-done.10.refs_2_, f32[32,32]{1,0:T(8,128)S(1)} %collective-permute-done.11.refs_3_), custom_call_target="tpu_custom_call" | custom-call | flops 4294967296 | tf_op jit(solution)/shard_map/orth/pallas_call | solution.py:425
  59.6 3.2 %collective-permute-done.13.refs_0_ = bf16[32,32,128]{2,1,0:T(8,128)(2,1)S(1)} collective-permute-done((bf16[32,32,128]{2,1,0:T(8,128)(2,1)S(1)}, bf16[32,32,128]{2,1,0:T(8,128)(2,1)S(1)}, u32[]{:S(2)}, u32[]{:S(2)}) %collective-permute-start.13) | collective-permute-done | bytes 262176 | tf_op jit(solution)/shard_map/ppermute | solution.py:335
  62.8 0.6 mix.1.mine_ref
  63.5 1.5 %collective-permute-done.14.other_ref = bf16[32,32,128]{2,1,0:T(8,128)(2,1)S(1)} collective-permute-done((bf16[32,32,128]{2,1,0:T(8,128)(2,1)S(1)}, bf16[32,32,128]{2,1,0:T(8,128)(2,1)S(1)}, u32[]{:S(2)}, u32[]{:S(2)}) %collective-permute-start.14) | collective-permute-done | bytes 262176 | tf_op jit(solution)/shard_map/ppermute | solution.py:335
  65.0 5.3 %adjoint.3 = (f32[8,32,128]{2,1,0:T(8,128)S(1)}, bf16[8,32,128]{2,1,0:T(8,128)(2,1)S(1)}, bf16[8,32,128]{2,1,0:T(8,128)(2,1)S(1)}, bf16[8,32,128]{2,1,0:T(8,128)(2,1)S(1)}) custom-call(s32[640]{0:T(1024)S(1)} %copy-done.1, s32[640]{0:T(1024)S(1)} %copy-done.2, s32[32,1,128]{2,1,0:T(1,128)S(1)} %bitcast.10, bf16[640,128,128]{2,1,0:T(8,128)(2,1)S(1)} %load.1.held_ref, ...), custom_call_target="tpu_custom_call" | custom-call | flops 5368709120 | tf_op jit(solution)/shard_map/adjoint/pallas_call | solution.py:445
  70.3 1.0 %collective-permute-start.15 = (bf16[8,32,128]{2,1,0:T(8,128)(2,1)S(1)}, bf16[8,32,128]{2,1,0:T(8,128)(2,1)S(1)}, u32[]{:S(2)}, u32[]{:S(2)}) collective-permute-start(bf16[8,32,128]{2,1,0:T(8,128)(2,1)S(1)} %get-tuple-element.52), channel_id=1, source_target_pairs={{0,4},{4,0},{8,12},{12,8},{1,5},{5,1},{9,13},{13,9},{2,6},{6,2},{1... | collective-permute-start | bytes 196616 | tf_op jit(solution)/shard_map/ppermute | solution.py:335
  71.3 1.6 %collective-permute-start.16 = (bf16[8,32,128]{2,1,0:T(8,128)(2,1)S(1)}, bf16[8,32,128]{2,1,0:T(8,128)(2,1)S(1)}, u32[]{:S(2)}, u32[]{:S(2)}) collective-permute-start(bf16[8,32,128]{2,1,0:T(8,128)(2,1)S(1)} %get-tuple-element.53), channel_id=1, source_target_pairs={{0,8},{4,12},{8,0},{12,4},{1,9},{5,13},{9,1},{13,5},{2,10},{6,14},... | collective-permute-start | bytes 196616 | tf_op jit(solution)/shard_map/ppermute | solution.py:335
  72.9 1.9 %collective-permute-start.17 = (bf16[8,32,128]{2,1,0:T(8,128)(2,1)S(1)}, bf16[8,32,128]{2,1,0:T(8,128)(2,1)S(1)}, u32[]{:S(2)}, u32[]{:S(2)}) collective-permute-start(bf16[8,32,128]{2,1,0:T(8,128)(2,1)S(1)} %get-tuple-element.54), channel_id=1, source_target_pairs={{0,12},{4,8},{8,4},{12,0},{1,13},{5,9},{9,5},{13,1},{2,14},{6,10},... | collective-permute-start | bytes 196616 | tf_op jit(solution)/shard_map/ppermute | solution.py:335
  74.7 4.8 %collective-permute-done.16 = bf16[8,32,128]{2,1,0:T(8,128)(2,1)S(1)} collective-permute-done((bf16[8,32,128]{2,1,0:T(8,128)(2,1)S(1)}, bf16[8,32,128]{2,1,0:T(8,128)(2,1)S(1)}, u32[]{:S(2)}, u32[]{:S(2)}) %collective-permute-start.16) | collective-permute-done | bytes 65568 | tf_op jit(solution)/shard_map/ppermute | solution.py:335
  79.6 2.1 %collective-permute-start.20 = (bf16[8,32,128]{2,1,0:T(8,128)(2,1)S(1)}, bf16[8,32,128]{2,1,0:T(8,128)(2,1)S(1)}, u32[]{:S(2)}, u32[]{:S(2)}) collective-permute-start(bf16[8,32,128]{2,1,0:T(8,128)(2,1)S(1)} %add_convert_fusion.1.refs_0_), channel_id=1, source_target_pairs={{0,12},{4,8},{8,4},{12,0},{1,13},{5,9},{9,5},{13,1},{2,14},{6,10},... | collective-permute-start | bytes 196616 | tf_op jit(solution)/shard_map/ppermute | solution.py:335
  81.7 0.7 collective-permute-start.19
  82.4 1.7 %collective-permute-start.18 = (bf16[8,32,128]{2,1,0:T(8,128)(2,1)S(1)}, bf16[8,32,128]{2,1,0:T(8,128)(2,1)S(1)}, u32[]{:S(2)}, u32[]{:S(2)}) collective-permute-start(bf16[8,32,128]{2,1,0:T(8,128)(2,1)S(1)} %add_convert_fusion.1.refs_0_), channel_id=1, source_target_pairs={{0,4},{4,0},{8,12},{12,8},{1,5},{5,1},{9,13},{13,9},{2,6},{6,2},{1... | collective-permute-start | bytes 196616 | tf_op jit(solution)/shard_map/ppermute | solution.py:335
  84.1 1.9 %collective-permute-done.20.refs_3_ = bf16[8,32,128]{2,1,0:T(8,128)(2,1)S(1)} collective-permute-done((bf16[8,32,128]{2,1,0:T(8,128)(2,1)S(1)}, bf16[8,32,128]{2,1,0:T(8,128)(2,1)S(1)}, u32[]{:S(2)}, u32[]{:S(2)}) %collective-permute-start.20) | collective-permute-done | bytes 65568 | tf_op jit(solution)/shard_map/ppermute | solution.py:335
  85.9 1.7 %collective-permute-done.19.refs_2_ = bf16[8,32,128]{2,1,0:T(8,128)(2,1)S(1)} collective-permute-done((bf16[8,32,128]{2,1,0:T(8,128)(2,1)S(1)}, bf16[8,32,128]{2,1,0:T(8,128)(2,1)S(1)}, u32[]{:S(2)}, u32[]{:S(2)}) %collective-permute-start.19) | collective-permute-done | bytes 65568 | tf_op jit(solution)/shard_map/ppermute | solution.py:335
  87.6 0.2 gram.3
  87.8 1.4 %collective-permute-start.22 = (f32[32,32]{1,0:T(8,128)S(1)}, f32[32,32]{1,0:T(8,128)S(1)}, u32[]{:S(2)}, u32[]{:S(2)}) collective-permute-start(f32[32,32]{1,0:T(8,128)S(1)} %get-tuple-element.56.refs_0_), channel_id=1, source_target_pairs={{0,2},{1,3},{2,0},{3,1},{4,6},{5,7},{6,4},{7,5},{8,10},{9,11},{10,... | collective-permute-start | bytes 12296 | tf_op jit(solution)/shard_map/ppermute | solution.py:335
  89.2 0.5 collective-permute-start.21
  89.7 1.4 %collective-permute-done.23.refs_3_ = f32[32,32]{1,0:T(8,128)S(1)} collective-permute-done((f32[32,32]{1,0:T(8,128)S(1)}, f32[32,32]{1,0:T(8,128)S(1)}, u32[]{:S(2)}, u32[]{:S(2)}) %collective-permute-start.23) | collective-permute-done | bytes 4128 | tf_op jit(solution)/shard_map/ppermute | solution.py:335
  91.1 0.6 collective-permute-done.22.refs_2_
  91.6 3.8 %basis.1 = f32[32,4096]{1,0:T(8,128)} custom-call(bf16[32,32,128]{2,1,0:T(8,128)(2,1)S(1)} %get-tuple-element.55.w_ref, f32[32,32]{1,0:T(8,128)S(1)} %get-tuple-element.56.refs_0_, f32[32,32]{1,0:T(8,128)S(1)} %collective-permute-done.21.refs_1_, f32[32,32]{1,0:T(8,128)S(1)} %collective-permute-done.22.refs_2_, f32[32,32]{1,0:T(8,128)S(1)} %collective-permute-done.23.refs_3_), custom_call_target="tpu_custom_call" | custom-call | flops 4294967296 | tf_op jit(solution)/shard_map/basis/pallas_call | solution.py:486
  (26 shorter events, 0.3 us)
Async XLA Ops:
  0.0 13.3 %copy-start.3 = (s32[8192]{0:T(1024)S(1)}, s32[8192]{0:T(1024)}, u32[]{:S(2)}) copy-start(s32[8192]{0:T(1024)} %param.9) | copy-start | bytes 98308
  8.7 1.7 %collective-permute-start = (bf16[32,32,128]{2,1,0:T(8,128)(2,1)S(1)}, bf16[32,32,128]{2,1,0:T(8,128)(2,1)S(1)}, u32[]{:S(2)}, u32[]{:S(2)}) collective-permute-start(bf16[32,32,128]{2,1,0:T(8,128)(2,1)S(1)} %get-tuple-element.32), channel_id=1, source_target_pairs={{0,1},{1,0},{2,3},{3,2},{4,5},{5,4},{6,7},{7,6},{8,9},{9,8},{10,11... | collective-permute-start | bytes 786440 | tf_op jit(solution)/shard_map/ppermute | solution.py:335
  10.4 10.0 %collective-permute-start.1 = (bf16[32,32,128]{2,1,0:T(8,128)(2,1)S(1)}, bf16[32,32,128]{2,1,0:T(8,128)(2,1)S(1)}, u32[]{:S(2)}, u32[]{:S(2)}) collective-permute-start(bf16[32,32,128]{2,1,0:T(8,128)(2,1)S(1)} %fusion), channel_id=1, source_target_pairs={{0,2},{1,3},{2,0},{3,1},{4,6},{5,7},{6,4},{7,5},{8,10},{9,11},{10,... | collective-permute-start | bytes 786440 | tf_op jit(solution)/shard_map/ppermute | solution.py:335
  13.3 8.8 %copy-start = (s32[4096]{0:T(1024)S(1)}, s32[4096]{0:T(1024)}, u32[]{:S(2)}) copy-start(s32[4096]{0:T(1024)} %param.10) | copy-start | bytes 49156
  13.3 8.8 %copy-start.1 = (s32[640]{0:T(1024)S(1)}, s32[640]{0:T(1024)}, u32[]{:S(2)}) copy-start(s32[640]{0:T(1024)} %rows_ref.5) | copy-start | bytes 7684
  13.4 8.8 %copy-start.2 = (s32[640]{0:T(1024)S(1)}, s32[640]{0:T(1024)}, u32[]{:S(2)}) copy-start(s32[640]{0:T(1024)} %cols_ref.5) | copy-start | bytes 7684
  20.5 1.6 %collective-permute-start.2 = (bf16[32,32,128]{2,1,0:T(8,128)(2,1)S(1)}, bf16[32,32,128]{2,1,0:T(8,128)(2,1)S(1)}, u32[]{:S(2)}, u32[]{:S(2)}) collective-permute-start(bf16[32,32,128]{2,1,0:T(8,128)(2,1)S(1)} %divide_convert_fusion.mine_ref), channel_id=1, source_target_pairs={{0,1},{1,0},{2,3},{3,2},{4,5},{5,4},{6,7},{7,6},{8,9},{9,8},{10,11... | collective-permute-start | bytes 786440 | tf_op jit(solution)/shard_map/ppermute | solution.py:335
  27.4 6.5 %collective-permute-start.3 = (bf16[8,32,128]{2,1,0:T(8,128)(2,1)S(1)}, bf16[8,32,128]{2,1,0:T(8,128)(2,1)S(1)}, u32[]{:S(2)}, u32[]{:S(2)}) collective-permute-start(bf16[8,32,128]{2,1,0:T(8,128)(2,1)S(1)} %get-tuple-element.39), channel_id=1, source_target_pairs={{0,4},{4,0},{8,12},{12,8},{1,5},{5,1},{9,13},{13,9},{2,6},{6,2},{1... | collective-permute-start | bytes 196616 | tf_op jit(solution)/shard_map/ppermute | solution.py:335
  29.0 7.5 %collective-permute-start.4 = (bf16[8,32,128]{2,1,0:T(8,128)(2,1)S(1)}, bf16[8,32,128]{2,1,0:T(8,128)(2,1)S(1)}, u32[]{:S(2)}, u32[]{:S(2)}) collective-permute-start(bf16[8,32,128]{2,1,0:T(8,128)(2,1)S(1)} %get-tuple-element.40), channel_id=1, source_target_pairs={{0,8},{4,12},{8,0},{12,4},{1,9},{5,13},{9,1},{13,5},{2,10},{6,14},... | collective-permute-start | bytes 196616 | tf_op jit(solution)/shard_map/ppermute | solution.py:335
  31.6 6.2 %collective-permute-start.5 = (bf16[8,32,128]{2,1,0:T(8,128)(2,1)S(1)}, bf16[8,32,128]{2,1,0:T(8,128)(2,1)S(1)}, u32[]{:S(2)}, u32[]{:S(2)}) collective-permute-start(bf16[8,32,128]{2,1,0:T(8,128)(2,1)S(1)} %get-tuple-element.41), channel_id=1, source_target_pairs={{0,12},{4,8},{8,4},{12,0},{1,13},{5,9},{9,5},{13,1},{2,14},{6,10},... | collective-permute-start | bytes 196616 | tf_op jit(solution)/shard_map/ppermute | solution.py:335
  37.9 6.3 %collective-permute-start.8 = (bf16[8,32,128]{2,1,0:T(8,128)(2,1)S(1)}, bf16[8,32,128]{2,1,0:T(8,128)(2,1)S(1)}, u32[]{:S(2)}, u32[]{:S(2)}) collective-permute-start(bf16[8,32,128]{2,1,0:T(8,128)(2,1)S(1)} %add_convert_fusion.2.refs_0_), channel_id=1, source_target_pairs={{0,12},{4,8},{8,4},{12,0},{1,13},{5,9},{9,5},{13,1},{2,14},{6,10},... | collective-permute-start | bytes 196616 | tf_op jit(solution)/shard_map/ppermute | solution.py:335
  39.9 5.7 %collective-permute-start.7 = (bf16[8,32,128]{2,1,0:T(8,128)(2,1)S(1)}, bf16[8,32,128]{2,1,0:T(8,128)(2,1)S(1)}, u32[]{:S(2)}, u32[]{:S(2)}) collective-permute-start(bf16[8,32,128]{2,1,0:T(8,128)(2,1)S(1)} %add_convert_fusion.2.refs_0_), channel_id=1, source_target_pairs={{0,8},{4,12},{8,0},{12,4},{1,9},{5,13},{9,1},{13,5},{2,10},{6,14},... | collective-permute-start | bytes 196616 | tf_op jit(solution)/shard_map/ppermute | solution.py:335
  40.2 5.4 %collective-permute-start.6 = (bf16[8,32,128]{2,1,0:T(8,128)(2,1)S(1)}, bf16[8,32,128]{2,1,0:T(8,128)(2,1)S(1)}, u32[]{:S(2)}, u32[]{:S(2)}) collective-permute-start(bf16[8,32,128]{2,1,0:T(8,128)(2,1)S(1)} %add_convert_fusion.2.refs_0_), channel_id=1, source_target_pairs={{0,4},{4,0},{8,12},{12,8},{1,5},{5,1},{9,13},{13,9},{2,6},{6,2},{1... | collective-permute-start | bytes 196616 | tf_op jit(solution)/shard_map/ppermute | solution.py:335
  51.8 2.2 %collective-permute-start.12 = (bf16[32,32,128]{2,1,0:T(8,128)(2,1)S(1)}, bf16[32,32,128]{2,1,0:T(8,128)(2,1)S(1)}, u32[]{:S(2)}, u32[]{:S(2)}) collective-permute-start(bf16[32,32,128]{2,1,0:T(8,128)(2,1)S(1)} %get-tuple-element.50), channel_id=1, source_target_pairs={{0,1},{1,0},{2,3},{3,2},{4,5},{5,4},{6,7},{7,6},{8,9},{9,8},{10,11... | collective-permute-start | bytes 786440 | tf_op jit(solution)/shard_map/ppermute | solution.py:335
  51.8 3.6 %collective-permute-start.11 = (f32[32,32]{1,0:T(8,128)S(1)}, f32[32,32]{1,0:T(8,128)S(1)}, u32[]{:S(2)}, u32[]{:S(2)}) collective-permute-start(f32[32,32]{1,0:T(8,128)S(1)} %get-tuple-element.46.refs_0_), channel_id=1, source_target_pairs={{0,3},{1,2},{2,1},{3,0},{4,7},{5,6},{6,5},{7,4},{8,11},{9,10},{10,... | collective-permute-start | bytes 12296 | tf_op jit(solution)/shard_map/ppermute | solution.py:335
  53.3 3.7 %collective-permute-start.10 = (f32[32,32]{1,0:T(8,128)S(1)}, f32[32,32]{1,0:T(8,128)S(1)}, u32[]{:S(2)}, u32[]{:S(2)}) collective-permute-start(f32[32,32]{1,0:T(8,128)S(1)} %get-tuple-element.46.refs_0_), channel_id=1, source_target_pairs={{0,2},{1,3},{2,0},{3,1},{4,6},{5,7},{6,4},{7,5},{8,10},{9,11},{10,... | collective-permute-start | bytes 12296 | tf_op jit(solution)/shard_map/ppermute | solution.py:335
  54.0 3.0 %collective-permute-start.9 = (f32[32,32]{1,0:T(8,128)S(1)}, f32[32,32]{1,0:T(8,128)S(1)}, u32[]{:S(2)}, u32[]{:S(2)}) collective-permute-start(f32[32,32]{1,0:T(8,128)S(1)} %get-tuple-element.46.refs_0_), channel_id=1, source_target_pairs={{0,1},{1,0},{2,3},{3,2},{4,5},{5,4},{6,7},{7,6},{8,9},{9,8},{10,11... | collective-permute-start | bytes 12296 | tf_op jit(solution)/shard_map/ppermute | solution.py:335
  54.1 8.8 %collective-permute-start.13 = (bf16[32,32,128]{2,1,0:T(8,128)(2,1)S(1)}, bf16[32,32,128]{2,1,0:T(8,128)(2,1)S(1)}, u32[]{:S(2)}, u32[]{:S(2)}) collective-permute-start(bf16[32,32,128]{2,1,0:T(8,128)(2,1)S(1)} %add_convert_fusion), channel_id=1, source_target_pairs={{0,2},{1,3},{2,0},{3,1},{4,6},{5,7},{6,4},{7,5},{8,10},{9,11},{10,... | collective-permute-start | bytes 786440 | tf_op jit(solution)/shard_map/ppermute | solution.py:335
  63.4 1.6 %collective-permute-start.14 = (bf16[32,32,128]{2,1,0:T(8,128)(2,1)S(1)}, bf16[32,32,128]{2,1,0:T(8,128)(2,1)S(1)}, u32[]{:S(2)}, u32[]{:S(2)}) collective-permute-start(bf16[32,32,128]{2,1,0:T(8,128)(2,1)S(1)} %mix.1.mine_ref), channel_id=1, source_target_pairs={{0,1},{1,0},{2,3},{3,2},{4,5},{5,4},{6,7},{7,6},{8,9},{9,8},{10,11... | collective-permute-start | bytes 786440 | tf_op jit(solution)/shard_map/ppermute | solution.py:335
  70.3 4.5 %collective-permute-start.15 = (bf16[8,32,128]{2,1,0:T(8,128)(2,1)S(1)}, bf16[8,32,128]{2,1,0:T(8,128)(2,1)S(1)}, u32[]{:S(2)}, u32[]{:S(2)}) collective-permute-start(bf16[8,32,128]{2,1,0:T(8,128)(2,1)S(1)} %get-tuple-element.52), channel_id=1, source_target_pairs={{0,4},{4,0},{8,12},{12,8},{1,5},{5,1},{9,13},{13,9},{2,6},{6,2},{1... | collective-permute-start | bytes 196616 | tf_op jit(solution)/shard_map/ppermute | solution.py:335
  71.3 8.2 %collective-permute-start.16 = (bf16[8,32,128]{2,1,0:T(8,128)(2,1)S(1)}, bf16[8,32,128]{2,1,0:T(8,128)(2,1)S(1)}, u32[]{:S(2)}, u32[]{:S(2)}) collective-permute-start(bf16[8,32,128]{2,1,0:T(8,128)(2,1)S(1)} %get-tuple-element.53), channel_id=1, source_target_pairs={{0,8},{4,12},{8,0},{12,4},{1,9},{5,13},{9,1},{13,5},{2,10},{6,14},... | collective-permute-start | bytes 196616 | tf_op jit(solution)/shard_map/ppermute | solution.py:335
  72.9 6.7 %collective-permute-start.17 = (bf16[8,32,128]{2,1,0:T(8,128)(2,1)S(1)}, bf16[8,32,128]{2,1,0:T(8,128)(2,1)S(1)}, u32[]{:S(2)}, u32[]{:S(2)}) collective-permute-start(bf16[8,32,128]{2,1,0:T(8,128)(2,1)S(1)} %get-tuple-element.54), channel_id=1, source_target_pairs={{0,12},{4,8},{8,4},{12,0},{1,13},{5,9},{9,5},{13,1},{2,14},{6,10},... | collective-permute-start | bytes 196616 | tf_op jit(solution)/shard_map/ppermute | solution.py:335
  79.6 6.3 %collective-permute-start.20 = (bf16[8,32,128]{2,1,0:T(8,128)(2,1)S(1)}, bf16[8,32,128]{2,1,0:T(8,128)(2,1)S(1)}, u32[]{:S(2)}, u32[]{:S(2)}) collective-permute-start(bf16[8,32,128]{2,1,0:T(8,128)(2,1)S(1)} %add_convert_fusion.1.refs_0_), channel_id=1, source_target_pairs={{0,12},{4,8},{8,4},{12,0},{1,13},{5,9},{9,5},{13,1},{2,14},{6,10},... | collective-permute-start | bytes 196616 | tf_op jit(solution)/shard_map/ppermute | solution.py:335
  81.7 5.9 %collective-permute-start.19 = (bf16[8,32,128]{2,1,0:T(8,128)(2,1)S(1)}, bf16[8,32,128]{2,1,0:T(8,128)(2,1)S(1)}, u32[]{:S(2)}, u32[]{:S(2)}) collective-permute-start(bf16[8,32,128]{2,1,0:T(8,128)(2,1)S(1)} %add_convert_fusion.1.refs_0_), channel_id=1, source_target_pairs={{0,8},{4,12},{8,0},{12,4},{1,9},{5,13},{9,1},{13,5},{2,10},{6,14},... | collective-permute-start | bytes 196616 | tf_op jit(solution)/shard_map/ppermute | solution.py:335
  82.4 5.2 %collective-permute-start.18 = (bf16[8,32,128]{2,1,0:T(8,128)(2,1)S(1)}, bf16[8,32,128]{2,1,0:T(8,128)(2,1)S(1)}, u32[]{:S(2)}, u32[]{:S(2)}) collective-permute-start(bf16[8,32,128]{2,1,0:T(8,128)(2,1)S(1)} %add_convert_fusion.1.refs_0_), channel_id=1, source_target_pairs={{0,4},{4,0},{8,12},{12,8},{1,5},{5,1},{9,13},{13,9},{2,6},{6,2},{1... | collective-permute-start | bytes 196616 | tf_op jit(solution)/shard_map/ppermute | solution.py:335
  87.8 3.3 %collective-permute-start.23 = (f32[32,32]{1,0:T(8,128)S(1)}, f32[32,32]{1,0:T(8,128)S(1)}, u32[]{:S(2)}, u32[]{:S(2)}) collective-permute-start(f32[32,32]{1,0:T(8,128)S(1)} %get-tuple-element.56.refs_0_), channel_id=1, source_target_pairs={{0,3},{1,2},{2,1},{3,0},{4,7},{5,6},{6,5},{7,4},{8,11},{9,10},{10,... | collective-permute-start | bytes 12296 | tf_op jit(solution)/shard_map/ppermute | solution.py:335
  87.8 3.8 %collective-permute-start.22 = (f32[32,32]{1,0:T(8,128)S(1)}, f32[32,32]{1,0:T(8,128)S(1)}, u32[]{:S(2)}, u32[]{:S(2)}) collective-permute-start(f32[32,32]{1,0:T(8,128)S(1)} %get-tuple-element.56.refs_0_), channel_id=1, source_target_pairs={{0,2},{1,3},{2,0},{3,1},{4,6},{5,7},{6,4},{7,5},{8,10},{9,11},{10,... | collective-permute-start | bytes 12296 | tf_op jit(solution)/shard_map/ppermute | solution.py:335
  89.2 2.4 %collective-permute-start.21 = (f32[32,32]{1,0:T(8,128)S(1)}, f32[32,32]{1,0:T(8,128)S(1)}, u32[]{:S(2)}, u32[]{:S(2)}) collective-permute-start(f32[32,32]{1,0:T(8,128)S(1)} %get-tuple-element.56.refs_0_), channel_id=1, source_target_pairs={{0,1},{1,0},{2,3},{3,2},{4,5},{5,4},{6,7},{7,6},{8,9},{9,8},{10,11... | collective-permute-start | bytes 12296 | tf_op jit(solution)/shard_map/ppermute | solution.py:335

commit v4 on v3

--- a/solution.py
+++ b/solution.py
@@ -10,6 +10,8 @@
 ITERS = 2
 TURNED = 3
 FIRST = 128
+SECOND = 160
+BACK = 320
 SLOTS = 3
 MIX = 8
 F32 = jnp.float32
@@ -40,9 +42,7 @@
 
 
 def unroll_of(total, most):
-    while total % most:
-        most //= 2
-    return most
+    return max(size for size in range(8, most + 1, 8) if total % size == 0)
 
 
 def add_group(pieces, ids_ref, first, base, accs):
@@ -342,9 +342,9 @@
     col_blocks = col_counts.shape[0] // box
     n_src, n_dst = lax.axis_size("src"), lax.axis_size("dst")
     box_total = float(col_blocks * box * n_dst)
-    unroll = unroll_of(total, 128)
+    unroll = unroll_of(total, SECOND)
     first_unroll = unroll_of(total, FIRST)
-    turned = unroll * TURNED // 8
+    turned = unroll * TURNED // 8 // 2 * 2
     half = row_blocks // 2
     size = col_blocks // n_src
     wide_counts = col_counts.reshape(1, col_blocks * box)
@@ -394,7 +394,7 @@
                 out_specs=[VMEM, VMEM],
                 out_shape=[keep_out, send_out],
                 scratch_shapes=accs,
-                compiler_params=params(),
+                compiler_params=params(12),
                 name="forward",
                 cost_estimate=forward_cost,
             )(block_rows, block_cols, held, flipped, w_full)
@@ -443,7 +443,7 @@
         other = swap(mine, "dst", 1)
         chunk = (size, side, box)
         outs = pl.pallas_call(
-            functools.partial(adjoint_kernel, unroll, n_src),
+            functools.partial(adjoint_kernel, unroll_of(total, BACK), n_src),
             in_specs=[SMEM, SMEM] + [VMEM] * 4,
             out_specs=[VMEM] * n_src,
             out_shape=[jax.ShapeDtypeStruct(chunk, F32)]
@@ -453,7 +453,7 @@
                 pltpu.VMEM((col_blocks, side, box), F32),
                 pltpu.VMEM((col_blocks, side, box), F32),
             ],
-            compiler_params=params(),
+            compiler_params=params(12),
             name="adjoint",
                 cost_estimate=adjoint_cost,
         )(block_rows, block_cols, tall_counts, held, mine, other)

time: 95.5 us -> 94.6 us (level)
  Pallas kernels: 41.6 us -> 40.6 us
where the time goes in v4:
time: 94.6 us; the launch traced here: 94.4 us
  Pallas kernels  40.6 us (43%)
  starting transfers between devices  26.9 us (28%)
  waiting for transfers between devices  26.4 us (28%)
    ppermute x24, starting transfers between devices, swap(): return lax.ppermute(x, axis, [(i, i ^ bits) for i in range(size)])  26.9 us
    ppermute x24, waiting for transfers between devices, swap(): return lax.ppermute(x, axis, [(i, i ^ bits) for i in range(size)])  26.4 us
    pallas_call x2, Pallas kernels, per_device(): pl.pallas_call(functools.partial(adjoint_kernel, unroll_of(total, BACK),...  9.78 us
    pallas_call x1, Pallas kernels, per_device(): pl.pallas_call(functools.partial(first_forward_kernel, first_unroll), in_...  8.65 us
    pallas_call x1, Pallas kernels, per_device(): pl.pallas_call(load_kernel, in_specs=[HBM], out_specs=VMEM, out_shape=plt...  6.99 us
    pallas_call x1, Pallas kernels, per_device(): pl.pallas_call(functools.partial(forward_kernel, unroll, turned), in_spec...  5.65 us
    pallas_call x1, Pallas kernels, per_device(): pl.pallas_call(functools.partial(basis_kernel, box_total), in_specs=[VMEM...  3.8 us
    pallas_call x1, Pallas kernels, per_device(): pl.pallas_call(functools.partial(orth_kernel, box_total), in_specs=[VMEM]...  2.64 us
  transfers between devices with their start and end apart: 24, of which 14 were waited for; matrix products, arithmetic and copies ran while one was open for 0% of the time, Pallas kernels for 12%

profile of v4, /device:TPU:0, one launch (start us, length us, event | category | flops | bytes accessed | tf_op | source)
XLA Modules:
  0.0 94.4 jit_solution(16290658251083745578)
XLA Ops:
  0.0 8.7 %first_forward.1 = (f32[32,32,128]{2,1,0:T(8,128)S(1)}, bf16[32,32,128]{2,1,0:T(8,128)(2,1)S(1)}) custom-call(s32[640]{0:T(1024)} %rows_ref.5, s32[640]{0:T(1024)} %cols_ref.5, f32[32,4096]{1,0:T(8,128)} %start_hbm.1, s32[1,4096]{1,0:T(1,128)} %bitcast.7, bf16[640,128,128]{2,1,0:T(8,128)(2,1)} %hbm_ref), custom_call_target="tpu_custom_call" | custom-call | flops 10737418240 | tf_op jit(solution)/shard_map/first_forward/pallas_call | solution.py:367
  8.7 0.5 collective-permute-start
  9.2 1.2 %collective-permute-done = bf16[32,32,128]{2,1,0:T(8,128)(2,1)S(1)} collective-permute-done((bf16[32,32,128]{2,1,0:T(8,128)(2,1)S(1)}, bf16[32,32,128]{2,1,0:T(8,128)(2,1)S(1)}, u32[]{:S(2)}, u32[]{:S(2)}) %collective-permute-start) | collective-permute-done | bytes 262176 | tf_op jit(solution)/shard_map/ppermute | solution.py:335
  10.4 2.9 %collective-permute-start.1 = (bf16[32,32,128]{2,1,0:T(8,128)(2,1)S(1)}, bf16[32,32,128]{2,1,0:T(8,128)(2,1)S(1)}, u32[]{:S(2)}, u32[]{:S(2)}) collective-permute-start(bf16[32,32,128]{2,1,0:T(8,128)(2,1)S(1)} %fusion), channel_id=1, source_target_pairs={{0,2},{1,3},{2,0},{3,1},{4,6},{5,7},{6,4},{7,5},{8,10},{9,11},{10,... | collective-permute-start | bytes 786440 | tf_op jit(solution)/shard_map/ppermute | solution.py:335
  13.4 7.0 %load.1.held_ref = bf16[640,128,128]{2,1,0:T(8,128)(2,1)S(1)} custom-call(bf16[640,128,128]{2,1,0:T(8,128)(2,1)} %hbm_ref), custom_call_target="tpu_custom_call" | custom-call | bytes 41943040 | tf_op jit(solution)/shard_map/load/pallas_call | solution.py:404
  20.4 0.1 convert_add_fusion
  20.5 0.1 collective-permute-start.2
  20.6 1.5 %collective-permute-done.2.other_ref = bf16[32,32,128]{2,1,0:T(8,128)(2,1)S(1)} collective-permute-done((bf16[32,32,128]{2,1,0:T(8,128)(2,1)S(1)}, bf16[32,32,128]{2,1,0:T(8,128)(2,1)S(1)}, u32[]{:S(2)}, u32[]{:S(2)}) %collective-permute-start.2) | collective-permute-done | bytes 262176 | tf_op jit(solution)/shard_map/ppermute | solution.py:335
  22.1 4.9 %adjoint.2 = (f32[8,32,128]{2,1,0:T(8,128)S(1)}, bf16[8,32,128]{2,1,0:T(8,128)(2,1)S(1)}, bf16[8,32,128]{2,1,0:T(8,128)(2,1)S(1)}, bf16[8,32,128]{2,1,0:T(8,128)(2,1)S(1)}) custom-call(s32[640]{0:T(1024)S(1)} %copy-done.1, s32[640]{0:T(1024)S(1)} %copy-done.2, s32[32,1,128]{2,1,0:T(1,128)S(1)} %bitcast.8, bf16[640,128,128]{2,1,0:T(8,128)(2,1)S(1)} %load.1.held_ref, ...), custom_call_target="tpu_custom_call" | custom-call | flops 5368709120 | tf_op jit(solution)/shard_map/adjoint/pallas_call | solution.py:445
  27.0 1.6 %collective-permute-start.3 = (bf16[8,32,128]{2,1,0:T(8,128)(2,1)S(1)}, bf16[8,32,128]{2,1,0:T(8,128)(2,1)S(1)}, u32[]{:S(2)}, u32[]{:S(2)}) collective-permute-start(bf16[8,32,128]{2,1,0:T(8,128)(2,1)S(1)} %get-tuple-element.39), channel_id=1, source_target_pairs={{0,4},{4,0},{8,12},{12,8},{1,5},{5,1},{9,13},{13,9},{2,6},{6,2},{1... | collective-permute-start | bytes 196616 | tf_op jit(solution)/shard_map/ppermute | solution.py:335
  28.7 2.6 %collective-permute-start.4 = (bf16[8,32,128]{2,1,0:T(8,128)(2,1)S(1)}, bf16[8,32,128]{2,1,0:T(8,128)(2,1)S(1)}, u32[]{:S(2)}, u32[]{:S(2)}) collective-permute-start(bf16[8,32,128]{2,1,0:T(8,128)(2,1)S(1)} %get-tuple-element.40), channel_id=1, source_target_pairs={{0,8},{4,12},{8,0},{12,4},{1,9},{5,13},{9,1},{13,5},{2,10},{6,14},... | collective-permute-start | bytes 196616 | tf_op jit(solution)/shard_map/ppermute | solution.py:335
  31.3 0.2 collective-permute-start.5
  31.5 2.1 %turn.1.turned_ref = bf16[240,128,128]{2,1,0:T(8,128)(2,1)S(1)} custom-call(bf16[640,128,128]{2,1,0:T(8,128)(2,1)S(1)} %load.1.held_ref), custom_call_target="tpu_custom_call" | custom-call | flops 5368709120 | tf_op jit(solution)/shard_map/turn/pallas_call | solution.py:464
  33.6 2.6 %collective-permute-done.4 = bf16[8,32,128]{2,1,0:T(8,128)(2,1)S(1)} collective-permute-done((bf16[8,32,128]{2,1,0:T(8,128)(2,1)S(1)}, bf16[8,32,128]{2,1,0:T(8,128)(2,1)S(1)}, u32[]{:S(2)}, u32[]{:S(2)}) %collective-permute-start.4) | collective-permute-done | bytes 65568 | tf_op jit(solution)/shard_map/ppermute | solution.py:335
  36.2 1.2 %collective-permute-done.5 = bf16[8,32,128]{2,1,0:T(8,128)(2,1)S(1)} collective-permute-done((bf16[8,32,128]{2,1,0:T(8,128)(2,1)S(1)}, bf16[8,32,128]{2,1,0:T(8,128)(2,1)S(1)}, u32[]{:S(2)}, u32[]{:S(2)}) %collective-permute-start.5) | collective-permute-done | bytes 65568 | tf_op jit(solution)/shard_map/ppermute | solution.py:335
  37.5 2.0 %collective-permute-start.8 = (bf16[8,32,128]{2,1,0:T(8,128)(2,1)S(1)}, bf16[8,32,128]{2,1,0:T(8,128)(2,1)S(1)}, u32[]{:S(2)}, u32[]{:S(2)}) collective-permute-start(bf16[8,32,128]{2,1,0:T(8,128)(2,1)S(1)} %add_convert_fusion.2.refs_0_), channel_id=1, source_target_pairs={{0,12},{4,8},{8,4},{12,0},{1,13},{5,9},{9,5},{13,1},{2,14},{6,10},... | collective-permute-start | bytes 196616 | tf_op jit(solution)/shard_map/ppermute | solution.py:335
  39.5 0.3 collective-permute-start.7
  39.8 2.1 %collective-permute-start.6 = (bf16[8,32,128]{2,1,0:T(8,128)(2,1)S(1)}, bf16[8,32,128]{2,1,0:T(8,128)(2,1)S(1)}, u32[]{:S(2)}, u32[]{:S(2)}) collective-permute-start(bf16[8,32,128]{2,1,0:T(8,128)(2,1)S(1)} %add_convert_fusion.2.refs_0_), channel_id=1, source_target_pairs={{0,4},{4,0},{8,12},{12,8},{1,5},{5,1},{9,13},{13,9},{2,6},{6,2},{1... | collective-permute-start | bytes 196616 | tf_op jit(solution)/shard_map/ppermute | solution.py:335
  41.9 1.8 %collective-permute-done.8.refs_3_ = bf16[8,32,128]{2,1,0:T(8,128)(2,1)S(1)} collective-permute-done((bf16[8,32,128]{2,1,0:T(8,128)(2,1)S(1)}, bf16[8,32,128]{2,1,0:T(8,128)(2,1)S(1)}, u32[]{:S(2)}, u32[]{:S(2)}) %collective-permute-start.8) | collective-permute-done | bytes 65568 | tf_op jit(solution)/shard_map/ppermute | solution.py:335
  43.7 1.5 %collective-permute-done.7.refs_2_ = bf16[8,32,128]{2,1,0:T(8,128)(2,1)S(1)} collective-permute-done((bf16[8,32,128]{2,1,0:T(8,128)(2,1)S(1)}, bf16[8,32,128]{2,1,0:T(8,128)(2,1)S(1)}, u32[]{:S(2)}, u32[]{:S(2)}) %collective-permute-start.7) | collective-permute-done | bytes 65568 | tf_op jit(solution)/shard_map/ppermute | solution.py:335
  45.3 0.2 gram.2
  45.5 5.7 %forward.1 = (f32[32,32,128]{2,1,0:T(8,128)S(1)}, bf16[32,32,128]{2,1,0:T(8,128)(2,1)S(1)}) custom-call(s32[640]{0:T(1024)S(1)} %copy-done.1, s32[640]{0:T(1024)S(1)} %copy-done.2, bf16[640,128,128]{2,1,0:T(8,128)(2,1)S(1)} %load.1.held_ref, bf16[240,128,128]{2,1,0:T(8,128)(2,1)S(1)} %turn.1.turned_ref, bf16[32,32,128]{2,1,0:T(8,128)(2,1)S(1)} %get-tuple-element.48.panel_ref), custom_call_target="tpu_custom_call" | custom-call | flops 10737418240 | tf_op jit(solution)/shard_map/forward/pallas_call | solution.py:391
  51.2 0.1 collective-permute-start.12
  51.2 1.4 %collective-permute-start.11 = (f32[32,32]{1,0:T(8,128)S(1)}, f32[32,32]{1,0:T(8,128)S(1)}, u32[]{:S(2)}, u32[]{:S(2)}) collective-permute-start(f32[32,32]{1,0:T(8,128)S(1)} %get-tuple-element.46.refs_0_), channel_id=1, source_target_pairs={{0,3},{1,2},{2,1},{3,0},{4,7},{5,6},{6,5},{7,4},{8,11},{9,10},{10,... | collective-permute-start | bytes 12296 | tf_op jit(solution)/shard_map/ppermute | solution.py:335
  52.7 0.7 collective-permute-start.10
  53.4 0.1 add_convert_fusion
  53.5 1.4 %collective-permute-start.13 = (bf16[32,32,128]{2,1,0:T(8,128)(2,1)S(1)}, bf16[32,32,128]{2,1,0:T(8,128)(2,1)S(1)}, u32[]{:S(2)}, u32[]{:S(2)}) collective-permute-start(bf16[32,32,128]{2,1,0:T(8,128)(2,1)S(1)} %add_convert_fusion), channel_id=1, source_target_pairs={{0,2},{1,3},{2,0},{3,1},{4,6},{5,7},{6,4},{7,5},{8,10},{9,11},{10,... | collective-permute-start | bytes 786440 | tf_op jit(solution)/shard_map/ppermute | solution.py:335
  54.9 1.6 %collective-permute-done.10.refs_2_ = f32[32,32]{1,0:T(8,128)S(1)} collective-permute-done((f32[32,32]{1,0:T(8,128)S(1)}, f32[32,32]{1,0:T(8,128)S(1)}, u32[]{:S(2)}, u32[]{:S(2)}) %collective-permute-start.10) | collective-permute-done | bytes 4128 | tf_op jit(solution)/shard_map/ppermute | solution.py:335
  56.4 2.6 %orth.1.matrix_ref = f32[32,32]{1,0:T(8,128)S(1)} custom-call(f32[32,32]{1,0:T(8,128)S(1)} %get-tuple-element.46.refs_0_, f32[32,32]{1,0:T(8,128)S(1)} %collective-permute-done.9.refs_1_, f32[32,32]{1,0:T(8,128)S(1)} %collective-permute-done.10.refs_2_, f32[32,32]{1,0:T(8,128)S(1)} %collective-permute-done.11.refs_3_), custom_call_target="tpu_custom_call" | custom-call | flops 4294967296 | tf_op jit(solution)/shard_map/orth/pallas_call | solution.py:425
  59.1 3.2 %collective-permute-done.13.refs_0_ = bf16[32,32,128]{2,1,0:T(8,128)(2,1)S(1)} collective-permute-done((bf16[32,32,128]{2,1,0:T(8,128)(2,1)S(1)}, bf16[32,32,128]{2,1,0:T(8,128)(2,1)S(1)}, u32[]{:S(2)}, u32[]{:S(2)}) %collective-permute-start.13) | collective-permute-done | bytes 262176 | tf_op jit(solution)/shard_map/ppermute | solution.py:335
  62.2 0.6 mix.1.mine_ref
  62.9 1.5 %collective-permute-done.14.other_ref = bf16[32,32,128]{2,1,0:T(8,128)(2,1)S(1)} collective-permute-done((bf16[32,32,128]{2,1,0:T(8,128)(2,1)S(1)}, bf16[32,32,128]{2,1,0:T(8,128)(2,1)S(1)}, u32[]{:S(2)}, u32[]{:S(2)}) %collective-permute-start.14) | collective-permute-done | bytes 262176 | tf_op jit(solution)/shard_map/ppermute | solution.py:335
  64.4 4.9 %adjoint.3 = (f32[8,32,128]{2,1,0:T(8,128)S(1)}, bf16[8,32,128]{2,1,0:T(8,128)(2,1)S(1)}, bf16[8,32,128]{2,1,0:T(8,128)(2,1)S(1)}, bf16[8,32,128]{2,1,0:T(8,128)(2,1)S(1)}) custom-call(s32[640]{0:T(1024)S(1)} %copy-done.1, s32[640]{0:T(1024)S(1)} %copy-done.2, s32[32,1,128]{2,1,0:T(1,128)S(1)} %bitcast.10, bf16[640,128,128]{2,1,0:T(8,128)(2,1)S(1)} %load.1.held_ref, ...), custom_call_target="tpu_custom_call" | custom-call | flops 5368709120 | tf_op jit(solution)/shard_map/adjoint/pallas_call | solution.py:445
  69.3 1.0 %collective-permute-start.15 = (bf16[8,32,128]{2,1,0:T(8,128)(2,1)S(1)}, bf16[8,32,128]{2,1,0:T(8,128)(2,1)S(1)}, u32[]{:S(2)}, u32[]{:S(2)}) collective-permute-start(bf16[8,32,128]{2,1,0:T(8,128)(2,1)S(1)} %get-tuple-element.52), channel_id=1, source_target_pairs={{0,4},{4,0},{8,12},{12,8},{1,5},{5,1},{9,13},{13,9},{2,6},{6,2},{1... | collective-permute-start | bytes 196616 | tf_op jit(solution)/shard_map/ppermute | solution.py:335
  70.3 1.6 %collective-permute-start.16 = (bf16[8,32,128]{2,1,0:T(8,128)(2,1)S(1)}, bf16[8,32,128]{2,1,0:T(8,128)(2,1)S(1)}, u32[]{:S(2)}, u32[]{:S(2)}) collective-permute-start(bf16[8,32,128]{2,1,0:T(8,128)(2,1)S(1)} %get-tuple-element.53), channel_id=1, source_target_pairs={{0,8},{4,12},{8,0},{12,4},{1,9},{5,13},{9,1},{13,5},{2,10},{6,14},... | collective-permute-start | bytes 196616 | tf_op jit(solution)/shard_map/ppermute | solution.py:335
  71.9 1.9 %collective-permute-start.17 = (bf16[8,32,128]{2,1,0:T(8,128)(2,1)S(1)}, bf16[8,32,128]{2,1,0:T(8,128)(2,1)S(1)}, u32[]{:S(2)}, u32[]{:S(2)}) collective-permute-start(bf16[8,32,128]{2,1,0:T(8,128)(2,1)S(1)} %get-tuple-element.54), channel_id=1, source_target_pairs={{0,12},{4,8},{8,4},{12,0},{1,13},{5,9},{9,5},{13,1},{2,14},{6,10},... | collective-permute-start | bytes 196616 | tf_op jit(solution)/shard_map/ppermute | solution.py:335
  73.8 4.8 %collective-permute-done.16 = bf16[8,32,128]{2,1,0:T(8,128)(2,1)S(1)} collective-permute-done((bf16[8,32,128]{2,1,0:T(8,128)(2,1)S(1)}, bf16[8,32,128]{2,1,0:T(8,128)(2,1)S(1)}, u32[]{:S(2)}, u32[]{:S(2)}) %collective-permute-start.16) | collective-permute-done | bytes 65568 | tf_op jit(solution)/shard_map/ppermute | solution.py:335
  78.6 2.0 %collective-permute-start.20 = (bf16[8,32,128]{2,1,0:T(8,128)(2,1)S(1)}, bf16[8,32,128]{2,1,0:T(8,128)(2,1)S(1)}, u32[]{:S(2)}, u32[]{:S(2)}) collective-permute-start(bf16[8,32,128]{2,1,0:T(8,128)(2,1)S(1)} %add_convert_fusion.1.refs_0_), channel_id=1, source_target_pairs={{0,12},{4,8},{8,4},{12,0},{1,13},{5,9},{9,5},{13,1},{2,14},{6,10},... | collective-permute-start | bytes 196616 | tf_op jit(solution)/shard_map/ppermute | solution.py:335
  80.7 0.7 collective-permute-start.19
  81.4 1.7 %collective-permute-start.18 = (bf16[8,32,128]{2,1,0:T(8,128)(2,1)S(1)}, bf16[8,32,128]{2,1,0:T(8,128)(2,1)S(1)}, u32[]{:S(2)}, u32[]{:S(2)}) collective-permute-start(bf16[8,32,128]{2,1,0:T(8,128)(2,1)S(1)} %add_convert_fusion.1.refs_0_), channel_id=1, source_target_pairs={{0,4},{4,0},{8,12},{12,8},{1,5},{5,1},{9,13},{13,9},{2,6},{6,2},{1... | collective-permute-start | bytes 196616 | tf_op jit(solution)/shard_map/ppermute | solution.py:335
  83.1 1.9 %collective-permute-done.20.refs_3_ = bf16[8,32,128]{2,1,0:T(8,128)(2,1)S(1)} collective-permute-done((bf16[8,32,128]{2,1,0:T(8,128)(2,1)S(1)}, bf16[8,32,128]{2,1,0:T(8,128)(2,1)S(1)}, u32[]{:S(2)}, u32[]{:S(2)}) %collective-permute-start.20) | collective-permute-done | bytes 65568 | tf_op jit(solution)/shard_map/ppermute | solution.py:335
  85.0 1.7 %collective-permute-done.19.refs_2_ = bf16[8,32,128]{2,1,0:T(8,128)(2,1)S(1)} collective-permute-done((bf16[8,32,128]{2,1,0:T(8,128)(2,1)S(1)}, bf16[8,32,128]{2,1,0:T(8,128)(2,1)S(1)}, u32[]{:S(2)}, u32[]{:S(2)}) %collective-permute-start.19) | collective-permute-done | bytes 65568 | tf_op jit(solution)/shard_map/ppermute | solution.py:335
  86.6 0.2 gram.3
  86.8 1.4 %collective-permute-start.22 = (f32[32,32]{1,0:T(8,128)S(1)}, f32[32,32]{1,0:T(8,128)S(1)}, u32[]{:S(2)}, u32[]{:S(2)}) collective-permute-start(f32[32,32]{1,0:T(8,128)S(1)} %get-tuple-element.56.refs_0_), channel_id=1, source_target_pairs={{0,2},{1,3},{2,0},{3,1},{4,6},{5,7},{6,4},{7,5},{8,10},{9,11},{10,... | collective-permute-start | bytes 12296 | tf_op jit(solution)/shard_map/ppermute | solution.py:335
  88.2 0.5 collective-permute-start.21
  88.7 1.4 %collective-permute-done.23.refs_3_ = f32[32,32]{1,0:T(8,128)S(1)} collective-permute-done((f32[32,32]{1,0:T(8,128)S(1)}, f32[32,32]{1,0:T(8,128)S(1)}, u32[]{:S(2)}, u32[]{:S(2)}) %collective-permute-start.23) | collective-permute-done | bytes 4128 | tf_op jit(solution)/shard_map/ppermute | solution.py:335
  90.1 0.6 collective-permute-done.22.refs_2_
  90.6 3.8 %basis.1 = f32[32,4096]{1,0:T(8,128)} custom-call(bf16[32,32,128]{2,1,0:T(8,128)(2,1)S(1)} %get-tuple-element.55.w_ref, f32[32,32]{1,0:T(8,128)S(1)} %get-tuple-element.56.refs_0_, f32[32,32]{1,0:T(8,128)S(1)} %collective-permute-done.21.refs_1_, f32[32,32]{1,0:T(8,128)S(1)} %collective-permute-done.22.refs_2_, f32[32,32]{1,0:T(8,128)S(1)} %collective-permute-done.23.refs_3_), custom_call_target="tpu_custom_call" | custom-call | flops 4294967296 | tf_op jit(solution)/shard_map/basis/pallas_call | solution.py:486
  (26 shorter events, 0.3 us)
Async XLA Ops:
  0.0 13.3 %copy-start.3 = (s32[8192]{0:T(1024)S(1)}, s32[8192]{0:T(1024)}, u32[]{:S(2)}) copy-start(s32[8192]{0:T(1024)} %param.9) | copy-start | bytes 98308
  8.7 1.7 %collective-permute-start = (bf16[32,32,128]{2,1,0:T(8,128)(2,1)S(1)}, bf16[32,32,128]{2,1,0:T(8,128)(2,1)S(1)}, u32[]{:S(2)}, u32[]{:S(2)}) collective-permute-start(bf16[32,32,128]{2,1,0:T(8,128)(2,1)S(1)} %get-tuple-element.32), channel_id=1, source_target_pairs={{0,1},{1,0},{2,3},{3,2},{4,5},{5,4},{6,7},{7,6},{8,9},{9,8},{10,11... | collective-permute-start | bytes 786440 | tf_op jit(solution)/shard_map/ppermute | solution.py:335
  10.4 10.0 %collective-permute-start.1 = (bf16[32,32,128]{2,1,0:T(8,128)(2,1)S(1)}, bf16[32,32,128]{2,1,0:T(8,128)(2,1)S(1)}, u32[]{:S(2)}, u32[]{:S(2)}) collective-permute-start(bf16[32,32,128]{2,1,0:T(8,128)(2,1)S(1)} %fusion), channel_id=1, source_target_pairs={{0,2},{1,3},{2,0},{3,1},{4,6},{5,7},{6,4},{7,5},{8,10},{9,11},{10,... | collective-permute-start | bytes 786440 | tf_op jit(solution)/shard_map/ppermute | solution.py:335
  13.3 8.8 %copy-start = (s32[4096]{0:T(1024)S(1)}, s32[4096]{0:T(1024)}, u32[]{:S(2)}) copy-start(s32[4096]{0:T(1024)} %param.10) | copy-start | bytes 49156
  13.3 8.8 %copy-start.1 = (s32[640]{0:T(1024)S(1)}, s32[640]{0:T(1024)}, u32[]{:S(2)}) copy-start(s32[640]{0:T(1024)} %rows_ref.5) | copy-start | bytes 7684
  13.3 8.8 %copy-start.2 = (s32[640]{0:T(1024)S(1)}, s32[640]{0:T(1024)}, u32[]{:S(2)}) copy-start(s32[640]{0:T(1024)} %cols_ref.5) | copy-start | bytes 7684
  20.5 1.6 %collective-permute-start.2 = (bf16[32,32,128]{2,1,0:T(8,128)(2,1)S(1)}, bf16[32,32,128]{2,1,0:T(8,128)(2,1)S(1)}, u32[]{:S(2)}, u32[]{:S(2)}) collective-permute-start(bf16[32,32,128]{2,1,0:T(8,128)(2,1)S(1)} %divide_convert_fusion.mine_ref), channel_id=1, source_target_pairs={{0,1},{1,0},{2,3},{3,2},{4,5},{5,4},{6,7},{7,6},{8,9},{9,8},{10,11... | collective-permute-start | bytes 786440 | tf_op jit(solution)/shard_map/ppermute | solution.py:335
  27.0 6.5 %collective-permute-start.3 = (bf16[8,32,128]{2,1,0:T(8,128)(2,1)S(1)}, bf16[8,32,128]{2,1,0:T(8,128)(2,1)S(1)}, u32[]{:S(2)}, u32[]{:S(2)}) collective-permute-start(bf16[8,32,128]{2,1,0:T(8,128)(2,1)S(1)} %get-tuple-element.39), channel_id=1, source_target_pairs={{0,4},{4,0},{8,12},{12,8},{1,5},{5,1},{9,13},{13,9},{2,6},{6,2},{1... | collective-permute-start | bytes 196616 | tf_op jit(solution)/shard_map/ppermute | solution.py:335
  28.7 7.5 %collective-permute-start.4 = (bf16[8,32,128]{2,1,0:T(8,128)(2,1)S(1)}, bf16[8,32,128]{2,1,0:T(8,128)(2,1)S(1)}, u32[]{:S(2)}, u32[]{:S(2)}) collective-permute-start(bf16[8,32,128]{2,1,0:T(8,128)(2,1)S(1)} %get-tuple-element.40), channel_id=1, source_target_pairs={{0,8},{4,12},{8,0},{12,4},{1,9},{5,13},{9,1},{13,5},{2,10},{6,14},... | collective-permute-start | bytes 196616 | tf_op jit(solution)/shard_map/ppermute | solution.py:335
  31.3 6.2 %collective-permute-start.5 = (bf16[8,32,128]{2,1,0:T(8,128)(2,1)S(1)}, bf16[8,32,128]{2,1,0:T(8,128)(2,1)S(1)}, u32[]{:S(2)}, u32[]{:S(2)}) collective-permute-start(bf16[8,32,128]{2,1,0:T(8,128)(2,1)S(1)} %get-tuple-element.41), channel_id=1, source_target_pairs={{0,12},{4,8},{8,4},{12,0},{1,13},{5,9},{9,5},{13,1},{2,14},{6,10},... | collective-permute-start | bytes 196616 | tf_op jit(solution)/shard_map/ppermute | solution.py:335
  37.5 6.3 %collective-permute-start.8 = (bf16[8,32,128]{2,1,0:T(8,128)(2,1)S(1)}, bf16[8,32,128]{2,1,0:T(8,128)(2,1)S(1)}, u32[]{:S(2)}, u32[]{:S(2)}) collective-permute-start(bf16[8,32,128]{2,1,0:T(8,128)(2,1)S(1)} %add_convert_fusion.2.refs_0_), channel_id=1, source_target_pairs={{0,12},{4,8},{8,4},{12,0},{1,13},{5,9},{9,5},{13,1},{2,14},{6,10},... | collective-permute-start | bytes 196616 | tf_op jit(solution)/shard_map/ppermute | solution.py:335
  39.5 5.7 %collective-permute-start.7 = (bf16[8,32,128]{2,1,0:T(8,128)(2,1)S(1)}, bf16[8,32,128]{2,1,0:T(8,128)(2,1)S(1)}, u32[]{:S(2)}, u32[]{:S(2)}) collective-permute-start(bf16[8,32,128]{2,1,0:T(8,128)(2,1)S(1)} %add_convert_fusion.2.refs_0_), channel_id=1, source_target_pairs={{0,8},{4,12},{8,0},{12,4},{1,9},{5,13},{9,1},{13,5},{2,10},{6,14},... | collective-permute-start | bytes 196616 | tf_op jit(solution)/shard_map/ppermute | solution.py:335
  39.8 5.4 %collective-permute-start.6 = (bf16[8,32,128]{2,1,0:T(8,128)(2,1)S(1)}, bf16[8,32,128]{2,1,0:T(8,128)(2,1)S(1)}, u32[]{:S(2)}, u32[]{:S(2)}) collective-permute-start(bf16[8,32,128]{2,1,0:T(8,128)(2,1)S(1)} %add_convert_fusion.2.refs_0_), channel_id=1, source_target_pairs={{0,4},{4,0},{8,12},{12,8},{1,5},{5,1},{9,13},{13,9},{2,6},{6,2},{1... | collective-permute-start | bytes 196616 | tf_op jit(solution)/shard_map/ppermute | solution.py:335
  51.2 2.2 %collective-permute-start.12 = (bf16[32,32,128]{2,1,0:T(8,128)(2,1)S(1)}, bf16[32,32,128]{2,1,0:T(8,128)(2,1)S(1)}, u32[]{:S(2)}, u32[]{:S(2)}) collective-permute-start(bf16[32,32,128]{2,1,0:T(8,128)(2,1)S(1)} %get-tuple-element.50), channel_id=1, source_target_pairs={{0,1},{1,0},{2,3},{3,2},{4,5},{5,4},{6,7},{7,6},{8,9},{9,8},{10,11... | collective-permute-start | bytes 786440 | tf_op jit(solution)/shard_map/ppermute | solution.py:335
  51.2 3.6 %collective-permute-start.11 = (f32[32,32]{1,0:T(8,128)S(1)}, f32[32,32]{1,0:T(8,128)S(1)}, u32[]{:S(2)}, u32[]{:S(2)}) collective-permute-start(f32[32,32]{1,0:T(8,128)S(1)} %get-tuple-element.46.refs_0_), channel_id=1, source_target_pairs={{0,3},{1,2},{2,1},{3,0},{4,7},{5,6},{6,5},{7,4},{8,11},{9,10},{10,... | collective-permute-start | bytes 12296 | tf_op jit(solution)/shard_map/ppermute | solution.py:335
  52.7 3.7 %collective-permute-start.10 = (f32[32,32]{1,0:T(8,128)S(1)}, f32[32,32]{1,0:T(8,128)S(1)}, u32[]{:S(2)}, u32[]{:S(2)}) collective-permute-start(f32[32,32]{1,0:T(8,128)S(1)} %get-tuple-element.46.refs_0_), channel_id=1, source_target_pairs={{0,2},{1,3},{2,0},{3,1},{4,6},{5,7},{6,4},{7,5},{8,10},{9,11},{10,... | collective-permute-start | bytes 12296 | tf_op jit(solution)/shard_map/ppermute | solution.py:335
  53.4 3.0 %collective-permute-start.9 = (f32[32,32]{1,0:T(8,128)S(1)}, f32[32,32]{1,0:T(8,128)S(1)}, u32[]{:S(2)}, u32[]{:S(2)}) collective-permute-start(f32[32,32]{1,0:T(8,128)S(1)} %get-tuple-element.46.refs_0_), channel_id=1, source_target_pairs={{0,1},{1,0},{2,3},{3,2},{4,5},{5,4},{6,7},{7,6},{8,9},{9,8},{10,11... | collective-permute-start | bytes 12296 | tf_op jit(solution)/shard_map/ppermute | solution.py:335
  53.5 8.8 %collective-permute-start.13 = (bf16[32,32,128]{2,1,0:T(8,128)(2,1)S(1)}, bf16[32,32,128]{2,1,0:T(8,128)(2,1)S(1)}, u32[]{:S(2)}, u32[]{:S(2)}) collective-permute-start(bf16[32,32,128]{2,1,0:T(8,128)(2,1)S(1)} %add_convert_fusion), channel_id=1, source_target_pairs={{0,2},{1,3},{2,0},{3,1},{4,6},{5,7},{6,4},{7,5},{8,10},{9,11},{10,... | collective-permute-start | bytes 786440 | tf_op jit(solution)/shard_map/ppermute | solution.py:335
  62.8 1.6 %collective-permute-start.14 = (bf16[32,32,128]{2,1,0:T(8,128)(2,1)S(1)}, bf16[32,32,128]{2,1,0:T(8,128)(2,1)S(1)}, u32[]{:S(2)}, u32[]{:S(2)}) collective-permute-start(bf16[32,32,128]{2,1,0:T(8,128)(2,1)S(1)} %mix.1.mine_ref), channel_id=1, source_target_pairs={{0,1},{1,0},{2,3},{3,2},{4,5},{5,4},{6,7},{7,6},{8,9},{9,8},{10,11... | collective-permute-start | bytes 786440 | tf_op jit(solution)/shard_map/ppermute | solution.py:335
  69.3 4.5 %collective-permute-start.15 = (bf16[8,32,128]{2,1,0:T(8,128)(2,1)S(1)}, bf16[8,32,128]{2,1,0:T(8,128)(2,1)S(1)}, u32[]{:S(2)}, u32[]{:S(2)}) collective-permute-start(bf16[8,32,128]{2,1,0:T(8,128)(2,1)S(1)} %get-tuple-element.52), channel_id=1, source_target_pairs={{0,4},{4,0},{8,12},{12,8},{1,5},{5,1},{9,13},{13,9},{2,6},{6,2},{1... | collective-permute-start | bytes 196616 | tf_op jit(solution)/shard_map/ppermute | solution.py:335
  70.3 8.3 %collective-permute-start.16 = (bf16[8,32,128]{2,1,0:T(8,128)(2,1)S(1)}, bf16[8,32,128]{2,1,0:T(8,128)(2,1)S(1)}, u32[]{:S(2)}, u32[]{:S(2)}) collective-permute-start(bf16[8,32,128]{2,1,0:T(8,128)(2,1)S(1)} %get-tuple-element.53), channel_id=1, source_target_pairs={{0,8},{4,12},{8,0},{12,4},{1,9},{5,13},{9,1},{13,5},{2,10},{6,14},... | collective-permute-start | bytes 196616 | tf_op jit(solution)/shard_map/ppermute | solution.py:335
  71.9 6.7 %collective-permute-start.17 = (bf16[8,32,128]{2,1,0:T(8,128)(2,1)S(1)}, bf16[8,32,128]{2,1,0:T(8,128)(2,1)S(1)}, u32[]{:S(2)}, u32[]{:S(2)}) collective-permute-start(bf16[8,32,128]{2,1,0:T(8,128)(2,1)S(1)} %get-tuple-element.54), channel_id=1, source_target_pairs={{0,12},{4,8},{8,4},{12,0},{1,13},{5,9},{9,5},{13,1},{2,14},{6,10},... | collective-permute-start | bytes 196616 | tf_op jit(solution)/shard_map/ppermute | solution.py:335
  78.6 6.3 %collective-permute-start.20 = (bf16[8,32,128]{2,1,0:T(8,128)(2,1)S(1)}, bf16[8,32,128]{2,1,0:T(8,128)(2,1)S(1)}, u32[]{:S(2)}, u32[]{:S(2)}) collective-permute-start(bf16[8,32,128]{2,1,0:T(8,128)(2,1)S(1)} %add_convert_fusion.1.refs_0_), channel_id=1, source_target_pairs={{0,12},{4,8},{8,4},{12,0},{1,13},{5,9},{9,5},{13,1},{2,14},{6,10},... | collective-permute-start | bytes 196616 | tf_op jit(solution)/shard_map/ppermute | solution.py:335
  80.7 6.0 %collective-permute-start.19 = (bf16[8,32,128]{2,1,0:T(8,128)(2,1)S(1)}, bf16[8,32,128]{2,1,0:T(8,128)(2,1)S(1)}, u32[]{:S(2)}, u32[]{:S(2)}) collective-permute-start(bf16[8,32,128]{2,1,0:T(8,128)(2,1)S(1)} %add_convert_fusion.1.refs_0_), channel_id=1, source_target_pairs={{0,8},{4,12},{8,0},{12,4},{1,9},{5,13},{9,1},{13,5},{2,10},{6,14},... | collective-permute-start | bytes 196616 | tf_op jit(solution)/shard_map/ppermute | solution.py:335
  81.4 5.2 %collective-permute-start.18 = (bf16[8,32,128]{2,1,0:T(8,128)(2,1)S(1)}, bf16[8,32,128]{2,1,0:T(8,128)(2,1)S(1)}, u32[]{:S(2)}, u32[]{:S(2)}) collective-permute-start(bf16[8,32,128]{2,1,0:T(8,128)(2,1)S(1)} %add_convert_fusion.1.refs_0_), channel_id=1, source_target_pairs={{0,4},{4,0},{8,12},{12,8},{1,5},{5,1},{9,13},{13,9},{2,6},{6,2},{1... | collective-permute-start | bytes 196616 | tf_op jit(solution)/shard_map/ppermute | solution.py:335
  86.8 3.3 %collective-permute-start.23 = (f32[32,32]{1,0:T(8,128)S(1)}, f32[32,32]{1,0:T(8,128)S(1)}, u32[]{:S(2)}, u32[]{:S(2)}) collective-permute-start(f32[32,32]{1,0:T(8,128)S(1)} %get-tuple-element.56.refs_0_), channel_id=1, source_target_pairs={{0,3},{1,2},{2,1},{3,0},{4,7},{5,6},{6,5},{7,4},{8,11},{9,10},{10,... | collective-permute-start | bytes 12296 | tf_op jit(solution)/shard_map/ppermute | solution.py:335
  86.8 3.8 %collective-permute-start.22 = (f32[32,32]{1,0:T(8,128)S(1)}, f32[32,32]{1,0:T(8,128)S(1)}, u32[]{:S(2)}, u32[]{:S(2)}) collective-permute-start(f32[32,32]{1,0:T(8,128)S(1)} %get-tuple-element.56.refs_0_), channel_id=1, source_target_pairs={{0,2},{1,3},{2,0},{3,1},{4,6},{5,7},{6,4},{7,5},{8,10},{9,11},{10,... | collective-permute-start | bytes 12296 | tf_op jit(solution)/shard_map/ppermute | solution.py:335
  88.2 2.4 %collective-permute-start.21 = (f32[32,32]{1,0:T(8,128)S(1)}, f32[32,32]{1,0:T(8,128)S(1)}, u32[]{:S(2)}, u32[]{:S(2)}) collective-permute-start(f32[32,32]{1,0:T(8,128)S(1)} %get-tuple-element.56.refs_0_), channel_id=1, source_target_pairs={{0,1},{1,0},{2,3},{3,2},{4,5},{5,4},{6,7},{7,6},{8,9},{9,8},{10,11... | collective-permute-start | bytes 12296 | tf_op jit(solution)/shard_map/ppermute | solution.py:335

commit v5 on v4

--- a/solution.py
+++ b/solution.py
@@ -10,8 +10,8 @@
 ITERS = 2
 TURNED = 3
 FIRST = 128
-SECOND = 160
-BACK = 320
+SECOND = 320
+BACK = 640
 SLOTS = 3
 MIX = 8
 F32 = jnp.float32
@@ -394,7 +394,7 @@
                 out_specs=[VMEM, VMEM],
                 out_shape=[keep_out, send_out],
                 scratch_shapes=accs,
-                compiler_params=params(12),
+                compiler_params=params(24),
                 name="forward",
                 cost_estimate=forward_cost,
             )(block_rows, block_cols, held, flipped, w_full)
@@ -453,7 +453,7 @@
                 pltpu.VMEM((col_blocks, side, box), F32),
                 pltpu.VMEM((col_blocks, side, box), F32),
             ],
-            compiler_params=params(12),
+            compiler_params=params(24),
             name="adjoint",
                 cost_estimate=adjoint_cost,
         )(block_rows, block_cols, tall_counts, held, mine, other)

time: 94.6 us -> 112 us (1.18)
  local copies, waits for them, and re-layouts: 0.02 us -> 20.9 us
  waiting for transfers between devices: 26.4 us -> 24.3 us
    unnamed x8 -> x14, local copies, waits for them, and re-layouts: 0.02 us -> 20.9 us
    ppermute x24, waiting for transfers between devices: 26.4 us -> 24.3 us  [swap(): return lax.ppermute(x, axis, [(i, i ^ bits) for i in range(size)])]
  transfers between devices with their start and end apart: 24 -> 24, of which waited for: 14 -> 14; matrix products, arithmetic and copies ran while one was open for 0% -> 0% of each run, Pallas kernels for 12% -> 10%
where the time goes in v5:
time: 112 us
  Pallas kernels  39.7 us (35%)
  starting transfers between devices  26.8 us (24%)
  waiting for transfers between devices  24.3 us (22%)
  local copies, waits for them, and re-layouts  20.9 us (19%)
    ppermute x24, starting transfers between devices, swap(): return lax.ppermute(x, axis, [(i, i ^ bits) for i in range(size)])  26.8 us
    ppermute x24, waiting for transfers between devices, swap(): return lax.ppermute(x, axis, [(i, i ^ bits) for i in range(size)])  24.3 us
    unnamed x14, local copies, waits for them, and re-layouts  20.9 us
    pallas_call x2, Pallas kernels, per_device(): pl.pallas_call(functools.partial(adjoint_kernel, unroll_of(total, BACK),...  9.16 us
    pallas_call x1, Pallas kernels, per_device(): pl.pallas_call(functools.partial(first_forward_kernel, first_unroll), in_...  8.64 us
    pallas_call x1, Pallas kernels, per_device(): pl.pallas_call(load_kernel, in_specs=[HBM], out_specs=VMEM, out_shape=plt...  6.99 us
    pallas_call x1, Pallas kernels, per_device(): pl.pallas_call(functools.partial(forward_kernel, unroll, turned), in_spec...  5.36 us
    pallas_call x1, Pallas kernels, per_device(): pl.pallas_call(functools.partial(basis_kernel, box_total), in_specs=[VMEM...  3.8 us
  transfers between devices with their start and end apart: 24, of which 14 were waited for; matrix products, arithmetic and copies ran while one was open for 0% of the time, Pallas kernels for 10%

profile of v5, /device:TPU:0, one launch (start us, length us, event | category | flops | bytes accessed | tf_op | source)
XLA Modules:
  0.0 112.3 jit_solution(14134467977763285934)
XLA Ops:
  0.0 8.6 %first_forward.1 = (f32[32,32,128]{2,1,0:T(8,128)S(1)}, bf16[32,32,128]{2,1,0:T(8,128)(2,1)S(1)}) custom-call(s32[640]{0:T(1024)} %rows_ref.5, s32[640]{0:T(1024)} %cols_ref.5, f32[32,4096]{1,0:T(8,128)} %start_hbm.1, s32[1,4096]{1,0:T(1,128)} %bitcast.7, bf16[640,128,128]{2,1,0:T(8,128)(2,1)} %hbm_ref), custom_call_target="tpu_custom_call" | custom-call | flops 10737418240 | tf_op jit(solution)/shard_map/first_forward/pallas_call | solution.py:367
  8.7 0.5 collective-permute-start
  9.2 1.2 %collective-permute-done = bf16[32,32,128]{2,1,0:T(8,128)(2,1)S(1)} collective-permute-done((bf16[32,32,128]{2,1,0:T(8,128)(2,1)S(1)}, bf16[32,32,128]{2,1,0:T(8,128)(2,1)S(1)}, u32[]{:S(2)}, u32[]{:S(2)}) %collective-permute-start) | collective-permute-done | bytes 262176 | tf_op jit(solution)/shard_map/ppermute | solution.py:335
  10.4 2.9 %collective-permute-start.1 = (bf16[32,32,128]{2,1,0:T(8,128)(2,1)S(1)}, bf16[32,32,128]{2,1,0:T(8,128)(2,1)S(1)}, u32[]{:S(2)}, u32[]{:S(2)}) collective-permute-start(bf16[32,32,128]{2,1,0:T(8,128)(2,1)S(1)} %fusion), channel_id=1, source_target_pairs={{0,2},{1,3},{2,0},{3,1},{4,6},{5,7},{6,4},{7,5},{8,10},{9,11},{10,... | collective-permute-start | bytes 786440 | tf_op jit(solution)/shard_map/ppermute | solution.py:335
  13.4 7.0 %load.1.held_ref = bf16[640,128,128]{2,1,0:T(8,128)(2,1)S(1)} custom-call(bf16[640,128,128]{2,1,0:T(8,128)(2,1)} %hbm_ref), custom_call_target="tpu_custom_call" | custom-call | bytes 41943040 | tf_op jit(solution)/shard_map/load/pallas_call | solution.py:404
  20.4 0.1 convert_add_fusion
  20.6 1.5 %collective-permute-done.2.other_ref = bf16[32,32,128]{2,1,0:T(8,128)(2,1)S(1)} collective-permute-done((bf16[32,32,128]{2,1,0:T(8,128)(2,1)S(1)}, bf16[32,32,128]{2,1,0:T(8,128)(2,1)S(1)}, u32[]{:S(2)}, u32[]{:S(2)}) %collective-permute-start.2) | collective-permute-done | bytes 262176 | tf_op jit(solution)/shard_map/ppermute | solution.py:335
  22.1 4.6 %adjoint.2 = (f32[8,32,128]{2,1,0:T(8,128)S(1)}, bf16[8,32,128]{2,1,0:T(8,128)(2,1)S(1)}, bf16[8,32,128]{2,1,0:T(8,128)(2,1)S(1)}, bf16[8,32,128]{2,1,0:T(8,128)(2,1)S(1)}) custom-call(s32[640]{0:T(1024)S(1)} %copy-done.4, s32[640]{0:T(1024)S(1)} %copy-done.5, s32[32,1,128]{2,1,0:T(1,128)S(1)} %bitcast.8, bf16[640,128,128]{2,1,0:T(8,128)(2,1)S(1)} %load.1.held_ref, ...), custom_call_target="tpu_custom_call" | custom-call | flops 5368709120 | tf_op jit(solution)/shard_map/adjoint/pallas_call | solution.py:445
  26.7 7.0 %copy-done = bf16[640,128,128]{2,1,0:T(8,128)(2,1)} copy-done((bf16[640,128,128]{2,1,0:T(8,128)(2,1)}, bf16[640,128,128]{2,1,0:T(8,128)(2,1)S(1)}, u32[]{:S(2)}) %copy-start) | copy-done | bytes 20971544
  33.7 1.6 %collective-permute-start.3 = (bf16[8,32,128]{2,1,0:T(8,128)(2,1)S(1)}, bf16[8,32,128]{2,1,0:T(8,128)(2,1)S(1)}, u32[]{:S(2)}, u32[]{:S(2)}) collective-permute-start(bf16[8,32,128]{2,1,0:T(8,128)(2,1)S(1)} %get-tuple-element.39), channel_id=1, source_target_pairs={{0,4},{4,0},{8,12},{12,8},{1,5},{5,1},{9,13},{13,9},{2,6},{6,2},{1... | collective-permute-start | bytes 196616 | tf_op jit(solution)/shard_map/ppermute | solution.py:335
  35.3 2.6 %collective-permute-start.4 = (bf16[8,32,128]{2,1,0:T(8,128)(2,1)S(1)}, bf16[8,32,128]{2,1,0:T(8,128)(2,1)S(1)}, u32[]{:S(2)}, u32[]{:S(2)}) collective-permute-start(bf16[8,32,128]{2,1,0:T(8,128)(2,1)S(1)} %get-tuple-element.40), channel_id=1, source_target_pairs={{0,8},{4,12},{8,0},{12,4},{1,9},{5,13},{9,1},{13,5},{2,10},{6,14},... | collective-permute-start | bytes 196616 | tf_op jit(solution)/shard_map/ppermute | solution.py:335
  37.9 0.2 collective-permute-start.5
  38.1 7.0 %copy-done.1 = bf16[640,128,128]{2,1,0:T(8,128)(2,1)S(1)} copy-done((bf16[640,128,128]{2,1,0:T(8,128)(2,1)S(1)}, bf16[640,128,128]{2,1,0:T(8,128)(2,1)}, u32[]{:S(2)}) %copy-start.1) | copy-done | bytes 20971544
  45.1 2.1 %turn.1.turned_ref = bf16[240,128,128]{2,1,0:T(8,128)(2,1)S(1)} custom-call(bf16[640,128,128]{2,1,0:T(8,128)(2,1)S(1)} %copy-done.1), custom_call_target="tpu_custom_call" | custom-call | flops 5368709120 | tf_op jit(solution)/shard_map/turn/pallas_call | solution.py:464
  47.2 3.7 %collective-permute-start.8 = (bf16[8,32,128]{2,1,0:T(8,128)(2,1)S(1)}, bf16[8,32,128]{2,1,0:T(8,128)(2,1)S(1)}, u32[]{:S(2)}, u32[]{:S(2)}) collective-permute-start(bf16[8,32,128]{2,1,0:T(8,128)(2,1)S(1)} %add_convert_fusion.2.refs_0_), channel_id=1, source_target_pairs={{0,12},{4,8},{8,4},{12,0},{1,13},{5,9},{9,5},{13,1},{2,14},{6,10},... | collective-permute-start | bytes 196616 | tf_op jit(solution)/shard_map/ppermute | solution.py:335
  50.9 0.8 collective-permute-start.6
  51.7 1.8 %collective-permute-done.8.refs_3_ = bf16[8,32,128]{2,1,0:T(8,128)(2,1)S(1)} collective-permute-done((bf16[8,32,128]{2,1,0:T(8,128)(2,1)S(1)}, bf16[8,32,128]{2,1,0:T(8,128)(2,1)S(1)}, u32[]{:S(2)}, u32[]{:S(2)}) %collective-permute-start.8) | collective-permute-done | bytes 65568 | tf_op jit(solution)/shard_map/ppermute | solution.py:335
  53.5 2.7 %collective-permute-done.7.refs_2_ = bf16[8,32,128]{2,1,0:T(8,128)(2,1)S(1)} collective-permute-done((bf16[8,32,128]{2,1,0:T(8,128)(2,1)S(1)}, bf16[8,32,128]{2,1,0:T(8,128)(2,1)S(1)}, u32[]{:S(2)}, u32[]{:S(2)}) %collective-permute-start.7) | collective-permute-done | bytes 65568 | tf_op jit(solution)/shard_map/ppermute | solution.py:335
  56.1 0.3 collective-permute-done.6.refs_1_
  56.4 0.2 gram.2
  56.6 7.0 %copy-done.2 = bf16[640,128,128]{2,1,0:T(8,128)(2,1)S(1)} copy-done((bf16[640,128,128]{2,1,0:T(8,128)(2,1)S(1)}, bf16[640,128,128]{2,1,0:T(8,128)(2,1)}, u32[]{:S(2)}) %copy-start.2) | copy-done | bytes 20971544
  63.6 5.4 %forward.1 = (f32[32,32,128]{2,1,0:T(8,128)S(1)}, bf16[32,32,128]{2,1,0:T(8,128)(2,1)S(1)}) custom-call(s32[640]{0:T(1024)S(1)} %copy-done.4, s32[640]{0:T(1024)S(1)} %copy-done.5, bf16[640,128,128]{2,1,0:T(8,128)(2,1)S(1)} %copy-done.2, bf16[240,128,128]{2,1,0:T(8,128)(2,1)S(1)} %turn.1.turned_ref, bf16[32,32,128]{2,1,0:T(8,128)(2,1)S(1)} %get-tuple-element.48.panel_ref), custom_call_target="tpu_custom_call" | custom-call | flops 10737418240 | tf_op jit(solution)/shard_map/forward/pallas_call | solution.py:391
  69.1 1.4 %collective-permute-start.11 = (f32[32,32]{1,0:T(8,128)S(1)}, f32[32,32]{1,0:T(8,128)S(1)}, u32[]{:S(2)}, u32[]{:S(2)}) collective-permute-start(f32[32,32]{1,0:T(8,128)S(1)} %get-tuple-element.46.refs_0_), channel_id=1, source_target_pairs={{0,3},{1,2},{2,1},{3,0},{4,7},{5,6},{6,5},{7,4},{8,11},{9,10},{10,... | collective-permute-start | bytes 12296 | tf_op jit(solution)/shard_map/ppermute | solution.py:335
  70.5 0.7 collective-permute-start.10
  71.2 0.1 add_convert_fusion
  71.3 1.4 %collective-permute-start.13 = (bf16[32,32,128]{2,1,0:T(8,128)(2,1)S(1)}, bf16[32,32,128]{2,1,0:T(8,128)(2,1)S(1)}, u32[]{:S(2)}, u32[]{:S(2)}) collective-permute-start(bf16[32,32,128]{2,1,0:T(8,128)(2,1)S(1)} %add_convert_fusion), channel_id=1, source_target_pairs={{0,2},{1,3},{2,0},{3,1},{4,6},{5,7},{6,4},{7,5},{8,10},{9,11},{10,... | collective-permute-start | bytes 786440 | tf_op jit(solution)/shard_map/ppermute | solution.py:335
  72.7 1.6 %collective-permute-done.10.refs_2_ = f32[32,32]{1,0:T(8,128)S(1)} collective-permute-done((f32[32,32]{1,0:T(8,128)S(1)}, f32[32,32]{1,0:T(8,128)S(1)}, u32[]{:S(2)}, u32[]{:S(2)}) %collective-permute-start.10) | collective-permute-done | bytes 4128 | tf_op jit(solution)/shard_map/ppermute | solution.py:335
  74.2 2.6 %orth.1.matrix_ref = f32[32,32]{1,0:T(8,128)S(1)} custom-call(f32[32,32]{1,0:T(8,128)S(1)} %get-tuple-element.46.refs_0_, f32[32,32]{1,0:T(8,128)S(1)} %collective-permute-done.9.refs_1_, f32[32,32]{1,0:T(8,128)S(1)} %collective-permute-done.10.refs_2_, f32[32,32]{1,0:T(8,128)S(1)} %collective-permute-done.11.refs_3_), custom_call_target="tpu_custom_call" | custom-call | flops 4294967296 | tf_op jit(solution)/shard_map/orth/pallas_call | solution.py:425
  76.9 3.2 %collective-permute-done.13.refs_0_ = bf16[32,32,128]{2,1,0:T(8,128)(2,1)S(1)} collective-permute-done((bf16[32,32,128]{2,1,0:T(8,128)(2,1)S(1)}, bf16[32,32,128]{2,1,0:T(8,128)(2,1)S(1)}, u32[]{:S(2)}, u32[]{:S(2)}) %collective-permute-start.13) | collective-permute-done | bytes 262176 | tf_op jit(solution)/shard_map/ppermute | solution.py:335
  80.1 0.6 mix.1.mine_ref
  80.7 1.5 %collective-permute-done.14.other_ref = bf16[32,32,128]{2,1,0:T(8,128)(2,1)S(1)} collective-permute-done((bf16[32,32,128]{2,1,0:T(8,128)(2,1)S(1)}, bf16[32,32,128]{2,1,0:T(8,128)(2,1)S(1)}, u32[]{:S(2)}, u32[]{:S(2)}) %collective-permute-start.14) | collective-permute-done | bytes 262176 | tf_op jit(solution)/shard_map/ppermute | solution.py:335
  82.3 4.6 %adjoint.3 = (f32[8,32,128]{2,1,0:T(8,128)S(1)}, bf16[8,32,128]{2,1,0:T(8,128)(2,1)S(1)}, bf16[8,32,128]{2,1,0:T(8,128)(2,1)S(1)}, bf16[8,32,128]{2,1,0:T(8,128)(2,1)S(1)}) custom-call(s32[640]{0:T(1024)S(1)} %copy-done.4, s32[640]{0:T(1024)S(1)} %copy-done.5, s32[32,1,128]{2,1,0:T(1,128)S(1)} %bitcast.10, bf16[640,128,128]{2,1,0:T(8,128)(2,1)S(1)} %copy-done.2, ...), custom_call_target="tpu_custom_call" | custom-call | flops 5368709120 | tf_op jit(solution)/shard_map/adjoint/pallas_call | solution.py:445
  86.8 0.7 collective-permute-start.15
  87.6 1.9 %collective-permute-start.16 = (bf16[8,32,128]{2,1,0:T(8,128)(2,1)S(1)}, bf16[8,32,128]{2,1,0:T(8,128)(2,1)S(1)}, u32[]{:S(2)}, u32[]{:S(2)}) collective-permute-start(bf16[8,32,128]{2,1,0:T(8,128)(2,1)S(1)} %get-tuple-element.53), channel_id=1, source_target_pairs={{0,8},{4,12},{8,0},{12,4},{1,9},{5,13},{9,1},{13,5},{2,10},{6,14},... | collective-permute-start | bytes 196616 | tf_op jit(solution)/shard_map/ppermute | solution.py:335
  89.4 1.9 %collective-permute-start.17 = (bf16[8,32,128]{2,1,0:T(8,128)(2,1)S(1)}, bf16[8,32,128]{2,1,0:T(8,128)(2,1)S(1)}, u32[]{:S(2)}, u32[]{:S(2)}) collective-permute-start(bf16[8,32,128]{2,1,0:T(8,128)(2,1)S(1)} %get-tuple-element.54), channel_id=1, source_target_pairs={{0,12},{4,8},{8,4},{12,0},{1,13},{5,9},{9,5},{13,1},{2,14},{6,10},... | collective-permute-start | bytes 196616 | tf_op jit(solution)/shard_map/ppermute | solution.py:335
  91.3 0.6 collective-permute-done.15
  91.9 4.1 %collective-permute-done.16 = bf16[8,32,128]{2,1,0:T(8,128)(2,1)S(1)} collective-permute-done((bf16[8,32,128]{2,1,0:T(8,128)(2,1)S(1)}, bf16[8,32,128]{2,1,0:T(8,128)(2,1)S(1)}, u32[]{:S(2)}, u32[]{:S(2)}) %collective-permute-start.16) | collective-permute-done | bytes 65568 | tf_op jit(solution)/shard_map/ppermute | solution.py:335
  96.0 2.1 %collective-permute-start.20 = (bf16[8,32,128]{2,1,0:T(8,128)(2,1)S(1)}, bf16[8,32,128]{2,1,0:T(8,128)(2,1)S(1)}, u32[]{:S(2)}, u32[]{:S(2)}) collective-permute-start(bf16[8,32,128]{2,1,0:T(8,128)(2,1)S(1)} %add_convert_fusion.1.refs_0_), channel_id=1, source_target_pairs={{0,12},{4,8},{8,4},{12,0},{1,13},{5,9},{9,5},{13,1},{2,14},{6,10},... | collective-permute-start | bytes 196616 | tf_op jit(solution)/shard_map/ppermute | solution.py:335
  98.1 0.8 collective-permute-start.19
  98.9 1.6 %collective-permute-start.18 = (bf16[8,32,128]{2,1,0:T(8,128)(2,1)S(1)}, bf16[8,32,128]{2,1,0:T(8,128)(2,1)S(1)}, u32[]{:S(2)}, u32[]{:S(2)}) collective-permute-start(bf16[8,32,128]{2,1,0:T(8,128)(2,1)S(1)} %add_convert_fusion.1.refs_0_), channel_id=1, source_target_pairs={{0,4},{4,0},{8,12},{12,8},{1,5},{5,1},{9,13},{13,9},{2,6},{6,2},{1... | collective-permute-start | bytes 196616 | tf_op jit(solution)/shard_map/ppermute | solution.py:335
  100.5 2.4 %collective-permute-done.20.refs_3_ = bf16[8,32,128]{2,1,0:T(8,128)(2,1)S(1)} collective-permute-done((bf16[8,32,128]{2,1,0:T(8,128)(2,1)S(1)}, bf16[8,32,128]{2,1,0:T(8,128)(2,1)S(1)}, u32[]{:S(2)}, u32[]{:S(2)}) %collective-permute-start.20) | collective-permute-done | bytes 65568 | tf_op jit(solution)/shard_map/ppermute | solution.py:335
  102.9 1.5 %collective-permute-done.19.refs_2_ = bf16[8,32,128]{2,1,0:T(8,128)(2,1)S(1)} collective-permute-done((bf16[8,32,128]{2,1,0:T(8,128)(2,1)S(1)}, bf16[8,32,128]{2,1,0:T(8,128)(2,1)S(1)}, u32[]{:S(2)}, u32[]{:S(2)}) %collective-permute-start.19) | collective-permute-done | bytes 65568 | tf_op jit(solution)/shard_map/ppermute | solution.py:335
  104.4 0.2 gram.3
  104.7 1.4 %collective-permute-start.22 = (f32[32,32]{1,0:T(8,128)S(1)}, f32[32,32]{1,0:T(8,128)S(1)}, u32[]{:S(2)}, u32[]{:S(2)}) collective-permute-start(f32[32,32]{1,0:T(8,128)S(1)} %get-tuple-element.56.refs_0_), channel_id=1, source_target_pairs={{0,2},{1,3},{2,0},{3,1},{4,6},{5,7},{6,4},{7,5},{8,10},{9,11},{10,... | collective-permute-start | bytes 12296 | tf_op jit(solution)/shard_map/ppermute | solution.py:335
  106.1 0.5 collective-permute-start.21
  106.5 1.4 %collective-permute-done.23.refs_3_ = f32[32,32]{1,0:T(8,128)S(1)} collective-permute-done((f32[32,32]{1,0:T(8,128)S(1)}, f32[32,32]{1,0:T(8,128)S(1)}, u32[]{:S(2)}, u32[]{:S(2)}) %collective-permute-start.23) | collective-permute-done | bytes 4128 | tf_op jit(solution)/shard_map/ppermute | solution.py:335
  107.9 0.5 collective-permute-done.22.refs_2_
  108.5 3.8 %basis.1 = f32[32,4096]{1,0:T(8,128)} custom-call(bf16[32,32,128]{2,1,0:T(8,128)(2,1)S(1)} %get-tuple-element.55.w_ref, f32[32,32]{1,0:T(8,128)S(1)} %get-tuple-element.56.refs_0_, f32[32,32]{1,0:T(8,128)S(1)} %collective-permute-done.21.refs_1_, f32[32,32]{1,0:T(8,128)S(1)} %collective-permute-done.22.refs_2_, f32[32,32]{1,0:T(8,128)S(1)} %collective-permute-done.23.refs_3_), custom_call_target="tpu_custom_call" | custom-call | flops 4294967296 | tf_op jit(solution)/shard_map/basis/pallas_call | solution.py:486
  (32 shorter events, 0.5 us)
Async XLA Ops:
  0.0 13.3 %copy-start.6 = (s32[8192]{0:T(1024)S(1)}, s32[8192]{0:T(1024)}, u32[]{:S(2)}) copy-start(s32[8192]{0:T(1024)} %param.9) | copy-start | bytes 98308
  8.7 1.7 %collective-permute-start = (bf16[32,32,128]{2,1,0:T(8,128)(2,1)S(1)}, bf16[32,32,128]{2,1,0:T(8,128)(2,1)S(1)}, u32[]{:S(2)}, u32[]{:S(2)}) collective-permute-start(bf16[32,32,128]{2,1,0:T(8,128)(2,1)S(1)} %get-tuple-element.32), channel_id=1, source_target_pairs={{0,1},{1,0},{2,3},{3,2},{4,5},{5,4},{6,7},{7,6},{8,9},{9,8},{10,11... | collective-permute-start | bytes 786440 | tf_op jit(solution)/shard_map/ppermute | solution.py:335
  10.4 10.0 %collective-permute-start.1 = (bf16[32,32,128]{2,1,0:T(8,128)(2,1)S(1)}, bf16[32,32,128]{2,1,0:T(8,128)(2,1)S(1)}, u32[]{:S(2)}, u32[]{:S(2)}) collective-permute-start(bf16[32,32,128]{2,1,0:T(8,128)(2,1)S(1)} %fusion), channel_id=1, source_target_pairs={{0,2},{1,3},{2,0},{3,1},{4,6},{5,7},{6,4},{7,5},{8,10},{9,11},{10,... | collective-permute-start | bytes 786440 | tf_op jit(solution)/shard_map/ppermute | solution.py:335
  13.3 8.8 %copy-start.3 = (s32[4096]{0:T(1024)S(1)}, s32[4096]{0:T(1024)}, u32[]{:S(2)}) copy-start(s32[4096]{0:T(1024)} %param.10) | copy-start | bytes 49156
  13.3 8.8 %copy-start.4 = (s32[640]{0:T(1024)S(1)}, s32[640]{0:T(1024)}, u32[]{:S(2)}) copy-start(s32[640]{0:T(1024)} %rows_ref.5) | copy-start | bytes 7684
  13.3 8.8 %copy-start.5 = (s32[640]{0:T(1024)S(1)}, s32[640]{0:T(1024)}, u32[]{:S(2)}) copy-start(s32[640]{0:T(1024)} %cols_ref.5) | copy-start | bytes 7684
  20.5 1.6 %collective-permute-start.2 = (bf16[32,32,128]{2,1,0:T(8,128)(2,1)S(1)}, bf16[32,32,128]{2,1,0:T(8,128)(2,1)S(1)}, u32[]{:S(2)}, u32[]{:S(2)}) collective-permute-start(bf16[32,32,128]{2,1,0:T(8,128)(2,1)S(1)} %divide_convert_fusion.mine_ref), channel_id=1, source_target_pairs={{0,1},{1,0},{2,3},{3,2},{4,5},{5,4},{6,7},{7,6},{8,9},{9,8},{10,11... | collective-permute-start | bytes 786440 | tf_op jit(solution)/shard_map/ppermute | solution.py:335
  26.7 7.0 %copy-start = (bf16[640,128,128]{2,1,0:T(8,128)(2,1)}, bf16[640,128,128]{2,1,0:T(8,128)(2,1)S(1)}, u32[]{:S(2)}) copy-start(bf16[640,128,128]{2,1,0:T(8,128)(2,1)S(1)} %load.1.held_ref) | copy-start | bytes 62914564
  33.7 13.4 %collective-permute-start.3 = (bf16[8,32,128]{2,1,0:T(8,128)(2,1)S(1)}, bf16[8,32,128]{2,1,0:T(8,128)(2,1)S(1)}, u32[]{:S(2)}, u32[]{:S(2)}) collective-permute-start(bf16[8,32,128]{2,1,0:T(8,128)(2,1)S(1)} %get-tuple-element.39), channel_id=1, source_target_pairs={{0,4},{4,0},{8,12},{12,8},{1,5},{5,1},{9,13},{13,9},{2,6},{6,2},{1... | collective-permute-start | bytes 196616 | tf_op jit(solution)/shard_map/ppermute | solution.py:335
  35.3 11.8 %collective-permute-start.4 = (bf16[8,32,128]{2,1,0:T(8,128)(2,1)S(1)}, bf16[8,32,128]{2,1,0:T(8,128)(2,1)S(1)}, u32[]{:S(2)}, u32[]{:S(2)}) collective-permute-start(bf16[8,32,128]{2,1,0:T(8,128)(2,1)S(1)} %get-tuple-element.40), channel_id=1, source_target_pairs={{0,8},{4,12},{8,0},{12,4},{1,9},{5,13},{9,1},{13,5},{2,10},{6,14},... | collective-permute-start | bytes 196616 | tf_op jit(solution)/shard_map/ppermute | solution.py:335
  37.9 9.3 %collective-permute-start.5 = (bf16[8,32,128]{2,1,0:T(8,128)(2,1)S(1)}, bf16[8,32,128]{2,1,0:T(8,128)(2,1)S(1)}, u32[]{:S(2)}, u32[]{:S(2)}) collective-permute-start(bf16[8,32,128]{2,1,0:T(8,128)(2,1)S(1)} %get-tuple-element.41), channel_id=1, source_target_pairs={{0,12},{4,8},{8,4},{12,0},{1,13},{5,9},{9,5},{13,1},{2,14},{6,10},... | collective-permute-start | bytes 196616 | tf_op jit(solution)/shard_map/ppermute | solution.py:335
  38.1 7.0 %copy-start.1 = (bf16[640,128,128]{2,1,0:T(8,128)(2,1)S(1)}, bf16[640,128,128]{2,1,0:T(8,128)(2,1)}, u32[]{:S(2)}) copy-start(bf16[640,128,128]{2,1,0:T(8,128)(2,1)} %copy-done) | copy-start | bytes 62914564
  47.2 6.2 %collective-permute-start.8 = (bf16[8,32,128]{2,1,0:T(8,128)(2,1)S(1)}, bf16[8,32,128]{2,1,0:T(8,128)(2,1)S(1)}, u32[]{:S(2)}, u32[]{:S(2)}) collective-permute-start(bf16[8,32,128]{2,1,0:T(8,128)(2,1)S(1)} %add_convert_fusion.2.refs_0_), channel_id=1, source_target_pairs={{0,12},{4,8},{8,4},{12,0},{1,13},{5,9},{9,5},{13,1},{2,14},{6,10},... | collective-permute-start | bytes 196616 | tf_op jit(solution)/shard_map/ppermute | solution.py:335
  50.9 5.2 %collective-permute-start.7 = (bf16[8,32,128]{2,1,0:T(8,128)(2,1)S(1)}, bf16[8,32,128]{2,1,0:T(8,128)(2,1)S(1)}, u32[]{:S(2)}, u32[]{:S(2)}) collective-permute-start(bf16[8,32,128]{2,1,0:T(8,128)(2,1)S(1)} %add_convert_fusion.2.refs_0_), channel_id=1, source_target_pairs={{0,8},{4,12},{8,0},{12,4},{1,9},{5,13},{9,1},{13,5},{2,10},{6,14},... | collective-permute-start | bytes 196616 | tf_op jit(solution)/shard_map/ppermute | solution.py:335
  50.9 5.5 %collective-permute-start.6 = (bf16[8,32,128]{2,1,0:T(8,128)(2,1)S(1)}, bf16[8,32,128]{2,1,0:T(8,128)(2,1)S(1)}, u32[]{:S(2)}, u32[]{:S(2)}) collective-permute-start(bf16[8,32,128]{2,1,0:T(8,128)(2,1)S(1)} %add_convert_fusion.2.refs_0_), channel_id=1, source_target_pairs={{0,4},{4,0},{8,12},{12,8},{1,5},{5,1},{9,13},{13,9},{2,6},{6,2},{1... | collective-permute-start | bytes 196616 | tf_op jit(solution)/shard_map/ppermute | solution.py:335
  56.6 7.0 %copy-start.2 = (bf16[640,128,128]{2,1,0:T(8,128)(2,1)S(1)}, bf16[640,128,128]{2,1,0:T(8,128)(2,1)}, u32[]{:S(2)}) copy-start(bf16[640,128,128]{2,1,0:T(8,128)(2,1)} %copy-done) | copy-start | bytes 62914564
  69.0 2.2 %collective-permute-start.12 = (bf16[32,32,128]{2,1,0:T(8,128)(2,1)S(1)}, bf16[32,32,128]{2,1,0:T(8,128)(2,1)S(1)}, u32[]{:S(2)}, u32[]{:S(2)}) collective-permute-start(bf16[32,32,128]{2,1,0:T(8,128)(2,1)S(1)} %get-tuple-element.50), channel_id=1, source_target_pairs={{0,1},{1,0},{2,3},{3,2},{4,5},{5,4},{6,7},{7,6},{8,9},{9,8},{10,11... | collective-permute-start | bytes 786440 | tf_op jit(solution)/shard_map/ppermute | solution.py:335
  69.1 3.6 %collective-permute-start.11 = (f32[32,32]{1,0:T(8,128)S(1)}, f32[32,32]{1,0:T(8,128)S(1)}, u32[]{:S(2)}, u32[]{:S(2)}) collective-permute-start(f32[32,32]{1,0:T(8,128)S(1)} %get-tuple-element.46.refs_0_), channel_id=1, source_target_pairs={{0,3},{1,2},{2,1},{3,0},{4,7},{5,6},{6,5},{7,4},{8,11},{9,10},{10,... | collective-permute-start | bytes 12296 | tf_op jit(solution)/shard_map/ppermute | solution.py:335
  70.5 3.7 %collective-permute-start.10 = (f32[32,32]{1,0:T(8,128)S(1)}, f32[32,32]{1,0:T(8,128)S(1)}, u32[]{:S(2)}, u32[]{:S(2)}) collective-permute-start(f32[32,32]{1,0:T(8,128)S(1)} %get-tuple-element.46.refs_0_), channel_id=1, source_target_pairs={{0,2},{1,3},{2,0},{3,1},{4,6},{5,7},{6,4},{7,5},{8,10},{9,11},{10,... | collective-permute-start | bytes 12296 | tf_op jit(solution)/shard_map/ppermute | solution.py:335
  71.2 3.0 %collective-permute-start.9 = (f32[32,32]{1,0:T(8,128)S(1)}, f32[32,32]{1,0:T(8,128)S(1)}, u32[]{:S(2)}, u32[]{:S(2)}) collective-permute-start(f32[32,32]{1,0:T(8,128)S(1)} %get-tuple-element.46.refs_0_), channel_id=1, source_target_pairs={{0,1},{1,0},{2,3},{3,2},{4,5},{5,4},{6,7},{7,6},{8,9},{9,8},{10,11... | collective-permute-start | bytes 12296 | tf_op jit(solution)/shard_map/ppermute | solution.py:335
  71.3 8.8 %collective-permute-start.13 = (bf16[32,32,128]{2,1,0:T(8,128)(2,1)S(1)}, bf16[32,32,128]{2,1,0:T(8,128)(2,1)S(1)}, u32[]{:S(2)}, u32[]{:S(2)}) collective-permute-start(bf16[32,32,128]{2,1,0:T(8,128)(2,1)S(1)} %add_convert_fusion), channel_id=1, source_target_pairs={{0,2},{1,3},{2,0},{3,1},{4,6},{5,7},{6,4},{7,5},{8,10},{9,11},{10,... | collective-permute-start | bytes 786440 | tf_op jit(solution)/shard_map/ppermute | solution.py:335
  80.7 1.6 %collective-permute-start.14 = (bf16[32,32,128]{2,1,0:T(8,128)(2,1)S(1)}, bf16[32,32,128]{2,1,0:T(8,128)(2,1)S(1)}, u32[]{:S(2)}, u32[]{:S(2)}) collective-permute-start(bf16[32,32,128]{2,1,0:T(8,128)(2,1)S(1)} %mix.1.mine_ref), channel_id=1, source_target_pairs={{0,1},{1,0},{2,3},{3,2},{4,5},{5,4},{6,7},{7,6},{8,9},{9,8},{10,11... | collective-permute-start | bytes 786440 | tf_op jit(solution)/shard_map/ppermute | solution.py:335
  86.8 5.0 %collective-permute-start.15 = (bf16[8,32,128]{2,1,0:T(8,128)(2,1)S(1)}, bf16[8,32,128]{2,1,0:T(8,128)(2,1)S(1)}, u32[]{:S(2)}, u32[]{:S(2)}) collective-permute-start(bf16[8,32,128]{2,1,0:T(8,128)(2,1)S(1)} %get-tuple-element.52), channel_id=1, source_target_pairs={{0,4},{4,0},{8,12},{12,8},{1,5},{5,1},{9,13},{13,9},{2,6},{6,2},{1... | collective-permute-start | bytes 196616 | tf_op jit(solution)/shard_map/ppermute | solution.py:335
  87.6 8.4 %collective-permute-start.16 = (bf16[8,32,128]{2,1,0:T(8,128)(2,1)S(1)}, bf16[8,32,128]{2,1,0:T(8,128)(2,1)S(1)}, u32[]{:S(2)}, u32[]{:S(2)}) collective-permute-start(bf16[8,32,128]{2,1,0:T(8,128)(2,1)S(1)} %get-tuple-element.53), channel_id=1, source_target_pairs={{0,8},{4,12},{8,0},{12,4},{1,9},{5,13},{9,1},{13,5},{2,10},{6,14},... | collective-permute-start | bytes 196616 | tf_op jit(solution)/shard_map/ppermute | solution.py:335
  89.4 6.5 %collective-permute-start.17 = (bf16[8,32,128]{2,1,0:T(8,128)(2,1)S(1)}, bf16[8,32,128]{2,1,0:T(8,128)(2,1)S(1)}, u32[]{:S(2)}, u32[]{:S(2)}) collective-permute-start(bf16[8,32,128]{2,1,0:T(8,128)(2,1)S(1)} %get-tuple-element.54), channel_id=1, source_target_pairs={{0,12},{4,8},{8,4},{12,0},{1,13},{5,9},{9,5},{13,1},{2,14},{6,10},... | collective-permute-start | bytes 196616 | tf_op jit(solution)/shard_map/ppermute | solution.py:335
  96.0 6.9 %collective-permute-start.20 = (bf16[8,32,128]{2,1,0:T(8,128)(2,1)S(1)}, bf16[8,32,128]{2,1,0:T(8,128)(2,1)S(1)}, u32[]{:S(2)}, u32[]{:S(2)}) collective-permute-start(bf16[8,32,128]{2,1,0:T(8,128)(2,1)S(1)} %add_convert_fusion.1.refs_0_), channel_id=1, source_target_pairs={{0,12},{4,8},{8,4},{12,0},{1,13},{5,9},{9,5},{13,1},{2,14},{6,10},... | collective-permute-start | bytes 196616 | tf_op jit(solution)/shard_map/ppermute | solution.py:335
  98.1 6.3 %collective-permute-start.19 = (bf16[8,32,128]{2,1,0:T(8,128)(2,1)S(1)}, bf16[8,32,128]{2,1,0:T(8,128)(2,1)S(1)}, u32[]{:S(2)}, u32[]{:S(2)}) collective-permute-start(bf16[8,32,128]{2,1,0:T(8,128)(2,1)S(1)} %add_convert_fusion.1.refs_0_), channel_id=1, source_target_pairs={{0,8},{4,12},{8,0},{12,4},{1,9},{5,13},{9,1},{13,5},{2,10},{6,14},... | collective-permute-start | bytes 196616 | tf_op jit(solution)/shard_map/ppermute | solution.py:335
  98.9 5.5 %collective-permute-start.18 = (bf16[8,32,128]{2,1,0:T(8,128)(2,1)S(1)}, bf16[8,32,128]{2,1,0:T(8,128)(2,1)S(1)}, u32[]{:S(2)}, u32[]{:S(2)}) collective-permute-start(bf16[8,32,128]{2,1,0:T(8,128)(2,1)S(1)} %add_convert_fusion.1.refs_0_), channel_id=1, source_target_pairs={{0,4},{4,0},{8,12},{12,8},{1,5},{5,1},{9,13},{13,9},{2,6},{6,2},{1... | collective-permute-start | bytes 196616 | tf_op jit(solution)/shard_map/ppermute | solution.py:335
  104.7 3.3 %collective-permute-start.23 = (f32[32,32]{1,0:T(8,128)S(1)}, f32[32,32]{1,0:T(8,128)S(1)}, u32[]{:S(2)}, u32[]{:S(2)}) collective-permute-start(f32[32,32]{1,0:T(8,128)S(1)} %get-tuple-element.56.refs_0_), channel_id=1, source_target_pairs={{0,3},{1,2},{2,1},{3,0},{4,7},{5,6},{6,5},{7,4},{8,11},{9,10},{10,... | collective-permute-start | bytes 12296 | tf_op jit(solution)/shard_map/ppermute | solution.py:335
  104.7 3.8 %collective-permute-start.22 = (f32[32,32]{1,0:T(8,128)S(1)}, f32[32,32]{1,0:T(8,128)S(1)}, u32[]{:S(2)}, u32[]{:S(2)}) collective-permute-start(f32[32,32]{1,0:T(8,128)S(1)} %get-tuple-element.56.refs_0_), channel_id=1, source_target_pairs={{0,2},{1,3},{2,0},{3,1},{4,6},{5,7},{6,4},{7,5},{8,10},{9,11},{10,... | collective-permute-start | bytes 12296 | tf_op jit(solution)/shard_map/ppermute | solution.py:335
  106.1 2.4 %collective-permute-start.21 = (f32[32,32]{1,0:T(8,128)S(1)}, f32[32,32]{1,0:T(8,128)S(1)}, u32[]{:S(2)}, u32[]{:S(2)}) collective-permute-start(f32[32,32]{1,0:T(8,128)S(1)} %get-tuple-element.56.refs_0_), channel_id=1, source_target_pairs={{0,1},{1,0},{2,3},{3,2},{4,5},{5,4},{6,7},{7,6},{8,9},{9,8},{10,11... | collective-permute-start | bytes 12296 | tf_op jit(solution)/shard_map/ppermute | solution.py:335
